TPU v7x, 128 devices: a whole 4x4x4 slice. The times are simulated.
128 devices in a mesh: dp: 8 (over x, core), mp: 16 (over z, y).
Axes of the slice: x: 4, y: 4, z: 4, core: 2. Of those that a mesh axis runs over, the one named last changes fastest.
Arguments:
- gradient: float32 [8, 1024, 5120], P('dp', 'mp'), may hold values from -40 to 40
- feedback: float32 [8, 1024, 5120], P('dp', 'mp'), may hold values from -3 to 3
- q_previous: float32 [16, 5120], replicated, may hold values from -6 to 6
Outputs:
- new_feedback: float32 [8, 1024, 5120], P('dp', 'mp')
- p_ortho: float32 [16, 1024], P(None, 'mp')
- q_factor: float32 [16, 5120], replicated
All inputs are finite; a program needn't handle non-finite values.
Results may differ from a plain program's by a relative error of at most 0.000075.
Values sent between devices are 32-bit elements; how exact they have to be, the bound alone decides.
No kernel may reach another device: no remote copies, remote signals or barrier semaphores. Data moves between devices by JAX's collectives and lax.ppermute only.
A program may use at most 64 MiB of HBM per device.

v0:
```python
import jax
import jax.numpy as jnp
from jax import lax
from jax.sharding import PartitionSpec as P


def contract(left, right, left_dim, right_dim):
    return lax.dot_general(
        left,
        right,
        (((left_dim,), (right_dim,)), ((), ())),
        precision=lax.Precision.HIGHEST,
        preferred_element_type=jnp.float32,
    )


def body(gradient, feedback, q_previous):
    replicas = lax.axis_size("dp")
    corrected = gradient + feedback
    local = corrected[0]
    p_term = contract(q_previous, local, 1, 1)
    p_mean = lax.psum(p_term, "dp") / replicas
    rank = p_mean.shape[0]

    def one_row(index, finished):
        target = lax.dynamic_slice_in_dim(p_mean, index, 1, 0)
        coefs = lax.psum(contract(finished, target, 1, 1), "mp")
        remain = target - contract(coefs, finished, 0, 0)
        length = lax.psum(jnp.sum(remain * remain), "mp")
        return lax.dynamic_update_slice_in_dim(finished, remain / jnp.sqrt(length), index, 0)

    p_ortho = lax.fori_loop(0, rank, one_row, jnp.zeros_like(p_mean))
    q_term = contract(p_ortho, local, 1, 0)
    q_factor = lax.psum(q_term, ("dp", "mp")) / replicas
    update = contract(p_ortho, q_factor, 0, 0)
    new_feedback = corrected - update[None]
    return (new_feedback, p_ortho, q_factor)


def solution(mesh):
    return jax.shard_map(
        body,
        mesh=mesh,
        in_specs=(P("dp", "mp", None), P("dp", "mp", None), P()),
        out_specs=(P("dp", "mp", None), P(None, "mp"), P()),
        check_vma=False,
    )
```

profile of v0, /device:TPU:1, one launch (start us, length us, event | category | flops | bytes accessed | tf_op | source)
XLA Modules:
  0.0 1383.5 jit_solution(1256633599682821178)
XLA Ops:
  7.2 1.9 add.33
  9.1 1.1 fusion.7
  10.2 13.4 psum.36
  23.7 981.2 %while.13 = (s32[]{:T(128)}, f32[16,64]{1,0:T(8,128)S(1)}, f32[16,64]{1,0:T(8,128)S(1)}, s32[]{:T(128)}, s32[]{:T(128)}) while((s32[]{:T(128)}, f32[16,64]{1,0:T(8,128)S(1)}, f32[16,64]{1,0:T(8,128)S(1)}, s32[]{:T(128)}, s32[]{:T(128)}) %tuple.35), condition=%wide.region_5.0_spmd, body=%wide.region_1.0_spmd.sunk | while | flops 24850 | bytes 14697 | solution.py:32
  23.7 0.1 convolution_bitcast_fusion.3
  23.8 35.1 %psum.40 = f32[16]{0:T(128)S(1)} all-reduce(f32[16]{0:T(128)S(1)} %convolution_bitcast_fusion.3), channel_id=1, replica_groups=mesh['dp'=8,'mp'=16] {'mp'}, use_global_device_ids=true, to_apply=%region_2.0 | all-reduce | flops 16 | bytes 128 | tf_op jit(solution)/shard_map/while/body/eval_jaxpr/psum | solution.py:27
  59.0 0.7 multiply_reduce_fusion.2
  59.7 29.2 %psum.41 = f32[]{:T(128)} all-reduce(f32[]{:T(128)} %get-tuple-element.98), channel_id=1, replica_groups=mesh['dp'=8,'mp'=16] {'mp'}, use_global_device_ids=true, to_apply=%region_4.0 | all-reduce | flops 1 | bytes 8 | tf_op jit(solution)/shard_map/while/body/eval_jaxpr/psum | solution.py:29
  89.6 0.1 convolution_bitcast_fusion.3
  89.8 30.2 %psum.40 = f32[16]{0:T(128)S(1)} all-reduce(f32[16]{0:T(128)S(1)} %convolution_bitcast_fusion.3), channel_id=1, replica_groups=mesh['dp'=8,'mp'=16] {'mp'}, use_global_device_ids=true, to_apply=%region_2.0 | all-reduce | flops 16 | bytes 128 | tf_op jit(solution)/shard_map/while/body/eval_jaxpr/psum | solution.py:27
  120.0 0.7 multiply_reduce_fusion.2
  120.7 29.2 %psum.41 = f32[]{:T(128)} all-reduce(f32[]{:T(128)} %get-tuple-element.98), channel_id=1, replica_groups=mesh['dp'=8,'mp'=16] {'mp'}, use_global_device_ids=true, to_apply=%region_4.0 | all-reduce | flops 1 | bytes 8 | tf_op jit(solution)/shard_map/while/body/eval_jaxpr/psum | solution.py:29
  150.7 0.1 convolution_bitcast_fusion.3
  150.8 30.3 %psum.40 = f32[16]{0:T(128)S(1)} all-reduce(f32[16]{0:T(128)S(1)} %convolution_bitcast_fusion.3), channel_id=1, replica_groups=mesh['dp'=8,'mp'=16] {'mp'}, use_global_device_ids=true, to_apply=%region_2.0 | all-reduce | flops 16 | bytes 128 | tf_op jit(solution)/shard_map/while/body/eval_jaxpr/psum | solution.py:27
  181.2 0.7 multiply_reduce_fusion.2
  181.9 29.3 %psum.41 = f32[]{:T(128)} all-reduce(f32[]{:T(128)} %get-tuple-element.98), channel_id=1, replica_groups=mesh['dp'=8,'mp'=16] {'mp'}, use_global_device_ids=true, to_apply=%region_4.0 | all-reduce | flops 1 | bytes 8 | tf_op jit(solution)/shard_map/while/body/eval_jaxpr/psum | solution.py:29
  212.0 0.1 convolution_bitcast_fusion.3
  212.1 30.1 %psum.40 = f32[16]{0:T(128)S(1)} all-reduce(f32[16]{0:T(128)S(1)} %convolution_bitcast_fusion.3), channel_id=1, replica_groups=mesh['dp'=8,'mp'=16] {'mp'}, use_global_device_ids=true, to_apply=%region_2.0 | all-reduce | flops 16 | bytes 128 | tf_op jit(solution)/shard_map/while/body/eval_jaxpr/psum | solution.py:27
  242.3 0.7 multiply_reduce_fusion.2
  243.0 29.2 %psum.41 = f32[]{:T(128)} all-reduce(f32[]{:T(128)} %get-tuple-element.98), channel_id=1, replica_groups=mesh['dp'=8,'mp'=16] {'mp'}, use_global_device_ids=true, to_apply=%region_4.0 | all-reduce | flops 1 | bytes 8 | tf_op jit(solution)/shard_map/while/body/eval_jaxpr/psum | solution.py:29
  273.0 0.1 convolution_bitcast_fusion.3
  273.1 30.1 %psum.40 = f32[16]{0:T(128)S(1)} all-reduce(f32[16]{0:T(128)S(1)} %convolution_bitcast_fusion.3), channel_id=1, replica_groups=mesh['dp'=8,'mp'=16] {'mp'}, use_global_device_ids=true, to_apply=%region_2.0 | all-reduce | flops 16 | bytes 128 | tf_op jit(solution)/shard_map/while/body/eval_jaxpr/psum | solution.py:27
  303.2 0.7 multiply_reduce_fusion.2
  304.0 29.2 %psum.41 = f32[]{:T(128)} all-reduce(f32[]{:T(128)} %get-tuple-element.98), channel_id=1, replica_groups=mesh['dp'=8,'mp'=16] {'mp'}, use_global_device_ids=true, to_apply=%region_4.0 | all-reduce | flops 1 | bytes 8 | tf_op jit(solution)/shard_map/while/body/eval_jaxpr/psum | solution.py:29
  333.9 0.1 convolution_bitcast_fusion.3
  334.1 30.1 %psum.40 = f32[16]{0:T(128)S(1)} all-reduce(f32[16]{0:T(128)S(1)} %convolution_bitcast_fusion.3), channel_id=1, replica_groups=mesh['dp'=8,'mp'=16] {'mp'}, use_global_device_ids=true, to_apply=%region_2.0 | all-reduce | flops 16 | bytes 128 | tf_op jit(solution)/shard_map/while/body/eval_jaxpr/psum | solution.py:27
  364.2 0.7 multiply_reduce_fusion.2
  364.9 29.1 %psum.41 = f32[]{:T(128)} all-reduce(f32[]{:T(128)} %get-tuple-element.98), channel_id=1, replica_groups=mesh['dp'=8,'mp'=16] {'mp'}, use_global_device_ids=true, to_apply=%region_4.0 | all-reduce | flops 1 | bytes 8 | tf_op jit(solution)/shard_map/while/body/eval_jaxpr/psum | solution.py:29
  394.8 0.1 convolution_bitcast_fusion.3
  394.9 30.5 %psum.40 = f32[16]{0:T(128)S(1)} all-reduce(f32[16]{0:T(128)S(1)} %convolution_bitcast_fusion.3), channel_id=1, replica_groups=mesh['dp'=8,'mp'=16] {'mp'}, use_global_device_ids=true, to_apply=%region_2.0 | all-reduce | flops 16 | bytes 128 | tf_op jit(solution)/shard_map/while/body/eval_jaxpr/psum | solution.py:27
  425.4 0.7 multiply_reduce_fusion.2
  426.1 29.3 %psum.41 = f32[]{:T(128)} all-reduce(f32[]{:T(128)} %get-tuple-element.98), channel_id=1, replica_groups=mesh['dp'=8,'mp'=16] {'mp'}, use_global_device_ids=true, to_apply=%region_4.0 | all-reduce | flops 1 | bytes 8 | tf_op jit(solution)/shard_map/while/body/eval_jaxpr/psum | solution.py:29
  456.2 0.1 convolution_bitcast_fusion.3
  456.3 30.1 %psum.40 = f32[16]{0:T(128)S(1)} all-reduce(f32[16]{0:T(128)S(1)} %convolution_bitcast_fusion.3), channel_id=1, replica_groups=mesh['dp'=8,'mp'=16] {'mp'}, use_global_device_ids=true, to_apply=%region_2.0 | all-reduce | flops 16 | bytes 128 | tf_op jit(solution)/shard_map/while/body/eval_jaxpr/psum | solution.py:27
  486.4 0.7 multiply_reduce_fusion.2
  487.1 29.2 %psum.41 = f32[]{:T(128)} all-reduce(f32[]{:T(128)} %get-tuple-element.98), channel_id=1, replica_groups=mesh['dp'=8,'mp'=16] {'mp'}, use_global_device_ids=true, to_apply=%region_4.0 | all-reduce | flops 1 | bytes 8 | tf_op jit(solution)/shard_map/while/body/eval_jaxpr/psum | solution.py:29
  517.2 30.1 %psum.40 = f32[16]{0:T(128)S(1)} all-reduce(f32[16]{0:T(128)S(1)} %convolution_bitcast_fusion.3), channel_id=1, replica_groups=mesh['dp'=8,'mp'=16] {'mp'}, use_global_device_ids=true, to_apply=%region_2.0 | all-reduce | flops 16 | bytes 128 | tf_op jit(solution)/shard_map/while/body/eval_jaxpr/psum | solution.py:27
  547.3 0.7 multiply_reduce_fusion.2
  548.1 29.2 %psum.41 = f32[]{:T(128)} all-reduce(f32[]{:T(128)} %get-tuple-element.98), channel_id=1, replica_groups=mesh['dp'=8,'mp'=16] {'mp'}, use_global_device_ids=true, to_apply=%region_4.0 | all-reduce | flops 1 | bytes 8 | tf_op jit(solution)/shard_map/while/body/eval_jaxpr/psum | solution.py:29
  578.1 30.2 %psum.40 = f32[16]{0:T(128)S(1)} all-reduce(f32[16]{0:T(128)S(1)} %convolution_bitcast_fusion.3), channel_id=1, replica_groups=mesh['dp'=8,'mp'=16] {'mp'}, use_global_device_ids=true, to_apply=%region_2.0 | all-reduce | flops 16 | bytes 128 | tf_op jit(solution)/shard_map/while/body/eval_jaxpr/psum | solution.py:27
  608.3 0.7 multiply_reduce_fusion.2
  609.1 29.1 %psum.41 = f32[]{:T(128)} all-reduce(f32[]{:T(128)} %get-tuple-element.98), channel_id=1, replica_groups=mesh['dp'=8,'mp'=16] {'mp'}, use_global_device_ids=true, to_apply=%region_4.0 | all-reduce | flops 1 | bytes 8 | tf_op jit(solution)/shard_map/while/body/eval_jaxpr/psum | solution.py:29
  639.1 30.5 %psum.40 = f32[16]{0:T(128)S(1)} all-reduce(f32[16]{0:T(128)S(1)} %convolution_bitcast_fusion.3), channel_id=1, replica_groups=mesh['dp'=8,'mp'=16] {'mp'}, use_global_device_ids=true, to_apply=%region_2.0 | all-reduce | flops 16 | bytes 128 | tf_op jit(solution)/shard_map/while/body/eval_jaxpr/psum | solution.py:27
  669.6 0.7 multiply_reduce_fusion.2
  670.3 29.3 %psum.41 = f32[]{:T(128)} all-reduce(f32[]{:T(128)} %get-tuple-element.98), channel_id=1, replica_groups=mesh['dp'=8,'mp'=16] {'mp'}, use_global_device_ids=true, to_apply=%region_4.0 | all-reduce | flops 1 | bytes 8 | tf_op jit(solution)/shard_map/while/body/eval_jaxpr/psum | solution.py:29
  700.5 29.8 %psum.40 = f32[16]{0:T(128)S(1)} all-reduce(f32[16]{0:T(128)S(1)} %convolution_bitcast_fusion.3), channel_id=1, replica_groups=mesh['dp'=8,'mp'=16] {'mp'}, use_global_device_ids=true, to_apply=%region_2.0 | all-reduce | flops 16 | bytes 128 | tf_op jit(solution)/shard_map/while/body/eval_jaxpr/psum | solution.py:27
  730.3 0.7 multiply_reduce_fusion.2
  731.0 29.6 %psum.41 = f32[]{:T(128)} all-reduce(f32[]{:T(128)} %get-tuple-element.98), channel_id=1, replica_groups=mesh['dp'=8,'mp'=16] {'mp'}, use_global_device_ids=true, to_apply=%region_4.0 | all-reduce | flops 1 | bytes 8 | tf_op jit(solution)/shard_map/while/body/eval_jaxpr/psum | solution.py:29
  761.5 29.8 %psum.40 = f32[16]{0:T(128)S(1)} all-reduce(f32[16]{0:T(128)S(1)} %convolution_bitcast_fusion.3), channel_id=1, replica_groups=mesh['dp'=8,'mp'=16] {'mp'}, use_global_device_ids=true, to_apply=%region_2.0 | all-reduce | flops 16 | bytes 128 | tf_op jit(solution)/shard_map/while/body/eval_jaxpr/psum | solution.py:27
  791.3 0.7 multiply_reduce_fusion.2
  792.0 29.5 %psum.41 = f32[]{:T(128)} all-reduce(f32[]{:T(128)} %get-tuple-element.98), channel_id=1, replica_groups=mesh['dp'=8,'mp'=16] {'mp'}, use_global_device_ids=true, to_apply=%region_4.0 | all-reduce | flops 1 | bytes 8 | tf_op jit(solution)/shard_map/while/body/eval_jaxpr/psum | solution.py:29
  822.4 29.8 %psum.40 = f32[16]{0:T(128)S(1)} all-reduce(f32[16]{0:T(128)S(1)} %convolution_bitcast_fusion.3), channel_id=1, replica_groups=mesh['dp'=8,'mp'=16] {'mp'}, use_global_device_ids=true, to_apply=%region_2.0 | all-reduce | flops 16 | bytes 128 | tf_op jit(solution)/shard_map/while/body/eval_jaxpr/psum | solution.py:27
  852.3 0.7 multiply_reduce_fusion.2
  853.0 29.7 %psum.41 = f32[]{:T(128)} all-reduce(f32[]{:T(128)} %get-tuple-element.98), channel_id=1, replica_groups=mesh['dp'=8,'mp'=16] {'mp'}, use_global_device_ids=true, to_apply=%region_4.0 | all-reduce | flops 1 | bytes 8 | tf_op jit(solution)/shard_map/while/body/eval_jaxpr/psum | solution.py:29
  883.6 29.6 %psum.40 = f32[16]{0:T(128)S(1)} all-reduce(f32[16]{0:T(128)S(1)} %convolution_bitcast_fusion.3), channel_id=1, replica_groups=mesh['dp'=8,'mp'=16] {'mp'}, use_global_device_ids=true, to_apply=%region_2.0 | all-reduce | flops 16 | bytes 128 | tf_op jit(solution)/shard_map/while/body/eval_jaxpr/psum | solution.py:27
  913.2 0.7 multiply_reduce_fusion.2
  914.0 29.5 %psum.41 = f32[]{:T(128)} all-reduce(f32[]{:T(128)} %get-tuple-element.98), channel_id=1, replica_groups=mesh['dp'=8,'mp'=16] {'mp'}, use_global_device_ids=true, to_apply=%region_4.0 | all-reduce | flops 1 | bytes 8 | tf_op jit(solution)/shard_map/while/body/eval_jaxpr/psum | solution.py:29
  944.3 29.6 %psum.40 = f32[16]{0:T(128)S(1)} all-reduce(f32[16]{0:T(128)S(1)} %convolution_bitcast_fusion.3), channel_id=1, replica_groups=mesh['dp'=8,'mp'=16] {'mp'}, use_global_device_ids=true, to_apply=%region_2.0 | all-reduce | flops 16 | bytes 128 | tf_op jit(solution)/shard_map/while/body/eval_jaxpr/psum | solution.py:27
  973.9 0.7 multiply_reduce_fusion.2
  974.7 29.4 %psum.41 = f32[]{:T(128)} all-reduce(f32[]{:T(128)} %get-tuple-element.98), channel_id=1, replica_groups=mesh['dp'=8,'mp'=16] {'mp'}, use_global_device_ids=true, to_apply=%region_4.0 | all-reduce | flops 1 | bytes 8 | tf_op jit(solution)/shard_map/while/body/eval_jaxpr/psum | solution.py:29
  1004.9 1.5 fusion.3
  1006.4 367.0 %all-reduce.2.cloned.1.call-done = f32[16,5120]{1,0:T(8,128)} async-done(((f32[16,5120]{1,0:T(8,128)}), f32[16,5120]{1,0:T(8,128)}) %all-reduce.2.cloned.1.call-update) | async-done | bytes 327696 | tf_op jit(solution)/shard_map/psum | solution.py:34
  1373.3 1.0 broadcast_multiply_fusion
  1374.4 2.3 fusion.2
  (50 shorter events, 1.8 us)
Async XLA Ops:
  7.2 1.9 copy-start
  7.2 1366.2 %all-reduce.2.cloned.1.call-start = ((), (), s32[]{:S(2)}) async-start(), calls=%async_computation | async-start | bytes 655360 | tf_op jit(solution)/shard_map/psum | solution.py:34
  1004.9 369.5 %copy-start.1 = (f32[16,64]{1,0:T(8,128)}, f32[16,64]{1,0:T(8,128)S(1)}, u32[]{:S(2)}) copy-start(f32[16,64]{1,0:T(8,128)S(1)} %get-tuple-element.65) | copy-start | bytes 12292
  1374.3 2.3 copy-start.2
Sparse Core Ops, SparseCore 0:
  1006.5 366.8 all-reduce.1
where the time goes:
time: 1380 us
  blocking collectives  969 us (70%)
  waiting for transfers between devices  367 us (27%)
  matrix products  18.8 us (1%)
  between operations  14.1 us (1%)
    psum x16, blocking collectives, one_row(): coefs = lax.psum(contract(finished, target, 1, 1), 'mp')  486 us
    psum x16, blocking collectives, one_row(): length = lax.psum(jnp.sum(remain * remain), 'mp')  469 us
    psum x1, waiting for transfers between devices, body(): q_factor = lax.psum(q_term, ('dp', 'mp')) / replicas  367 us
  transfers between devices with their start and end apart: 1, of which 1 were waited for; matrix products, arithmetic and copies ran while one was open for 0% of the time, Pallas kernels for 0%

commit v1 on v0

v1 whole, which is shorter than its diff:
```python
import functools

import jax
import jax.numpy as jnp
from jax import lax
from jax.experimental import pallas as pl
from jax.experimental.pallas import tpu as pltpu
from jax.sharding import PartitionSpec as P

LANES = 128
SUBLANES = 8
STEPS = 4


def dot(left, right, left_dim, right_dim):
    return lax.dot_general(
        left,
        right,
        (((left_dim,), (right_dim,)), ((), ())),
        precision=lax.Precision.HIGHEST,
        preferred_element_type=jnp.float32,
    )


def correct_kernel(g_ref, f_ref, q_ref, c_ref, p_ref, acc):
    step = pl.program_id(0)
    local = g_ref[0] + f_ref[0]
    c_ref[...] = local
    part = dot(q_ref[...], local, 1, 1)

    @pl.when(step == 0)
    def _():
        acc[...] = part

    @pl.when(step > 0)
    def _():
        acc[...] += part

    @pl.when(step == pl.num_programs(0) - 1)
    def _():
        half = acc.shape[0] // 2
        packed = jnp.concatenate([acc[:half], acc[half:]], axis=1)
        p_ref[...] = jnp.broadcast_to(packed[None], p_ref.shape)


def group_mask(rank):
    row = lax.broadcasted_iota(jnp.int32, (rank, LANES), 0)
    lane = lax.broadcasted_iota(jnp.int32, (rank, LANES), 1)
    return lane - rank * (row % SUBLANES)


def project_kernel(p_ref, c_ref, msg_ref, mean_ref):
    total = p_ref[0]
    for n in range(1, p_ref.shape[0]):
        total = total + p_ref[n]
    total = total * (1.0 / p_ref.shape[0])
    half = total.shape[1] // 2
    mean = jnp.concatenate([total[:, :half], total[:, half:]], axis=0)
    mean_ref[...] = mean
    rank = mean.shape[0]
    groups = SUBLANES
    width = c_ref.shape[1] // groups
    for j in range(groups):
        out = dot(mean, c_ref[:, j * width : (j + 1) * width], 1, 0)
        for i in range(width // LANES):
            msg_ref[pl.ds(j * SUBLANES + i, rank, stride=groups * SUBLANES), :] = out[:, i * LANES : (i + 1) * LANES]
    tiled = jnp.concatenate([mean] * (LANES // rank), axis=0)
    gram = dot(mean, tiled, 1, 1)
    at = group_mask(rank)
    gram = jnp.where((at >= 0) & (at < rank), gram, 0.0)
    peers = msg_ref.shape[0] // SUBLANES
    for h in range(rank // SUBLANES):
        line = jnp.sum(gram[h * SUBLANES : (h + 1) * SUBLANES], axis=0, keepdims=True)
        msg_ref[pl.ds(5 + h, peers, stride=SUBLANES), :] = jnp.broadcast_to(line, (peers, LANES))
    msg_ref[pl.ds(7, peers, stride=SUBLANES), :] = jnp.zeros((peers, LANES), jnp.float32)


def sum_kernel(in_ref, out_ref):
    out_ref[...] = jnp.broadcast_to(jnp.sum(in_ref[...], axis=0, keepdims=True), out_ref.shape)


def inverse_factor(lines, rank, replicas):
    spread = jnp.concatenate(
        [jnp.broadcast_to(lines[h : h + 1], (SUBLANES, LANES)) for h in range(rank // SUBLANES)], axis=0
    ) * (1.0 / replicas)
    at = group_mask(rank)
    row = lax.broadcasted_iota(jnp.int32, (rank, LANES), 0)
    lane = lax.broadcasted_iota(jnp.int32, (rank, LANES), 1)
    cols = [
        jnp.broadcast_to(jnp.sum(jnp.where(at == j, spread, 0.0), axis=1, keepdims=True), (rank, LANES))
        for j in range(rank)
    ]
    right = jnp.where(row == lane, 1.0, 0.0)
    pivots = jnp.ones((rank, LANES), jnp.float32)
    for k in range(rank):
        pivot = cols[k][k : k + 1]
        pivots = jnp.where(row == k, pivot, pivots)
        factor = jnp.where(row > k, cols[k] * (1.0 / pivot), 0.0)
        for j in range(k + 1, rank):
            cols[j] = cols[j] - factor * cols[j][k : k + 1]
        right = right - factor * right[k : k + 1]
    return right * (1.0 / jnp.sqrt(pivots))


def finish_kernel(replicas, own_ref, all_ref, mean_ref, c_ref, nf_ref, po_ref, qf_ref, inv, ortho):
    step = pl.program_id(0)
    rank = mean_ref.shape[0]

    @pl.when(step == 0)
    def _():
        whole = inverse_factor(own_ref[5:7, :], rank, replicas)
        inv[...] = whole
        ortho[...] = dot(whole[:, :rank], mean_ref[...], 1, 0)
        po_ref[...] = ortho[...]

    block = c_ref.shape[1]
    per_group = all_ref.shape[0] // rank // SUBLANES
    width = block * pl.num_programs(0) // per_group
    lower = inv[:, :rank]
    left = ortho[...]
    for jj in range(block // width):
        j = step * (block // width) + jj
        raw = jnp.concatenate(
            [
                all_ref[pl.ds(j * SUBLANES + i, rank, stride=per_group * SUBLANES), :]
                for i in range(width // LANES)
            ],
            axis=1,
        ) * (1.0 / replicas)
        factor = dot(lower, raw, 1, 0)
        cols = slice(jj * width, (jj + 1) * width)
        qf_ref[:, cols] = factor
        nf_ref[0, :, cols] = c_ref[:, cols] - dot(left, factor, 0, 0)


def body(gradient, feedback, q_previous):
    f32 = jnp.float32
    dp, mp = lax.axis_size("dp"), lax.axis_size("mp")
    _, rows, width = gradient.shape
    rank = q_previous.shape[0]
    block = width // STEPS
    peers = dp * mp
    vmem = pl.BlockSpec(memory_space=pltpu.VMEM)
    params = pltpu.CompilerParams(vmem_limit_bytes=16 * 2**20)

    local, p_out = pl.pallas_call(
        correct_kernel,
        grid=(STEPS,),
        in_specs=[
            pl.BlockSpec((1, rows, block), lambda i: (0, 0, i)),
            pl.BlockSpec((1, rows, block), lambda i: (0, 0, i)),
            pl.BlockSpec((rank, block), lambda i: (0, i)),
        ],
        out_specs=[
            pl.BlockSpec((rows, block), lambda i: (0, i)),
            pl.BlockSpec((dp, rank // 2, 2 * rows), lambda i: (0, 0, 0)),
        ],
        out_shape=[
            jax.ShapeDtypeStruct((rows, width), f32),
            jax.ShapeDtypeStruct((dp, rank // 2, 2 * rows), f32),
        ],
        scratch_shapes=[pltpu.VMEM((rank, rows), f32)],
        compiler_params=params,
        name="correct",
    )(gradient, feedback, q_previous)
    p_all = lax.all_to_all(p_out, "dp", 0, 0, tiled=True)

    msg, p_mean = pl.pallas_call(
        project_kernel,
        in_specs=[vmem, vmem],
        out_specs=[vmem, vmem],
        out_shape=[
            jax.ShapeDtypeStruct((peers * SUBLANES, LANES), f32),
            jax.ShapeDtypeStruct((rank, rows), f32),
        ],
        compiler_params=params,
        name="project",
    )(p_all, local)
    terms = lax.all_to_all(msg.reshape(peers, SUBLANES, LANES), ("dp", "mp"), 0, 0, tiled=True)

    own = pl.pallas_call(
        sum_kernel,
        in_specs=[vmem],
        out_specs=vmem,
        out_shape=jax.ShapeDtypeStruct((peers, SUBLANES, LANES), f32),
        compiler_params=params,
        name="sum_terms",
    )(terms)
    whole = lax.all_to_all(own, ("dp", "mp"), 0, 0, tiled=True)

    new_feedback, p_ortho, q_factor = pl.pallas_call(
        functools.partial(finish_kernel, dp),
        grid=(STEPS,),
        in_specs=[
            pl.BlockSpec((SUBLANES, LANES), lambda i: (0, 0)),
            pl.BlockSpec((peers * SUBLANES, LANES), lambda i: (0, 0)),
            pl.BlockSpec((rank, rows), lambda i: (0, 0)),
            pl.BlockSpec((rows, block), lambda i: (0, i)),
        ],
        out_specs=[
            pl.BlockSpec((1, rows, block), lambda i: (0, 0, i)),
            pl.BlockSpec((rank, rows), lambda i: (0, 0)),
            pl.BlockSpec((rank, block), lambda i: (0, i)),
        ],
        out_shape=[
            jax.ShapeDtypeStruct((1, rows, width), f32),
            jax.ShapeDtypeStruct((rank, rows), f32),
            jax.ShapeDtypeStruct((rank, width), f32),
        ],
        scratch_shapes=[pltpu.VMEM((rank, LANES), f32), pltpu.VMEM((rank, rows), f32)],
        compiler_params=params,
        name="finish",
    )(own.reshape(peers * SUBLANES, LANES), whole.reshape(peers * SUBLANES, LANES), p_mean, local)
    return (new_feedback, p_ortho, q_factor)


def solution(mesh):
    return jax.shard_map(
        body,
        mesh=mesh,
        in_specs=(P("dp", "mp", None), P("dp", "mp", None), P()),
        out_specs=(P("dp", "mp", None), P(None, "mp"), P()),
        check_vma=False,
    )
```

time: 1380 us -> 62.8 us (0.05)
  blocking collectives: 969 us -> 50.9 us
  waiting for transfers between devices: 367 us -> 0 us
  matrix products: 18.8 us -> 0 us
    psum x33 -> x0, blocking collectives: 969 us -> none  [the longest x16 486 us: one_row(): coefs = lax.psum(contract(finished, target, 1, 1), 'mp')]
    psum x1 -> x0, waiting for transfers between devices: 367 us -> none  [body(): q_factor = lax.psum(q_term, ('dp', 'mp')) / replicas]
    all_to_all x0 -> x3, blocking collectives: none -> 50.9 us  [the longest x1 22.8 us: body(): lax.all_to_all(msg.reshape(peers, SUBLANES, LANES), ('dp', 'mp'), 0, 0, t...]
    dot_general x35 -> x0, matrix products: 18.8 us -> none  [contract(): lax.dot_general(left, right, (((left_dim,), (right_dim,)), ((), ())), pre...]
  transfers between devices with their start and end apart: 1 -> 0, of which waited for: 1 -> 0; matrix products, arithmetic and copies ran while one was open for 0% -> 0% of each run, Pallas kernels for 0% -> 0%
where the time goes in v1:
time: 62.8 us; the launch traced here: 62.5 us
  blocking collectives  50.9 us (81%)
  Pallas kernels  7.33 us (12%)
  local copies, waits for them, and re-layouts  3.6 us (6%)
  between operations  0.66 us (1%)
    all_to_all x1, blocking collectives, body(): lax.all_to_all(msg.reshape(peers, SUBLANES, LANES), ('dp', 'mp'), 0, 0, t...  22.8 us
    all_to_all x1, blocking collectives, body(): whole = lax.all_to_all(own, ('dp', 'mp'), 0, 0, tiled=True)  17.9 us
    all_to_all x1, blocking collectives, body(): p_all = lax.all_to_all(p_out, 'dp', 0, 0, tiled=True)  10.3 us
    pallas_call x1, Pallas kernels, body(): pl.pallas_call(functools.partial(finish_kernel, dp), grid=(STEPS,), in_sp...  4.21 us
    unnamed x6, local copies, waits for them, and re-layouts  3.6 us
    pallas_call x1, Pallas kernels, body(): pl.pallas_call(correct_kernel, grid=(STEPS,), in_specs=[pl.BlockSpec((1,...  1.99 us

profile of v1, /device:TPU:1, one launch (start us, length us, event | category | flops | bytes accessed | tf_op | source)
XLA Modules:
  0.0 62.5 jit_solution(5809651732130383577)
XLA Ops:
  0.6 0.0 copy-start
  0.6 1.3 %copy-done = f32[1,64,5120]{2,1,0:T(8,128)S(1)} copy-done((f32[1,64,5120]{2,1,0:T(8,128)S(1)}, f32[1,64,5120]{2,1,0:T(8,128)}, u32[]{:S(2)}) %copy-start) | copy-done | bytes 1310744
  1.9 0.0 copy-start.1
  1.9 1.3 %copy-done.1 = f32[1,64,5120]{2,1,0:T(8,128)S(1)} copy-done((f32[1,64,5120]{2,1,0:T(8,128)S(1)}, f32[1,64,5120]{2,1,0:T(8,128)}, u32[]{:S(2)}) %copy-start.1) | copy-done | bytes 1310744
  3.3 0.0 copy-start.2
  3.3 1.0 %copy-done.2 = f32[16,5120]{1,0:T(8,128)S(1)} copy-done((f32[16,5120]{1,0:T(8,128)S(1)}, f32[16,5120]{1,0:T(8,128)}, u32[]{:S(2)}) %copy-start.2) | copy-done | bytes 327704
  4.2 2.0 %correct.1 = (f32[64,5120]{1,0:T(8,128)S(1)}, f32[8,8,128]{2,1,0:T(8,128)S(1)}) custom-call(f32[1,64,5120]{2,1,0:T(8,128)S(1)} %copy-done, f32[1,64,5120]{2,1,0:T(8,128)S(1)} %copy-done.1, f32[16,5120]{1,0:T(8,128)S(1)} %copy-done.2), custom_call_target="tpu_custom_call" | custom-call | tf_op jit(solution)/shard_map/correct/pallas_call | solution.py:146
  6.2 10.3 %all_to_all.15.p_ref = f32[8,8,128]{2,1,0:T(8,128)S(1)} all-to-all(f32[8,8,128]{2,1,0:T(8,128)S(1)} %get-tuple-element.7), channel_id=1, replica_groups=mesh['dp'=8,'mp'=16] {'dp'}, dimensions={0} | all-to-all | bytes 65536 | tf_op jit(solution)/shard_map/all_to_all | solution.py:166
  16.6 1.0 %project.1 = (f32[1024,128]{1,0:T(8,128)S(1)}, f32[16,64]{1,0:T(8,128)S(1)}) custom-call(f32[8,8,128]{2,1,0:T(8,128)S(1)} %all_to_all.15.p_ref, f32[64,5120]{1,0:T(8,128)S(1)} %get-tuple-element.8.c_ref), custom_call_target="tpu_custom_call" | custom-call | tf_op jit(solution)/shard_map/project/pallas_call | solution.py:168
  17.5 22.8 %all_to_all.16.in_ref = f32[128,8,128]{2,1,0:T(8,128)S(1)} all-to-all(f32[128,8,128]{2,1,0:T(8,128)S(1)} %bitcast.5), channel_id=1, replica_groups=mesh['dp'=8,'mp'=16] {'dp','mp'}, dimensions={0} | all-to-all | bytes 1048576 | tf_op jit(solution)/shard_map/all_to_all | solution.py:179
  40.3 0.2 sum_terms.1
  40.4 17.9 %all_to_all.17 = f32[128,8,128]{2,1,0:T(8,128)S(1)} all-to-all(f32[128,8,128]{2,1,0:T(8,128)S(1)} %sum_terms.1), channel_id=1, replica_groups=mesh['dp'=8,'mp'=16] {'dp','mp'}, dimensions={0} | all-to-all | bytes 1048576 | tf_op jit(solution)/shard_map/all_to_all | solution.py:189
  58.3 4.2 %finish.1 = (f32[1,64,5120]{2,1,0:T(8,128)}, f32[16,64]{1,0:T(8,128)}, f32[16,5120]{1,0:T(8,128)}) custom-call(f32[1024,128]{1,0:T(8,128)S(1)} %bitcast.3, f32[1024,128]{1,0:T(8,128)S(1)} %bitcast.4, f32[16,64]{1,0:T(8,128)S(1)} %get-tuple-element.10.mean_ref, f32[64,5120]{1,0:T(8,128)S(1)} %get-tuple-element.8.c_ref), custom_call_target="tpu_custom_call" | custom-call | tf_op jit(solution)/shard_map/finish/pallas_call | solution.py:191
Async XLA Ops:
  0.6 1.3 %copy-start = (f32[1,64,5120]{2,1,0:T(8,128)S(1)}, f32[1,64,5120]{2,1,0:T(8,128)}, u32[]{:S(2)}) copy-start(f32[1,64,5120]{2,1,0:T(8,128)} %g_ref.1) | copy-start | bytes 3932164
  1.9 1.3 %copy-start.1 = (f32[1,64,5120]{2,1,0:T(8,128)S(1)}, f32[1,64,5120]{2,1,0:T(8,128)}, u32[]{:S(2)}) copy-start(f32[1,64,5120]{2,1,0:T(8,128)} %f_ref.1) | copy-start | bytes 3932164
  3.3 1.0 %copy-start.2 = (f32[16,5120]{1,0:T(8,128)S(1)}, f32[16,5120]{1,0:T(8,128)}, u32[]{:S(2)}) copy-start(f32[16,5120]{1,0:T(8,128)} %q_ref.1) | copy-start | bytes 983044

commit v2 on v0

v2 whole, which is shorter than its diff:
```python
import functools

import jax
import jax.numpy as jnp
from jax import lax
from jax.experimental import pallas as pl
from jax.experimental.pallas import tpu as pltpu
from jax.sharding import PartitionSpec as P

LANES = 128
IN_PARTS = 5
GROUPS = 8


def dot(left, right, left_dim, right_dim):
    return lax.dot_general(
        left,
        right,
        (((left_dim,), (right_dim,)), ((), ())),
        precision=lax.Precision.HIGHEST,
        preferred_element_type=jnp.float32,
    )


def correct_kernel(g_hbm, f_hbm, q_hbm, p_ref, g_buf, f_buf, q_buf, sems):
    width = g_buf.shape[1] // IN_PARTS
    copies = []
    for s in range(IN_PARTS):
        cols = pl.ds(s * width, width)
        part = [
            pltpu.make_async_copy(g_hbm.at[0, :, cols], g_buf.at[:, cols], sems.at[0, s]),
            pltpu.make_async_copy(f_hbm.at[0, :, cols], f_buf.at[:, cols], sems.at[1, s]),
            pltpu.make_async_copy(q_hbm.at[:, cols], q_buf.at[:, cols], sems.at[2, s]),
        ]
        for copy in part:
            copy.start()
        copies.append(part)
    total = None
    for s in range(IN_PARTS):
        for copy in copies[s]:
            copy.wait()
        cols = slice(s * width, (s + 1) * width)
        local = g_buf[:, cols] + f_buf[:, cols]
        part = dot(q_buf[:, cols], local, 1, 1)
        total = part if total is None else total + part
    half = total.shape[0] // 2
    packed = jnp.concatenate([total[:half], total[half:]], axis=1)
    p_ref[...] = jnp.broadcast_to(packed[None], p_ref.shape)


def project_kernel(p_ref, g_ref, f_ref, msg_ref, mean_ref, c_ref):
    replicas = p_ref.shape[0]
    total = p_ref[0]
    for n in range(1, replicas):
        total = total + p_ref[n]
    total = total * (1.0 / replicas)
    half = total.shape[1] // 2
    mean = jnp.concatenate([total[:, :half], total[:, half:]], axis=0)
    mean_ref[...] = mean
    rank = mean.shape[0]
    peers = rank * GROUPS
    length = msg_ref.shape[0] // peers
    width = c_ref.shape[1] // GROUPS
    tiles = width // LANES
    for j in range(GROUPS):
        cols = slice(j * width, (j + 1) * width)
        local = g_ref[0, :, cols] + f_ref[0, :, cols]
        c_ref[:, cols] = local
        out = dot(mean, local, 1, 0)
        for i in range(tiles):
            msg_ref[pl.ds(j * length + i, rank, stride=GROUPS * length), :] = out[:, i * LANES : (i + 1) * LANES]
    tiled = jnp.concatenate([mean] * (LANES // rank), axis=0)
    gram = dot(mean, tiled, 1, 1)
    share = rank // replicas
    row = lax.broadcasted_iota(jnp.int32, (rank, LANES), 0)
    lane = lax.broadcasted_iota(jnp.int32, (rank, LANES), 1)
    mine = row - share * lax.axis_index("dp")
    kept = (lane >= rank * mine) & (lane < rank * (mine + 1)) & (mine >= 0) & (mine < share)
    line = jnp.sum(jnp.where(kept, gram, 0.0), axis=0, keepdims=True)
    msg_ref[pl.ds(tiles, peers, stride=length), :] = jnp.broadcast_to(line, (peers, LANES))


def sum_kernel(replicas, in_ref, out_ref, gram_ref, part):
    peers = in_ref.shape[0] // 6
    total = in_ref[0:24]
    for s in range(1, peers // 4):
        total = total + in_ref[24 * s : 24 * (s + 1)]
    part[...] = total
    for i in range(5):
        line = jnp.sum(part[pl.ds(i, 4, stride=6), :], axis=0, keepdims=True)
        out_ref[pl.ds(i, peers, stride=5), :] = jnp.broadcast_to(line, (peers, LANES))
    shards = peers // replicas
    for n in range(replicas):
        terms = in_ref[pl.ds(n * shards * 6 + 5, shards, stride=6), :]
        line = jnp.sum(terms, axis=0, keepdims=True)
        share = gram_ref.shape[0] // replicas
        gram_ref[n * share : (n + 1) * share, :] = jnp.broadcast_to(line, (share, LANES))


def inverse_factor(spread, replicas):
    rank = spread.shape[0]
    share = rank // replicas
    row = lax.broadcasted_iota(jnp.int32, (rank, LANES), 0)
    lane = lax.broadcasted_iota(jnp.int32, (rank, LANES), 1)
    at = lane - rank * (row % share)
    cols = [
        jnp.broadcast_to(jnp.sum(jnp.where(at == j, spread, 0.0), axis=1, keepdims=True), (rank, LANES))
        for j in range(rank)
    ]
    right = jnp.where(row == lane, 1.0, 0.0)
    pivots = jnp.ones((rank, LANES), jnp.float32)
    for k in range(rank):
        pivot = cols[k][k : k + 1]
        pivots = jnp.where(row == k, pivot, pivots)
        factor = jnp.where(row > k, cols[k] * (1.0 / pivot), 0.0)
        for j in range(k + 1, rank):
            cols[j] = cols[j] - factor * cols[j][k : k + 1]
        right = right - factor * right[k : k + 1]
    return right * (1.0 / jnp.sqrt(pivots))


def finish_kernel(replicas, gram_ref, all_ref, mean_ref, c_ref, nf_hbm, po_ref, qf_hbm, nf_buf, qf_buf, sems):
    rank = mean_ref.shape[0]
    whole = inverse_factor(gram_ref[...], replicas)
    lower = whole[:, :rank]
    left = dot(lower, mean_ref[...], 1, 0)
    po_ref[...] = left
    scaled = lower * (1.0 / replicas)
    width = c_ref.shape[1] // GROUPS
    tiles = width // LANES
    copies = []
    for j in range(GROUPS):
        raw = jnp.concatenate(
            [all_ref[pl.ds(j * tiles + i, rank, stride=GROUPS * tiles), :] for i in range(tiles)], axis=1
        )
        factor = dot(scaled, raw, 1, 0)
        cols = slice(j * width, (j + 1) * width)
        qf_buf[:, cols] = factor
        nf_buf[:, cols] = c_ref[:, cols] - dot(left, factor, 0, 0)
        at = pl.ds(j * width, width)
        part = [
            pltpu.make_async_copy(nf_buf.at[:, at], nf_hbm.at[0, :, at], sems.at[0, j]),
            pltpu.make_async_copy(qf_buf.at[:, at], qf_hbm.at[:, at], sems.at[1, j]),
        ]
        for copy in part:
            copy.start()
        copies += part
    for copy in copies:
        copy.wait()


def body(gradient, feedback, q_previous):
    f32 = jnp.float32
    dp, mp = lax.axis_size("dp"), lax.axis_size("mp")
    _, rows, width = gradient.shape
    rank = q_previous.shape[0]
    peers = dp * mp
    tiles = width // GROUPS // LANES
    vmem = pl.BlockSpec(memory_space=pltpu.VMEM)
    hbm = pl.BlockSpec(memory_space=pltpu.HBM)
    params = pltpu.CompilerParams(vmem_limit_bytes=16 * 2**20)

    p_out = pl.pallas_call(
        correct_kernel,
        in_specs=[hbm, hbm, hbm],
        out_specs=vmem,
        out_shape=jax.ShapeDtypeStruct((dp, rank // 2, 2 * rows), f32),
        scratch_shapes=[
            pltpu.VMEM((rows, width), f32),
            pltpu.VMEM((rows, width), f32),
            pltpu.VMEM((rank, width), f32),
            pltpu.SemaphoreType.DMA((3, IN_PARTS)),
        ],
        compiler_params=pltpu.CompilerParams(vmem_limit_bytes=60 * 2**20),
        name="correct",
    )(gradient, feedback, q_previous)
    p_all = lax.all_to_all(p_out, "dp", 0, 0, tiled=True)

    msg, p_mean, local = pl.pallas_call(
        project_kernel,
        in_specs=[vmem] * 3,
        out_specs=[vmem] * 3,
        out_shape=[
            jax.ShapeDtypeStruct((peers * (tiles + 1), LANES), f32),
            jax.ShapeDtypeStruct((rank, rows), f32),
            jax.ShapeDtypeStruct((rows, width), f32),
        ],
        compiler_params=params,
        name="project",
    )(p_all, gradient, feedback)
    msg = msg.reshape(peers, 1, (tiles + 1) * LANES)
    terms = lax.all_to_all(msg, ("dp", "mp"), 0, 0, tiled=True)

    own, gram = pl.pallas_call(
        functools.partial(sum_kernel, dp),
        in_specs=[vmem],
        out_specs=[vmem, vmem],
        out_shape=[
            jax.ShapeDtypeStruct((peers * tiles, LANES), f32),
            jax.ShapeDtypeStruct((rank, LANES), f32),
        ],
        scratch_shapes=[pltpu.VMEM((24, LANES), f32)],
        compiler_params=params,
        name="sum_terms",
    )(terms.reshape(peers * (tiles + 1), LANES))
    own = own.reshape(peers, 1, tiles * LANES)
    whole = lax.all_to_all(own, ("dp", "mp"), 0, 0, tiled=True)

    new_feedback, p_ortho, q_factor = pl.pallas_call(
        functools.partial(finish_kernel, dp),
        in_specs=[vmem] * 4,
        out_specs=[hbm, vmem, hbm],
        out_shape=[
            jax.ShapeDtypeStruct((1, rows, width), f32),
            jax.ShapeDtypeStruct((rank, rows), f32),
            jax.ShapeDtypeStruct((rank, width), f32),
        ],
        scratch_shapes=[
            pltpu.VMEM((rows, width), f32),
            pltpu.VMEM((rank, width), f32),
            pltpu.SemaphoreType.DMA((2, GROUPS)),
        ],
        compiler_params=params,
        name="finish",
    )(gram, whole.reshape(peers * tiles, LANES), p_mean, local)
    return (new_feedback, p_ortho, q_factor)


def solution(mesh):
    return jax.shard_map(
        body,
        mesh=mesh,
        in_specs=(P("dp", "mp", None), P("dp", "mp", None), P()),
        out_specs=(P("dp", "mp", None), P(None, "mp"), P()),
        check_vma=False,
    )
```

time: 1380 us -> 58.4 us (0.04)
  blocking collectives: 969 us -> 47.9 us
  waiting for transfers between devices: 367 us -> 0 us
  matrix products: 18.8 us -> 0 us
    psum x33 -> x0, blocking collectives: 969 us -> none  [the longest x16 486 us: one_row(): coefs = lax.psum(contract(finished, target, 1, 1), 'mp')]
    psum x1 -> x0, waiting for transfers between devices: 367 us -> none  [body(): q_factor = lax.psum(q_term, ('dp', 'mp')) / replicas]
    all_to_all x0 -> x3, blocking collectives: none -> 47.9 us  [the longest x1 21.4 us: body(): terms = lax.all_to_all(msg, ('dp', 'mp'), 0, 0, tiled=True)]
    dot_general x35 -> x0, matrix products: 18.8 us -> none  [contract(): lax.dot_general(left, right, (((left_dim,), (right_dim,)), ((), ())), pre...]
  transfers between devices with their start and end apart: 1 -> 0, of which waited for: 1 -> 0; matrix products, arithmetic and copies ran while one was open for 0% -> 0% of each run, Pallas kernels for 0% -> 0%
where the time goes in v2:
time: 58.4 us; the launch traced here: 58.1 us
  blocking collectives  47.9 us (82%)
  Pallas kernels  9.61 us (16%)
  between operations  0.67 us (1%)
    all_to_all x1, blocking collectives, body(): terms = lax.all_to_all(msg, ('dp', 'mp'), 0, 0, tiled=True)  21.4 us
    all_to_all x1, blocking collectives, body(): whole = lax.all_to_all(own, ('dp', 'mp'), 0, 0, tiled=True)  15.9 us
    all_to_all x1, blocking collectives, body(): p_all = lax.all_to_all(p_out, 'dp', 0, 0, tiled=True)  10.5 us
    pallas_call x1, Pallas kernels, body(): pl.pallas_call(functools.partial(finish_kernel, dp), in_specs=[vmem] * 4,...  4.33 us
    pallas_call x1, Pallas kernels, body(): pl.pallas_call(correct_kernel, in_specs=[hbm, hbm, hbm], out_specs=vmem,...  4.26 us

profile of v2, /device:TPU:1, one launch (start us, length us, event | category | flops | bytes accessed | tf_op | source)
XLA Modules:
  0.0 58.1 jit_solution(2253771147808831395)
XLA Ops:
  0.6 0.0 copy-start.1
  0.6 0.0 copy-start
  0.7 4.3 %correct.1 = f32[8,8,128]{2,1,0:T(8,128)} custom-call(f32[1,64,5120]{2,1,0:T(8,128)} %g_ref.1, f32[1,64,5120]{2,1,0:T(8,128)} %f_ref.1, f32[16,5120]{1,0:T(8,128)} %q_hbm.1), custom_call_target="tpu_custom_call" | custom-call | tf_op jit(solution)/shard_map/correct/pallas_call | solution.py:163
  4.9 10.5 %all_to_all.15.p_ref = f32[8,8,128]{2,1,0:T(8,128)S(1)} all-to-all(f32[8,8,128]{2,1,0:T(8,128)} %correct.1), channel_id=1, replica_groups=mesh['dp'=8,'mp'=16] {'dp'}, dimensions={0} | all-to-all | bytes 65536 | tf_op jit(solution)/shard_map/all_to_all | solution.py:177
  15.4 0.0 copy-done.1
  15.5 0.0 copy-done
  15.5 0.9 %project.1 = (f32[768,128]{1,0:T(8,128)S(1)}, f32[16,64]{1,0:T(8,128)S(1)}, f32[64,5120]{1,0:T(8,128)S(1)}) custom-call(f32[8,8,128]{2,1,0:T(8,128)S(1)} %all_to_all.15.p_ref, f32[1,64,5120]{2,1,0:T(8,128)S(1)} %copy-done, f32[1,64,5120]{2,1,0:T(8,128)S(1)} %copy-done.1), custom_call_target="tpu_custom_call" | custom-call | tf_op jit(solution)/shard_map/project/pallas_call | solution.py:179
  16.4 21.4 %all_to_all.16 = f32[128,1,768]{2,1,0:T(1,128)S(1)} all-to-all(f32[128,1,768]{2,1,0:T(1,128)S(1)} %bitcast.6), channel_id=1, replica_groups=mesh['dp'=8,'mp'=16] {'dp','mp'}, dimensions={0} | all-to-all | bytes 786432 | tf_op jit(solution)/shard_map/all_to_all | solution.py:192
  37.8 0.1 sum_terms.1
  37.9 15.9 %all_to_all.17 = f32[128,1,640]{2,1,0:T(1,128)S(1)} all-to-all(f32[128,1,640]{2,1,0:T(1,128)S(1)} %bitcast.7), channel_id=1, replica_groups=mesh['dp'=8,'mp'=16] {'dp','mp'}, dimensions={0} | all-to-all | bytes 655360 | tf_op jit(solution)/shard_map/all_to_all | solution.py:207
  53.8 4.3 %finish.1 = (f32[1,64,5120]{2,1,0:T(8,128)}, f32[16,64]{1,0:T(8,128)}, f32[16,5120]{1,0:T(8,128)}) custom-call(f32[16,128]{1,0:T(8,128)S(1)} %get-tuple-element.9.gram_ref, f32[640,128]{1,0:T(8,128)S(1)} %bitcast.5, f32[16,64]{1,0:T(8,128)S(1)} %get-tuple-element.11.mean_ref, f32[64,5120]{1,0:T(8,128)S(1)} %get-tuple-element.12.c_ref), custom_call_target="tpu_custom_call" | custom-call | tf_op jit(solution)/shard_map/finish/pallas_call | solution.py:209
Async XLA Ops:
  0.6 14.8 %copy-start.1 = (f32[1,64,5120]{2,1,0:T(8,128)S(1)}, f32[1,64,5120]{2,1,0:T(8,128)}, u32[]{:S(2)}) copy-start(f32[1,64,5120]{2,1,0:T(8,128)} %f_ref.1) | copy-start | bytes 3932164
  0.6 14.8 %copy-start = (f32[1,64,5120]{2,1,0:T(8,128)S(1)}, f32[1,64,5120]{2,1,0:T(8,128)}, u32[]{:S(2)}) copy-start(f32[1,64,5120]{2,1,0:T(8,128)} %g_ref.1) | copy-start | bytes 3932164

commit v3 on v2

--- a/solution.py
+++ b/solution.py
@@ -9,6 +9,7 @@
 
 LANES = 128
 IN_PARTS = 5
+IN_TILE = 512
 GROUPS = 8
 
 
@@ -20,6 +21,25 @@
         precision=lax.Precision.HIGHEST,
         preferred_element_type=jnp.float32,
     )
+
+
+def split(x):
+    high = x.astype(jnp.bfloat16)
+    rest = x - high.astype(jnp.float32)
+    mid = rest.astype(jnp.bfloat16)
+    low = (rest - mid.astype(jnp.float32)).astype(jnp.bfloat16)
+    return high, mid, low
+
+
+def bf16_dot(left, right, left_dim, right_dim):
+    return lax.dot_general(
+        left, right, (((left_dim,), (right_dim,)), ((), ())), preferred_element_type=jnp.float32
+    )
+
+
+def fold(x, size, axis):
+    parts = [lax.slice_in_dim(x, n * size, (n + 1) * size, axis=axis) for n in range(3)]
+    return (parts[2] + parts[1]) + parts[0]
 
 
 def correct_kernel(g_hbm, f_hbm, q_hbm, p_ref, g_buf, f_buf, q_buf, sems):
@@ -39,10 +59,14 @@
     for s in range(IN_PARTS):
         for copy in copies[s]:
             copy.wait()
-        cols = slice(s * width, (s + 1) * width)
-        local = g_buf[:, cols] + f_buf[:, cols]
-        part = dot(q_buf[:, cols], local, 1, 1)
-        total = part if total is None else total + part
+        for at in range(s * width, (s + 1) * width, IN_TILE):
+            cols = slice(at, at + IN_TILE)
+            local = g_buf[:, cols] + f_buf[:, cols]
+            left = jnp.concatenate(split(q_buf[:, cols]), axis=0)
+            right = jnp.concatenate(split(local), axis=0)
+            part = bf16_dot(left, right, 1, 1)
+            total = part if total is None else total + part
+    total = fold(fold(total, total.shape[0] // 3, 0), total.shape[1] // 3, 1)
     half = total.shape[0] // 2
     packed = jnp.concatenate([total[:half], total[half:]], axis=1)
     p_ref[...] = jnp.broadcast_to(packed[None], p_ref.shape)
@@ -62,11 +86,17 @@
     length = msg_ref.shape[0] // peers
     width = c_ref.shape[1] // GROUPS
     tiles = width // LANES
+    high, mid, low = split(mean)
+    none = jnp.zeros_like(high)
+    left = jnp.concatenate(
+        [jnp.concatenate(parts, axis=1) for parts in ((high, high, high), (mid, mid, none), (low, none, none))], axis=0
+    )
     for j in range(GROUPS):
         cols = slice(j * width, (j + 1) * width)
         local = g_ref[0, :, cols] + f_ref[0, :, cols]
         c_ref[:, cols] = local
-        out = dot(mean, local, 1, 0)
+        right = jnp.concatenate(split(local), axis=0)
+        out = fold(bf16_dot(left, right, 1, 0), rank, 0)
         for i in range(tiles):
             msg_ref[pl.ds(j * length + i, rank, stride=GROUPS * length), :] = out[:, i * LANES : (i + 1) * LANES]
     tiled = jnp.concatenate([mean] * (LANES // rank), axis=0)
@@ -119,24 +149,31 @@
     return right * (1.0 / jnp.sqrt(pivots))
 
 
-def finish_kernel(replicas, gram_ref, all_ref, mean_ref, c_ref, nf_hbm, po_ref, qf_hbm, nf_buf, qf_buf, sems):
+def finish_kernel(
+    replicas, gram_ref, all_ref, mean_ref, c_ref, nf_hbm, po_hbm, qf_hbm, nf_buf, po_buf, qf_buf, sems, po_sem
+):
     rank = mean_ref.shape[0]
     whole = inverse_factor(gram_ref[...], replicas)
     lower = whole[:, :rank]
-    left = dot(lower, mean_ref[...], 1, 0)
-    po_ref[...] = left
+    ortho = dot(lower, mean_ref[...], 1, 0)
+    po_buf[...] = ortho
+    copies = [pltpu.make_async_copy(po_buf, po_hbm, po_sem)]
+    copies[0].start()
     scaled = lower * (1.0 / replicas)
+    both = jnp.concatenate([scaled, dot(ortho, scaled, 0, 0)], axis=0)
+    high, mid, low = split(both)
+    left = jnp.concatenate([high, high, mid, high, low, mid], axis=1)
     width = c_ref.shape[1] // GROUPS
     tiles = width // LANES
-    copies = []
     for j in range(GROUPS):
         raw = jnp.concatenate(
             [all_ref[pl.ds(j * tiles + i, rank, stride=GROUPS * tiles), :] for i in range(tiles)], axis=1
         )
-        factor = dot(scaled, raw, 1, 0)
+        high, mid, low = split(raw)
+        out = bf16_dot(left, jnp.concatenate([high, mid, high, low, high, mid], axis=0), 1, 0)
         cols = slice(j * width, (j + 1) * width)
-        qf_buf[:, cols] = factor
-        nf_buf[:, cols] = c_ref[:, cols] - dot(left, factor, 0, 0)
+        qf_buf[:, cols] = out[:rank]
+        nf_buf[:, cols] = c_ref[:, cols] - out[rank:]
         at = pl.ds(j * width, width)
         part = [
             pltpu.make_async_copy(nf_buf.at[:, at], nf_hbm.at[0, :, at], sems.at[0, j]),
@@ -171,7 +208,7 @@
             pltpu.VMEM((rank, width), f32),
             pltpu.SemaphoreType.DMA((3, IN_PARTS)),
         ],
-        compiler_params=pltpu.CompilerParams(vmem_limit_bytes=60 * 2**20),
+        compiler_params=pltpu.CompilerParams(vmem_limit_bytes=int(53.75 * 2**20)),
         name="correct",
     )(gradient, feedback, q_previous)
     p_all = lax.all_to_all(p_out, "dp", 0, 0, tiled=True)
@@ -209,7 +246,7 @@
     new_feedback, p_ortho, q_factor = pl.pallas_call(
         functools.partial(finish_kernel, dp),
         in_specs=[vmem] * 4,
-        out_specs=[hbm, vmem, hbm],
+        out_specs=[hbm] * 3,
         out_shape=[
             jax.ShapeDtypeStruct((1, rows, width), f32),
             jax.ShapeDtypeStruct((rank, rows), f32),
@@ -217,8 +254,10 @@
         ],
         scratch_shapes=[
             pltpu.VMEM((rows, width), f32),
+            pltpu.VMEM((rank, rows), f32),
             pltpu.VMEM((rank, width), f32),
             pltpu.SemaphoreType.DMA((2, GROUPS)),
+            pltpu.SemaphoreType.DMA,
         ],
         compiler_params=params,
         name="finish",

time: 58.4 us -> 54.2 us (0.928)
  Pallas kernels: 9.61 us -> 5.72 us
    pallas_call x1, Pallas kernels: 4.33 us -> 2.2 us  [body(): pl.pallas_call(functools.partial(finish_kernel, dp), in_specs=[vmem] * 4,...]
    pallas_call x1, Pallas kernels: 4.26 us -> 2.71 us  [body(): pl.pallas_call(correct_kernel, in_specs=[hbm, hbm, hbm], out_specs=vmem,...]
where the time goes in v3:
time: 54.2 us; the launch traced here: 54 us
  blocking collectives  47.6 us (88%)
  Pallas kernels  5.72 us (11%)
  between operations  0.67 us (1%)
    all_to_all x1, blocking collectives, body(): terms = lax.all_to_all(msg, ('dp', 'mp'), 0, 0, tiled=True)  21.4 us
    all_to_all x1, blocking collectives, body(): whole = lax.all_to_all(own, ('dp', 'mp'), 0, 0, tiled=True)  15.9 us
    all_to_all x1, blocking collectives, body(): p_all = lax.all_to_all(p_out, 'dp', 0, 0, tiled=True)  10.3 us
    pallas_call x1, Pallas kernels, body(): pl.pallas_call(correct_kernel, in_specs=[hbm, hbm, hbm], out_specs=vmem,...  2.71 us
    pallas_call x1, Pallas kernels, body(): pl.pallas_call(functools.partial(finish_kernel, dp), in_specs=[vmem] * 4,...  2.2 us

profile of v3, /device:TPU:1, one launch (start us, length us, event | category | flops | bytes accessed | tf_op | source)
XLA Modules:
  0.0 54.0 jit_solution(380824913032026906)
XLA Ops:
  0.6 0.0 copy-start.1
  0.6 0.0 copy-start
  0.7 2.7 %correct.1 = f32[8,8,128]{2,1,0:T(8,128)S(1)} custom-call(f32[1,64,5120]{2,1,0:T(8,128)} %g_ref.1, f32[1,64,5120]{2,1,0:T(8,128)} %f_ref.1, f32[16,5120]{1,0:T(8,128)} %q_hbm.1), custom_call_target="tpu_custom_call" | custom-call | tf_op jit(solution)/shard_map/correct/pallas_call | solution.py:200
  3.4 10.3 %all_to_all.15.p_ref = f32[8,8,128]{2,1,0:T(8,128)S(1)} all-to-all(f32[8,8,128]{2,1,0:T(8,128)S(1)} %correct.1), channel_id=1, replica_groups=mesh['dp'=8,'mp'=16] {'dp'}, dimensions={0} | all-to-all | bytes 65536 | tf_op jit(solution)/shard_map/all_to_all | solution.py:214
  13.7 0.0 copy-done.1
  13.7 0.0 copy-done
  13.7 0.7 %project.1 = (f32[768,128]{1,0:T(8,128)S(1)}, f32[16,64]{1,0:T(8,128)S(1)}, f32[64,5120]{1,0:T(8,128)S(1)}) custom-call(f32[8,8,128]{2,1,0:T(8,128)S(1)} %all_to_all.15.p_ref, f32[1,64,5120]{2,1,0:T(8,128)S(1)} %copy-done, f32[1,64,5120]{2,1,0:T(8,128)S(1)} %copy-done.1), custom_call_target="tpu_custom_call" | custom-call | tf_op jit(solution)/shard_map/project/pallas_call | solution.py:216
  14.4 21.4 %all_to_all.16 = f32[128,1,768]{2,1,0:T(1,128)S(1)} all-to-all(f32[128,1,768]{2,1,0:T(1,128)S(1)} %bitcast.6), channel_id=1, replica_groups=mesh['dp'=8,'mp'=16] {'dp','mp'}, dimensions={0} | all-to-all | bytes 786432 | tf_op jit(solution)/shard_map/all_to_all | solution.py:229
  35.9 0.1 sum_terms.1
  36.0 15.9 %all_to_all.17 = f32[128,1,640]{2,1,0:T(1,128)S(1)} all-to-all(f32[128,1,640]{2,1,0:T(1,128)S(1)} %bitcast.7), channel_id=1, replica_groups=mesh['dp'=8,'mp'=16] {'dp','mp'}, dimensions={0} | all-to-all | bytes 655360 | tf_op jit(solution)/shard_map/all_to_all | solution.py:244
  51.9 2.2 %finish.1 = (f32[1,64,5120]{2,1,0:T(8,128)}, f32[16,64]{1,0:T(8,128)}, f32[16,5120]{1,0:T(8,128)}) custom-call(f32[16,128]{1,0:T(8,128)S(1)} %get-tuple-element.9.gram_ref, f32[640,128]{1,0:T(8,128)S(1)} %bitcast.5, f32[16,64]{1,0:T(8,128)S(1)} %get-tuple-element.11.mean_ref, f32[64,5120]{1,0:T(8,128)S(1)} %get-tuple-element.12.c_ref), custom_call_target="tpu_custom_call" | custom-call | tf_op jit(solution)/shard_map/finish/pallas_call | solution.py:246
Async XLA Ops:
  0.6 13.1 %copy-start.1 = (f32[1,64,5120]{2,1,0:T(8,128)S(1)}, f32[1,64,5120]{2,1,0:T(8,128)}, u32[]{:S(2)}) copy-start(f32[1,64,5120]{2,1,0:T(8,128)} %f_ref.1) | copy-start | bytes 3932164
  0.6 13.0 %copy-start = (f32[1,64,5120]{2,1,0:T(8,128)S(1)}, f32[1,64,5120]{2,1,0:T(8,128)}, u32[]{:S(2)}) copy-start(f32[1,64,5120]{2,1,0:T(8,128)} %g_ref.1) | copy-start | bytes 3932164

commit v4 on v3

--- a/solution.py
+++ b/solution.py
@@ -1,4 +1,5 @@
 import functools
+import math
 
 import jax
 import jax.numpy as jnp
@@ -11,6 +12,9 @@
 IN_PARTS = 5
 IN_TILE = 512
 GROUPS = 8
+CORES = 2
+DP = ("x", "core")
+MP = ("z", "y")
 
 
 def dot(left, right, left_dim, right_dim):
@@ -72,6 +76,10 @@
     p_ref[...] = jnp.broadcast_to(packed[None], p_ref.shape)
 
 
+def owner_of(group):
+    return group % (GROUPS // CORES) * CORES + group // (GROUPS // CORES)
+
+
 def project_kernel(p_ref, g_ref, f_ref, msg_ref, mean_ref, c_ref):
     replicas = p_ref.shape[0]
     total = p_ref[0]
@@ -98,13 +106,14 @@
         right = jnp.concatenate(split(local), axis=0)
         out = fold(bf16_dot(left, right, 1, 0), rank, 0)
         for i in range(tiles):
-            msg_ref[pl.ds(j * length + i, rank, stride=GROUPS * length), :] = out[:, i * LANES : (i + 1) * LANES]
+            first = owner_of(j) * rank * length + i
+            msg_ref[pl.ds(first, rank, stride=length), :] = out[:, i * LANES : (i + 1) * LANES]
     tiled = jnp.concatenate([mean] * (LANES // rank), axis=0)
     gram = dot(mean, tiled, 1, 1)
     share = rank // replicas
     row = lax.broadcasted_iota(jnp.int32, (rank, LANES), 0)
     lane = lax.broadcasted_iota(jnp.int32, (rank, LANES), 1)
-    mine = row - share * lax.axis_index("dp")
+    mine = row - share * lax.axis_index(DP)
     kept = (lane >= rank * mine) & (lane < rank * (mine + 1)) & (mine >= 0) & (mine < share)
     line = jnp.sum(jnp.where(kept, gram, 0.0), axis=0, keepdims=True)
     msg_ref[pl.ds(tiles, peers, stride=length), :] = jnp.broadcast_to(line, (peers, LANES))
@@ -118,7 +127,8 @@
     part[...] = total
     for i in range(5):
         line = jnp.sum(part[pl.ds(i, 4, stride=6), :], axis=0, keepdims=True)
-        out_ref[pl.ds(i, peers, stride=5), :] = jnp.broadcast_to(line, (peers, LANES))
+        copies = out_ref.shape[0] // 5
+        out_ref[pl.ds(i, copies, stride=5), :] = jnp.broadcast_to(line, (copies, LANES))
     shards = peers // replicas
     for n in range(replicas):
         terms = in_ref[pl.ds(n * shards * 6 + 5, shards, stride=6), :]
@@ -149,35 +159,60 @@
     return right * (1.0 / jnp.sqrt(pivots))
 
 
-def finish_kernel(
-    replicas, gram_ref, all_ref, mean_ref, c_ref, nf_hbm, po_hbm, qf_hbm, nf_buf, po_buf, qf_buf, sems, po_sem
-):
+def half_block(left, half_ref, c_ref, core, n, rank):
+    groups = GROUPS // CORES
+    width = c_ref.shape[1] // GROUPS
+    tiles = width // LANES
+    raw = jnp.concatenate(
+        [half_ref[pl.ds(n * rank * tiles + i, rank, stride=tiles), :] for i in range(tiles)], axis=1
+    )
+    high, mid, low = split(raw)
+    out = bf16_dot(left, jnp.concatenate([high, mid, high, low, high, mid], axis=0), 1, 0)
+    at = pl.multiple_of((core * groups + n) * width, width)
+    return out[:rank], c_ref[:, pl.ds(at, width)] - out[rank:]
+
+
+def own_half_kernel(replicas, gram_ref, half_ref, mean_ref, c_ref, left_ref, po_ref, qf_ref, nf_ref):
     rank = mean_ref.shape[0]
     whole = inverse_factor(gram_ref[...], replicas)
     lower = whole[:, :rank]
     ortho = dot(lower, mean_ref[...], 1, 0)
-    po_buf[...] = ortho
-    copies = [pltpu.make_async_copy(po_buf, po_hbm, po_sem)]
-    copies[0].start()
+    po_ref[...] = ortho
     scaled = lower * (1.0 / replicas)
     both = jnp.concatenate([scaled, dot(ortho, scaled, 0, 0)], axis=0)
     high, mid, low = split(both)
     left = jnp.concatenate([high, high, mid, high, low, mid], axis=1)
+    left_ref[...] = left
     width = c_ref.shape[1] // GROUPS
-    tiles = width // LANES
-    for j in range(GROUPS):
-        raw = jnp.concatenate(
-            [all_ref[pl.ds(j * tiles + i, rank, stride=GROUPS * tiles), :] for i in range(tiles)], axis=1
-        )
-        high, mid, low = split(raw)
-        out = bf16_dot(left, jnp.concatenate([high, mid, high, low, high, mid], axis=0), 1, 0)
-        cols = slice(j * width, (j + 1) * width)
-        qf_buf[:, cols] = out[:rank]
-        nf_buf[:, cols] = c_ref[:, cols] - out[rank:]
-        at = pl.ds(j * width, width)
+    for n in range(GROUPS // CORES):
+        cols = slice(n * width, (n + 1) * width)
+        qf_ref[:, cols], nf_ref[:, cols] = half_block(left, half_ref, c_ref, lax.axis_index("core"), n, rank)
+
+
+def finish_kernel(
+    left_ref, po_ref, qf_ref, nf_ref, half_ref, c_ref, nf_hbm, po_hbm, qf_hbm, nf_buf, qf_buf, sems, half_sems
+):
+    rank = po_ref.shape[0]
+    core = lax.axis_index("core")
+    width = c_ref.shape[1] // GROUPS
+    groups = GROUPS // CORES
+    own = pl.ds(pl.multiple_of(core * groups * width, width), groups * width)
+    copies = [
+        pltpu.make_async_copy(nf_ref, nf_hbm.at[0, :, own], half_sems.at[0]),
+        pltpu.make_async_copy(qf_ref, qf_hbm.at[:, own], half_sems.at[1]),
+        pltpu.make_async_copy(po_ref, po_hbm, half_sems.at[2]),
+    ]
+    for copy in copies:
+        copy.start()
+    left = left_ref[...]
+    for n in range(groups):
+        cols = slice(n * width, (n + 1) * width)
+        qf_buf[:, cols], nf_buf[:, cols] = half_block(left, half_ref, c_ref, 1 - core, n, rank)
+        here = pl.ds(n * width, width)
+        there = pl.ds(pl.multiple_of(((1 - core) * groups + n) * width, width), width)
         part = [
-            pltpu.make_async_copy(nf_buf.at[:, at], nf_hbm.at[0, :, at], sems.at[0, j]),
-            pltpu.make_async_copy(qf_buf.at[:, at], qf_hbm.at[:, at], sems.at[1, j]),
+            pltpu.make_async_copy(nf_buf.at[:, here], nf_hbm.at[0, :, there], sems.at[0, n]),
+            pltpu.make_async_copy(qf_buf.at[:, here], qf_hbm.at[:, there], sems.at[1, n]),
         ]
         for copy in part:
             copy.start()
@@ -188,7 +223,7 @@
 
 def body(gradient, feedback, q_previous):
     f32 = jnp.float32
-    dp, mp = lax.axis_size("dp"), lax.axis_size("mp")
+    dp, mp = lax.axis_size(DP), lax.axis_size(MP)
     _, rows, width = gradient.shape
     rank = q_previous.shape[0]
     peers = dp * mp
@@ -211,7 +246,7 @@
         compiler_params=pltpu.CompilerParams(vmem_limit_bytes=int(53.75 * 2**20)),
         name="correct",
     )(gradient, feedback, q_previous)
-    p_all = lax.all_to_all(p_out, "dp", 0, 0, tiled=True)
+    p_all = lax.all_to_all(p_out, DP, 0, 0, tiled=True)
 
     msg, p_mean, local = pl.pallas_call(
         project_kernel,
@@ -226,26 +261,41 @@
         name="project",
     )(p_all, gradient, feedback)
     msg = msg.reshape(peers, 1, (tiles + 1) * LANES)
-    terms = lax.all_to_all(msg, ("dp", "mp"), 0, 0, tiled=True)
+    terms = lax.all_to_all(msg, DP + MP, 0, 0, tiled=True)
 
     own, gram = pl.pallas_call(
         functools.partial(sum_kernel, dp),
         in_specs=[vmem],
         out_specs=[vmem, vmem],
         out_shape=[
-            jax.ShapeDtypeStruct((peers * tiles, LANES), f32),
+            jax.ShapeDtypeStruct((peers // CORES * tiles, LANES), f32),
             jax.ShapeDtypeStruct((rank, LANES), f32),
         ],
         scratch_shapes=[pltpu.VMEM((24, LANES), f32)],
         compiler_params=params,
         name="sum_terms",
     )(terms.reshape(peers * (tiles + 1), LANES))
-    own = own.reshape(peers, 1, tiles * LANES)
-    whole = lax.all_to_all(own, ("dp", "mp"), 0, 0, tiled=True)
-
+    own = own.reshape(peers // CORES, 1, tiles * LANES)
+    half = lax.all_to_all(own, ("x",) + MP, 0, 0, tiled=True).reshape(peers // CORES * tiles, LANES)
+    other = lax.ppermute(half, "core", [(0, 1), (1, 0)])
+
+    left, p_ortho, q_half, f_half = pl.pallas_call(
+        functools.partial(own_half_kernel, dp),
+        in_specs=[vmem] * 4,
+        out_specs=[vmem] * 4,
+        out_shape=[
+            jax.ShapeDtypeStruct((rank + rows, 6 * rank), jnp.bfloat16),
+            jax.ShapeDtypeStruct((rank, rows), f32),
+            jax.ShapeDtypeStruct((rank, width // CORES), f32),
+            jax.ShapeDtypeStruct((rows, width // CORES), f32),
+        ],
+        compiler_params=params,
+        cost_estimate=pl.CostEstimate(flops=2 * rows * width * 96, bytes_accessed=8 * rows * width, transcendentals=0),
+        name="own_half",
+    )(gram, half, p_mean, local)
     new_feedback, p_ortho, q_factor = pl.pallas_call(
-        functools.partial(finish_kernel, dp),
-        in_specs=[vmem] * 4,
+        finish_kernel,
+        in_specs=[vmem] * 6,
         out_specs=[hbm] * 3,
         out_shape=[
             jax.ShapeDtypeStruct((1, rows, width), f32),
@@ -253,23 +303,24 @@
             jax.ShapeDtypeStruct((rank, width), f32),
         ],
         scratch_shapes=[
-            pltpu.VMEM((rows, width), f32),
-            pltpu.VMEM((rank, rows), f32),
-            pltpu.VMEM((rank, width), f32),
-            pltpu.SemaphoreType.DMA((2, GROUPS)),
-            pltpu.SemaphoreType.DMA,
+            pltpu.VMEM((rows, width // CORES), f32),
+            pltpu.VMEM((rank, width // CORES), f32),
+            pltpu.SemaphoreType.DMA((2, GROUPS // CORES)),
+            pltpu.SemaphoreType.DMA((3,)),
         ],
         compiler_params=params,
         name="finish",
-    )(gram, whole.reshape(peers * tiles, LANES), p_mean, local)
+    )(left, p_ortho, q_half, f_half, other, local)
     return (new_feedback, p_ortho, q_factor)
 
 
 def solution(mesh):
+    sizes = (mesh.shape["dp"] // CORES, CORES, math.isqrt(mesh.shape["mp"]), math.isqrt(mesh.shape["mp"]))
+    fine = jax.sharding.Mesh(mesh.devices.reshape(sizes), DP + MP)
     return jax.shard_map(
         body,
-        mesh=mesh,
-        in_specs=(P("dp", "mp", None), P("dp", "mp", None), P()),
-        out_specs=(P("dp", "mp", None), P(None, "mp"), P()),
+        mesh=fine,
+        in_specs=(P(DP, MP, None), P(DP, MP, None), P()),
+        out_specs=(P(DP, MP, None), P(None, MP), P()),
         check_vma=False,
     )

time: 54.2 us -> 53.5 us (0.987)
  blocking collectives: 47.6 us -> 44.6 us
  starting transfers between devices: 0 us -> 2.29 us
    all_to_all x3, blocking collectives: 47.6 us -> 44.6 us  [the longest x1 21.4 us: body(): terms = lax.all_to_all(msg, DP + MP, 0, 0, tiled=True)]
    ppermute x0 -> x1, starting transfers between devices: none -> 2.29 us  [body(): other = lax.ppermute(half, 'core', [(0, 1), (1, 0)])]
    pallas_call x1 -> x2, Pallas kernels: 2.2 us -> 2.25 us  [the longest x1 1.25 us: body(): pl.pallas_call(finish_kernel, in_specs=[vmem] * 6, out_specs=[hbm] * 3, o...]
  transfers between devices with their start and end apart: 0 -> 1, of which waited for: 0 -> 0; matrix products, arithmetic and copies ran while one was open for 0% -> 0% of each run, Pallas kernels for 0% -> 2%
where the time goes in v4:
time: 53.5 us; the launch traced here: 53.3 us
  blocking collectives  44.6 us (83%)
  Pallas kernels  5.74 us (11%)
  starting transfers between devices  2.29 us (4%)
  between operations  0.67 us (1%)
    all_to_all x1, blocking collectives, body(): terms = lax.all_to_all(msg, DP + MP, 0, 0, tiled=True)  21.4 us
    all_to_all x1, blocking collectives, body(): lax.all_to_all(own, ('x',) + MP, 0, 0, tiled=True)  12.8 us
    all_to_all x1, blocking collectives, body(): p_all = lax.all_to_all(p_out, DP, 0, 0, tiled=True)  10.3 us
    pallas_call x1, Pallas kernels, body(): pl.pallas_call(correct_kernel, in_specs=[hbm, hbm, hbm], out_specs=vmem,...  2.71 us
    ppermute x1, starting transfers between devices, body(): other = lax.ppermute(half, 'core', [(0, 1), (1, 0)])  2.29 us
    pallas_call x1, Pallas kernels, body(): pl.pallas_call(finish_kernel, in_specs=[vmem] * 6, out_specs=[hbm] * 3, o...  1.25 us
  transfers between devices with their start and end apart: 1, of which 0 were waited for; matrix products, arithmetic and copies ran while one was open for 0% of the time, Pallas kernels for 2%

profile of v4, /device:TPU:1, one launch (start us, length us, event | category | flops | bytes accessed | tf_op | source)
XLA Modules:
  0.0 53.3 jit_solution(7551376500369610001)
XLA Ops:
  0.6 0.0 copy-start.1
  0.6 0.0 copy-start
  0.7 2.7 %correct.1 = f32[8,8,128]{2,1,0:T(8,128)S(1)} custom-call(f32[1,64,5120]{2,1,0:T(8,128)} %g_ref.1, f32[1,64,5120]{2,1,0:T(8,128)} %f_ref.1, f32[16,5120]{1,0:T(8,128)} %q_hbm.1), custom_call_target="tpu_custom_call" | custom-call | tf_op jit(solution)/shard_map/correct/pallas_call | solution.py:235
  3.4 10.3 %all_to_all.15.p_ref = f32[8,8,128]{2,1,0:T(8,128)S(1)} all-to-all(f32[8,8,128]{2,1,0:T(8,128)S(1)} %correct.1), channel_id=1, replica_groups=mesh['x'=4,'core'=2,'z'=4,'y'=4] {'x','core'}, dimensions={0} | all-to-all | bytes 65536 | tf_op jit(solution)/shard_map/all_to_all | solution.py:249
  13.7 0.0 copy-done.1
  13.7 0.0 copy-done
  13.7 0.7 %project.1 = (f32[768,128]{1,0:T(8,128)S(1)}, f32[16,64]{1,0:T(8,128)S(1)}, f32[64,5120]{1,0:T(8,128)S(1)}) custom-call(f32[8,8,128]{2,1,0:T(8,128)S(1)} %all_to_all.15.p_ref, f32[1,64,5120]{2,1,0:T(8,128)S(1)} %copy-done, f32[1,64,5120]{2,1,0:T(8,128)S(1)} %copy-done.1), custom_call_target="tpu_custom_call" | custom-call | tf_op jit(solution)/shard_map/project/pallas_call | solution.py:251
  14.4 21.4 %all_to_all.16 = f32[128,1,768]{2,1,0:T(1,128)S(1)} all-to-all(f32[128,1,768]{2,1,0:T(1,128)S(1)} %bitcast.7), channel_id=1, replica_groups=mesh['x'=4,'core'=2,'z'=4,'y'=4] {'x','core','z','y'}, dimensions={0} | all-to-all | bytes 786432 | tf_op jit(solution)/shard_map/all_to_all | solution.py:264
  35.9 0.1 sum_terms.1
  35.9 12.8 %all_to_all.17 = f32[64,1,640]{2,1,0:T(1,128)S(1)} all-to-all(f32[64,1,640]{2,1,0:T(1,128)S(1)} %bitcast.8), channel_id=1, replica_groups=mesh['x'=4,'core'=2,'z'=4,'y'=4] {'x','z','y'}, dimensions={0} | all-to-all | bytes 327680 | tf_op jit(solution)/shard_map/all_to_all | solution.py:279
  48.8 2.3 %collective-permute-start = (f32[320,128]{1,0:T(8,128)S(1)}, f32[320,128]{1,0:T(8,128)S(1)}, u32[]{:S(2)}, u32[]{:S(2)}) collective-permute-start(f32[320,128]{1,0:T(8,128)S(1)} %bitcast.5), channel_id=1, source_target_pairs={{0,16},{16,0},{1,17},{17,1},{2,18},{18,2},{3,19},{19,3},{4,20},{20... | collective-permute-start | bytes 491528 | tf_op jit(solution)/shard_map/ppermute | solution.py:280
  51.1 1.0 %own_half.1 = (bf16[80,96]{1,0:T(8,128)(2,1)S(1)}, f32[16,64]{1,0:T(8,128)S(1)}, f32[16,2560]{1,0:T(8,128)S(1)}, f32[64,2560]{1,0:T(8,128)S(1)}) custom-call(f32[16,128]{1,0:T(8,128)S(1)} %get-tuple-element.13.gram_ref, f32[320,128]{1,0:T(8,128)S(1)} %bitcast.6, f32[16,64]{1,0:T(8,128)S(1)} %get-tuple-element.15.mean_ref, f32[64,5120]{1,0:T(8,128)S(1)} %get-tuple-element.16.c_ref), custom_call_target="tpu_custom_call" | custom-call | flops 62914560 | bytes 2621440 | tf_op jit(solution)/shard_map/own_half/pallas_call | solution.py:282
  52.1 0.0 collective-permute-done.half_ref
  52.1 1.3 %finish.1 = (f32[1,64,5120]{2,1,0:T(8,128)}, f32[16,64]{1,0:T(8,128)}, f32[16,5120]{1,0:T(8,128)}) custom-call(bf16[80,96]{1,0:T(8,128)(2,1)S(1)} %get-tuple-element.17.left_ref, f32[16,64]{1,0:T(8,128)S(1)} %get-tuple-element.18.po_ref, f32[16,2560]{1,0:T(8,128)S(1)} %get-tuple-element.19.qf_ref, f32[64,2560]{1,0:T(8,128)S(1)} %get-tuple-element.20.nf_ref, ...), custom_call_target="tpu_custom_call" | custom-call | tf_op jit(solution)/shard_map/finish/pallas_call | solution.py:296
Async XLA Ops:
  0.6 13.1 %copy-start.1 = (f32[1,64,5120]{2,1,0:T(8,128)S(1)}, f32[1,64,5120]{2,1,0:T(8,128)}, u32[]{:S(2)}) copy-start(f32[1,64,5120]{2,1,0:T(8,128)} %f_ref.1) | copy-start | bytes 3932164
  0.6 13.0 %copy-start = (f32[1,64,5120]{2,1,0:T(8,128)S(1)}, f32[1,64,5120]{2,1,0:T(8,128)}, u32[]{:S(2)}) copy-start(f32[1,64,5120]{2,1,0:T(8,128)} %g_ref.1) | copy-start | bytes 3932164
  48.8 3.3 %collective-permute-start = (f32[320,128]{1,0:T(8,128)S(1)}, f32[320,128]{1,0:T(8,128)S(1)}, u32[]{:S(2)}, u32[]{:S(2)}) collective-permute-start(f32[320,128]{1,0:T(8,128)S(1)} %bitcast.5), channel_id=1, source_target_pairs={{0,16},{16,0},{1,17},{17,1},{2,18},{18,2},{3,19},{19,3},{4,20},{20... | collective-permute-start | bytes 491528 | tf_op jit(solution)/shard_map/ppermute | solution.py:280

commit v5 on v4

--- a/solution.py
+++ b/solution.py
@@ -11,8 +11,8 @@
 LANES = 128
 IN_PARTS = 5
 IN_TILE = 512
-GROUPS = 8
 CORES = 2
+HALF_GROUPS = 4
 DP = ("x", "core")
 MP = ("z", "y")
 
@@ -76,11 +76,52 @@
     p_ref[...] = jnp.broadcast_to(packed[None], p_ref.shape)
 
 
-def owner_of(group):
-    return group % (GROUPS // CORES) * CORES + group // (GROUPS // CORES)
-
-
-def project_kernel(p_ref, g_ref, f_ref, msg_ref, mean_ref, c_ref):
+def member_of(place):
+    return (6 - place) % 4
+
+
+def chip_groups(sizes):
+    nx, nc, nz, ny = sizes
+    return [
+        [
+            ((member_of(i) * nc + core) * nz + member_of(j)) * ny + member_of(k)
+            for i in range(nx)
+            for j in range(nz)
+            for k in range(ny)
+        ]
+        for core in range(nc)
+    ]
+
+
+def column_at(core, n, width):
+    return pl.multiple_of((core * HALF_GROUPS + n) * width, width)
+
+
+def write_half(mean, core, g_ref, f_ref, msg_ref, c_ref):
+    rank = mean.shape[0]
+    width = c_ref.shape[1] // HALF_GROUPS
+    tiles = width // LANES
+    high, mid, low = split(mean)
+    none = jnp.zeros_like(high)
+    left = jnp.concatenate(
+        [jnp.concatenate(parts, axis=1) for parts in ((high, high, high), (mid, mid, none), (low, none, none))], axis=0
+    )
+    for n in range(HALF_GROUPS):
+        cols = pl.ds(column_at(core, n, width), width)
+        local = g_ref[0, :, cols] + f_ref[0, :, cols]
+        c_ref[:, n * width : (n + 1) * width] = local
+        out = fold(bf16_dot(left, jnp.concatenate(split(local), axis=0), 1, 0), rank, 0)
+        for i in range(tiles):
+            first = n * rank * (tiles + 1) + i
+            msg_ref[pl.ds(first, rank, stride=tiles + 1), :] = out[:, i * LANES : (i + 1) * LANES]
+
+
+def write_last(msg_ref, line):
+    count = msg_ref.shape[0] // 6
+    msg_ref[pl.ds(5, count, stride=6), :] = jnp.broadcast_to(line, (count, LANES))
+
+
+def other_kernel(p_ref, g_ref, f_ref, msg_ref, mean_ref, c_ref):
     replicas = p_ref.shape[0]
     total = p_ref[0]
     for n in range(1, replicas):
@@ -89,37 +130,24 @@
     half = total.shape[1] // 2
     mean = jnp.concatenate([total[:, :half], total[:, half:]], axis=0)
     mean_ref[...] = mean
+    write_half(mean, 1 - lax.axis_index("core"), g_ref, f_ref, msg_ref, c_ref)
+    write_last(msg_ref, jnp.zeros((1, LANES), jnp.float32))
+
+
+def own_kernel(mean_ref, g_ref, f_ref, msg_ref, c_ref):
+    mean = mean_ref[...]
     rank = mean.shape[0]
-    peers = rank * GROUPS
-    length = msg_ref.shape[0] // peers
-    width = c_ref.shape[1] // GROUPS
-    tiles = width // LANES
-    high, mid, low = split(mean)
-    none = jnp.zeros_like(high)
-    left = jnp.concatenate(
-        [jnp.concatenate(parts, axis=1) for parts in ((high, high, high), (mid, mid, none), (low, none, none))], axis=0
-    )
-    for j in range(GROUPS):
-        cols = slice(j * width, (j + 1) * width)
-        local = g_ref[0, :, cols] + f_ref[0, :, cols]
-        c_ref[:, cols] = local
-        right = jnp.concatenate(split(local), axis=0)
-        out = fold(bf16_dot(left, right, 1, 0), rank, 0)
-        for i in range(tiles):
-            first = owner_of(j) * rank * length + i
-            msg_ref[pl.ds(first, rank, stride=length), :] = out[:, i * LANES : (i + 1) * LANES]
-    tiled = jnp.concatenate([mean] * (LANES // rank), axis=0)
-    gram = dot(mean, tiled, 1, 1)
-    share = rank // replicas
+    write_half(mean, lax.axis_index("core"), g_ref, f_ref, msg_ref, c_ref)
+    gram = dot(mean, jnp.concatenate([mean] * (LANES // rank), axis=0), 1, 1)
+    share = rank // HALF_GROUPS
     row = lax.broadcasted_iota(jnp.int32, (rank, LANES), 0)
     lane = lax.broadcasted_iota(jnp.int32, (rank, LANES), 1)
-    mine = row - share * lax.axis_index(DP)
+    mine = row - share * member_of(lax.axis_index("x"))
     kept = (lane >= rank * mine) & (lane < rank * (mine + 1)) & (mine >= 0) & (mine < share)
-    line = jnp.sum(jnp.where(kept, gram, 0.0), axis=0, keepdims=True)
-    msg_ref[pl.ds(tiles, peers, stride=length), :] = jnp.broadcast_to(line, (peers, LANES))
-
-
-def sum_kernel(replicas, in_ref, out_ref, gram_ref, part):
+    write_last(msg_ref, jnp.sum(jnp.where(kept, gram, 0.0), axis=0, keepdims=True))
+
+
+def sum_kernel(in_ref, out_ref, gram_ref, part):
     peers = in_ref.shape[0] // 6
     total = in_ref[0:24]
     for s in range(1, peers // 4):
@@ -127,19 +155,18 @@
     part[...] = total
     for i in range(5):
         line = jnp.sum(part[pl.ds(i, 4, stride=6), :], axis=0, keepdims=True)
-        copies = out_ref.shape[0] // 5
-        out_ref[pl.ds(i, copies, stride=5), :] = jnp.broadcast_to(line, (copies, LANES))
-    shards = peers // replicas
-    for n in range(replicas):
+        out_ref[pl.ds(i, peers, stride=5), :] = jnp.broadcast_to(line, (peers, LANES))
+    shards = peers // HALF_GROUPS
+    share = gram_ref.shape[0] // HALF_GROUPS
+    for n in range(HALF_GROUPS):
         terms = in_ref[pl.ds(n * shards * 6 + 5, shards, stride=6), :]
         line = jnp.sum(terms, axis=0, keepdims=True)
-        share = gram_ref.shape[0] // replicas
         gram_ref[n * share : (n + 1) * share, :] = jnp.broadcast_to(line, (share, LANES))
 
 
-def inverse_factor(spread, replicas):
+def inverse_factor(spread):
     rank = spread.shape[0]
-    share = rank // replicas
+    share = rank // HALF_GROUPS
     row = lax.broadcasted_iota(jnp.int32, (rank, LANES), 0)
     lane = lax.broadcasted_iota(jnp.int32, (rank, LANES), 1)
     at = lane - rank * (row % share)
@@ -159,22 +186,20 @@
     return right * (1.0 / jnp.sqrt(pivots))
 
 
-def half_block(left, half_ref, c_ref, core, n, rank):
-    groups = GROUPS // CORES
-    width = c_ref.shape[1] // GROUPS
+def half_block(left, half_ref, c_ref, n, rank):
+    width = c_ref.shape[1] // HALF_GROUPS
     tiles = width // LANES
     raw = jnp.concatenate(
         [half_ref[pl.ds(n * rank * tiles + i, rank, stride=tiles), :] for i in range(tiles)], axis=1
     )
     high, mid, low = split(raw)
     out = bf16_dot(left, jnp.concatenate([high, mid, high, low, high, mid], axis=0), 1, 0)
-    at = pl.multiple_of((core * groups + n) * width, width)
-    return out[:rank], c_ref[:, pl.ds(at, width)] - out[rank:]
+    return out[:rank], c_ref[:, n * width : (n + 1) * width] - out[rank:]
 
 
 def own_half_kernel(replicas, gram_ref, half_ref, mean_ref, c_ref, left_ref, po_ref, qf_ref, nf_ref):
     rank = mean_ref.shape[0]
-    whole = inverse_factor(gram_ref[...], replicas)
+    whole = inverse_factor(gram_ref[...])
     lower = whole[:, :rank]
     ortho = dot(lower, mean_ref[...], 1, 0)
     po_ref[...] = ortho
@@ -183,10 +208,10 @@
     high, mid, low = split(both)
     left = jnp.concatenate([high, high, mid, high, low, mid], axis=1)
     left_ref[...] = left
-    width = c_ref.shape[1] // GROUPS
-    for n in range(GROUPS // CORES):
+    width = c_ref.shape[1] // HALF_GROUPS
+    for n in range(HALF_GROUPS):
         cols = slice(n * width, (n + 1) * width)
-        qf_ref[:, cols], nf_ref[:, cols] = half_block(left, half_ref, c_ref, lax.axis_index("core"), n, rank)
+        qf_ref[:, cols], nf_ref[:, cols] = half_block(left, half_ref, c_ref, n, rank)
 
 
 def finish_kernel(
@@ -194,9 +219,8 @@
 ):
     rank = po_ref.shape[0]
     core = lax.axis_index("core")
-    width = c_ref.shape[1] // GROUPS
-    groups = GROUPS // CORES
-    own = pl.ds(pl.multiple_of(core * groups * width, width), groups * width)
+    width = c_ref.shape[1] // HALF_GROUPS
+    own = pl.ds(column_at(core, 0, width), HALF_GROUPS * width)
     copies = [
         pltpu.make_async_copy(nf_ref, nf_hbm.at[0, :, own], half_sems.at[0]),
         pltpu.make_async_copy(qf_ref, qf_hbm.at[:, own], half_sems.at[1]),
@@ -205,11 +229,11 @@
     for copy in copies:
         copy.start()
     left = left_ref[...]
-    for n in range(groups):
+    for n in range(HALF_GROUPS):
         cols = slice(n * width, (n + 1) * width)
-        qf_buf[:, cols], nf_buf[:, cols] = half_block(left, half_ref, c_ref, 1 - core, n, rank)
+        qf_buf[:, cols], nf_buf[:, cols] = half_block(left, half_ref, c_ref, n, rank)
         here = pl.ds(n * width, width)
-        there = pl.ds(pl.multiple_of(((1 - core) * groups + n) * width, width), width)
+        there = pl.ds(column_at(1 - core, n, width), width)
         part = [
             pltpu.make_async_copy(nf_buf.at[:, here], nf_hbm.at[0, :, there], sems.at[0, n]),
             pltpu.make_async_copy(qf_buf.at[:, here], qf_hbm.at[:, there], sems.at[1, n]),
@@ -226,8 +250,7 @@
     dp, mp = lax.axis_size(DP), lax.axis_size(MP)
     _, rows, width = gradient.shape
     rank = q_previous.shape[0]
-    peers = dp * mp
-    tiles = width // GROUPS // LANES
+    tiles = width // CORES // HALF_GROUPS // LANES
     vmem = pl.BlockSpec(memory_space=pltpu.VMEM)
     hbm = pl.BlockSpec(memory_space=pltpu.HBM)
     params = pltpu.CompilerParams(vmem_limit_bytes=16 * 2**20)
@@ -246,37 +269,51 @@
         compiler_params=pltpu.CompilerParams(vmem_limit_bytes=int(53.75 * 2**20)),
         name="correct",
     )(gradient, feedback, q_previous)
-    p_all = lax.all_to_all(p_out, DP, 0, 0, tiled=True)
-
-    msg, p_mean, local = pl.pallas_call(
-        project_kernel,
+    sizes = tuple(lax.axis_size(name) for name in DP + MP)
+    near = [[member_of(i) * CORES + core for i in range(sizes[0]) for core in (1, 0)]]
+    chips = chip_groups(sizes)
+    p_all = lax.all_to_all(p_out, DP, 0, 0, tiled=True, axis_index_groups=near)
+
+    count = sizes[0] * mp
+    half_out = [
+        jax.ShapeDtypeStruct((count * (tiles + 1), LANES), f32),
+        jax.ShapeDtypeStruct((rows, width // CORES), f32),
+    ]
+    msg_other, p_mean, local_other = pl.pallas_call(
+        other_kernel,
         in_specs=[vmem] * 3,
         out_specs=[vmem] * 3,
-        out_shape=[
-            jax.ShapeDtypeStruct((peers * (tiles + 1), LANES), f32),
-            jax.ShapeDtypeStruct((rank, rows), f32),
-            jax.ShapeDtypeStruct((rows, width), f32),
-        ],
-        compiler_params=params,
-        name="project",
+        out_shape=[half_out[0], jax.ShapeDtypeStruct((rank, rows), f32), half_out[1]],
+        compiler_params=params,
+        name="project_other",
     )(p_all, gradient, feedback)
-    msg = msg.reshape(peers, 1, (tiles + 1) * LANES)
-    terms = lax.all_to_all(msg, DP + MP, 0, 0, tiled=True)
+    arrived = lax.ppermute(msg_other, "core", [(0, 1), (1, 0)])
+    msg_own, local_own = pl.pallas_call(
+        own_kernel,
+        in_specs=[vmem] * 3,
+        out_specs=[vmem] * 2,
+        out_shape=half_out,
+        compiler_params=params,
+        cost_estimate=pl.CostEstimate(flops=2 * rows * width * 96, bytes_accessed=8 * rows * width, transcendentals=0),
+        name="project_own",
+    )(p_mean, gradient, feedback)
+    msg = (msg_own + arrived).reshape(count, 1, (tiles + 1) * LANES)
+    terms = lax.all_to_all(msg, DP + MP, 0, 0, tiled=True, axis_index_groups=chips)
 
     own, gram = pl.pallas_call(
-        functools.partial(sum_kernel, dp),
+        sum_kernel,
         in_specs=[vmem],
         out_specs=[vmem, vmem],
         out_shape=[
-            jax.ShapeDtypeStruct((peers // CORES * tiles, LANES), f32),
+            jax.ShapeDtypeStruct((count * tiles, LANES), f32),
             jax.ShapeDtypeStruct((rank, LANES), f32),
         ],
         scratch_shapes=[pltpu.VMEM((24, LANES), f32)],
         compiler_params=params,
         name="sum_terms",
-    )(terms.reshape(peers * (tiles + 1), LANES))
-    own = own.reshape(peers // CORES, 1, tiles * LANES)
-    half = lax.all_to_all(own, ("x",) + MP, 0, 0, tiled=True).reshape(peers // CORES * tiles, LANES)
+    )(terms.reshape(count * (tiles + 1), LANES))
+    own = own.reshape(count, 1, tiles * LANES)
+    half = lax.all_to_all(own, DP + MP, 0, 0, tiled=True, axis_index_groups=chips).reshape(count * tiles, LANES)
     other = lax.ppermute(half, "core", [(0, 1), (1, 0)])
 
     left, p_ortho, q_half, f_half = pl.pallas_call(
@@ -292,7 +329,7 @@
         compiler_params=params,
         cost_estimate=pl.CostEstimate(flops=2 * rows * width * 96, bytes_accessed=8 * rows * width, transcendentals=0),
         name="own_half",
-    )(gram, half, p_mean, local)
+    )(gram, half, p_mean, local_own)
     new_feedback, p_ortho, q_factor = pl.pallas_call(
         finish_kernel,
         in_specs=[vmem] * 6,
@@ -305,12 +342,12 @@
         scratch_shapes=[
             pltpu.VMEM((rows, width // CORES), f32),
             pltpu.VMEM((rank, width // CORES), f32),
-            pltpu.SemaphoreType.DMA((2, GROUPS // CORES)),
+            pltpu.SemaphoreType.DMA((2, HALF_GROUPS)),
             pltpu.SemaphoreType.DMA((3,)),
         ],
         compiler_params=params,
         name="finish",
-    )(left, p_ortho, q_half, f_half, other, local)
+    )(left, p_ortho, q_half, f_half, other, local_other)
     return (new_feedback, p_ortho, q_factor)
 
 

time: 53.5 us -> 47.5 us (0.89)
  blocking collectives: 44.6 us -> 37 us
  starting transfers between devices: 2.29 us -> 2.96 us
  waiting for transfers between devices: 0.03 us -> 0.62 us
    all_to_all x3, blocking collectives: 44.6 us -> 37 us  [the longest x1 15.6 us: body(): lax.all_to_all(msg, DP + MP, 0, 0, tiled=True, axis_index_groups=chips)]
    ppermute x0 -> x1, waiting for transfers between devices: none -> 0.58 us  [body(): arrived = lax.ppermute(msg_other, 'core', [(0, 1), (1, 0)])]
  transfers between devices with their start and end apart: 1 -> 2, of which waited for: 0 -> 1; matrix products, arithmetic and copies ran while one was open for 0% -> 0% of each run, Pallas kernels for 2% -> 3%
where the time goes in v5:
time: 47.5 us; the launch traced here: 47.3 us
  blocking collectives  37 us (78%)
  Pallas kernels  5.98 us (13%)
  starting transfers between devices  2.96 us (6%)
  between operations  0.68 us (1%)
  waiting for transfers between devices  0.62 us (1%)
    all_to_all x1, blocking collectives, body(): lax.all_to_all(msg, DP + MP, 0, 0, tiled=True, axis_index_groups=chips)  15.6 us
    all_to_all x1, blocking collectives, body(): lax.all_to_all(own, DP + MP, 0, 0, tiled=True, axis_index_groups=chips)  12.9 us
    all_to_all x1, blocking collectives, body(): p_all = lax.all_to_all(p_out, DP, 0, 0, tiled=True, axis_index_groups=near)  8.51 us
    pallas_call x1, Pallas kernels, body(): pl.pallas_call(correct_kernel, in_specs=[hbm, hbm, hbm], out_specs=vmem,...  2.71 us
    ppermute x1, starting transfers between devices, body(): other = lax.ppermute(half, 'core', [(0, 1), (1, 0)])  2.53 us
    pallas_call x1, Pallas kernels, body(): pl.pallas_call(finish_kernel, in_specs=[vmem] * 6, out_specs=[hbm] * 3, o...  1.34 us
    pallas_call x1, Pallas kernels, body(): pl.pallas_call(functools.partial(own_half_kernel, dp), in_specs=[vmem] *...  0.99 us
  transfers between devices with their start and end apart: 2, of which 1 were waited for; matrix products, arithmetic and copies ran while one was open for 0% of the time, Pallas kernels for 3%

profile of v5, /device:TPU:1, one launch (start us, length us, event | category | flops | bytes accessed | tf_op | source)
XLA Modules:
  0.0 47.3 jit_solution(14778689230187703287)
XLA Ops:
  0.6 0.0 copy-start.1
  0.6 0.0 copy-start
  0.7 2.7 %correct.1 = f32[8,8,128]{2,1,0:T(8,128)S(1)} custom-call(f32[1,64,5120]{2,1,0:T(8,128)} %g_ref.3, f32[1,64,5120]{2,1,0:T(8,128)} %f_ref.3, f32[16,5120]{1,0:T(8,128)} %q_hbm.1), custom_call_target="tpu_custom_call" | custom-call | tf_op jit(solution)/shard_map/correct/pallas_call | solution.py:258
  3.4 8.5 %all_to_all.15.p_ref = f32[8,8,128]{2,1,0:T(8,128)S(1)} all-to-all(f32[8,8,128]{2,1,0:T(8,128)S(1)} %correct.1), channel_id=1, replica_groups={{80,64,48,32,16,0,112,96},{81,65,49,33,17,1,113,97},{82,66,50,34,18,2,1..., dimensions={0} | all-to-all | bytes 65536 | tf_op jit(solution)/shard_map/all_to_all | solution.py:275
  11.9 0.0 copy-done.1
  11.9 0.0 copy-done
  11.9 0.4 project_other.1
  12.3 0.4 collective-permute-start
  12.7 0.5 %project_own.1 = (f32[384,128]{1,0:T(8,128)S(1)}, f32[64,2560]{1,0:T(8,128)S(1)}) custom-call(f32[16,64]{1,0:T(8,128)S(1)} %get-tuple-element.14.mean_ref, f32[1,64,5120]{2,1,0:T(8,128)S(1)} %copy-done, f32[1,64,5120]{2,1,0:T(8,128)S(1)} %copy-done.1), custom_call_target="tpu_custom_call" | custom-call | flops 62914560 | bytes 2621440 | tf_op jit(solution)/shard_map/project_own/pallas_call | solution.py:291
  13.2 0.6 %collective-permute-done = f32[384,128]{1,0:T(8,128)S(1)} collective-permute-done((f32[384,128]{1,0:T(8,128)S(1)}, f32[384,128]{1,0:T(8,128)S(1)}, u32[]{:S(2)}, u32[]{:S(2)}) %collective-permute-start) | collective-permute-done | bytes 196640 | tf_op jit(solution)/shard_map/ppermute | solution.py:290
  13.8 15.6 %all_to_all.16 = f32[64,1,768]{2,1,0:T(1,128)S(1)} all-to-all(f32[64,1,768]{2,1,0:T(1,128)S(1)} %bitcast.8), channel_id=1, replica_groups={{74,73,72,75,70,69,68,71,66,65,64,67,78,77,76,79,42,41,40,43,38,37,36,3..., dimensions={0} | all-to-all | bytes 393216 | tf_op jit(solution)/shard_map/all_to_all | solution.py:301
  29.5 12.9 %all_to_all.17 = f32[64,1,640]{2,1,0:T(1,128)S(1)} all-to-all(f32[64,1,640]{2,1,0:T(1,128)S(1)} %bitcast.7), channel_id=1, replica_groups={{74,73,72,75,70,69,68,71,66,65,64,67,78,77,76,79,42,41,40,43,38,37,36,3..., dimensions={0} | all-to-all | bytes 327680 | tf_op jit(solution)/shard_map/all_to_all | solution.py:316
  42.4 2.5 %collective-permute-start.1 = (f32[320,128]{1,0:T(8,128)S(1)}, f32[320,128]{1,0:T(8,128)S(1)}, u32[]{:S(2)}, u32[]{:S(2)}) collective-permute-start(f32[320,128]{1,0:T(8,128)S(1)} %bitcast.5), channel_id=1, source_target_pairs={{0,16},{16,0},{1,17},{17,1},{2,18},{18,2},{3,19},{19,3},{4,20},{20... | collective-permute-start | bytes 491528 | tf_op jit(solution)/shard_map/ppermute | solution.py:317
  44.9 1.0 %own_half.1 = (bf16[80,96]{1,0:T(8,128)(2,1)S(1)}, f32[16,64]{1,0:T(8,128)S(1)}, f32[16,2560]{1,0:T(8,128)S(1)}, f32[64,2560]{1,0:T(8,128)S(1)}) custom-call(f32[16,128]{1,0:T(8,128)S(1)} %get-tuple-element.17.gram_ref, f32[320,128]{1,0:T(8,128)S(1)} %bitcast.6, f32[16,64]{1,0:T(8,128)S(1)} %get-tuple-element.14.mean_ref, f32[64,2560]{1,0:T(8,128)S(1)} %get-tuple-element.19.c_ref), custom_call_target="tpu_custom_call" | custom-call | flops 62914560 | bytes 2621440 | tf_op jit(solution)/shard_map/own_half/pallas_call | solution.py:319
  45.9 0.0 collective-permute-done.1.half_ref
  45.9 1.3 %finish.1 = (f32[1,64,5120]{2,1,0:T(8,128)}, f32[16,64]{1,0:T(8,128)}, f32[16,5120]{1,0:T(8,128)}) custom-call(bf16[80,96]{1,0:T(8,128)(2,1)S(1)} %get-tuple-element.20.left_ref, f32[16,64]{1,0:T(8,128)S(1)} %get-tuple-element.21.po_ref, f32[16,2560]{1,0:T(8,128)S(1)} %get-tuple-element.22.qf_ref, f32[64,2560]{1,0:T(8,128)S(1)} %get-tuple-element.23.nf_ref, ...), custom_call_target="tpu_custom_call" | custom-call | tf_op jit(solution)/shard_map/finish/pallas_call | solution.py:333
  (2 shorter events, 0.1 us)
Async XLA Ops:
  0.6 11.2 %copy-start.1 = (f32[1,64,5120]{2,1,0:T(8,128)S(1)}, f32[1,64,5120]{2,1,0:T(8,128)}, u32[]{:S(2)}) copy-start(f32[1,64,5120]{2,1,0:T(8,128)} %f_ref.3) | copy-start | bytes 3932164
  0.6 11.2 %copy-start = (f32[1,64,5120]{2,1,0:T(8,128)S(1)}, f32[1,64,5120]{2,1,0:T(8,128)}, u32[]{:S(2)}) copy-start(f32[1,64,5120]{2,1,0:T(8,128)} %g_ref.3) | copy-start | bytes 3932164
  12.3 1.5 %collective-permute-start = (f32[384,128]{1,0:T(8,128)S(1)}, f32[384,128]{1,0:T(8,128)S(1)}, u32[]{:S(2)}, u32[]{:S(2)}) collective-permute-start(f32[384,128]{1,0:T(8,128)S(1)} %get-tuple-element.16), channel_id=1, source_target_pairs={{0,16},{16,0},{1,17},{17,1},{2,18},{18,2},{3,19},{19,3},{4,20},{20... | collective-permute-start | bytes 589832 | tf_op jit(solution)/shard_map/ppermute | solution.py:290
  42.4 3.6 %collective-permute-start.1 = (f32[320,128]{1,0:T(8,128)S(1)}, f32[320,128]{1,0:T(8,128)S(1)}, u32[]{:S(2)}, u32[]{:S(2)}) collective-permute-start(f32[320,128]{1,0:T(8,128)S(1)} %bitcast.5), channel_id=1, source_target_pairs={{0,16},{16,0},{1,17},{17,1},{2,18},{18,2},{3,19},{19,3},{4,20},{20... | collective-permute-start | bytes 491528 | tf_op jit(solution)/shard_map/ppermute | solution.py:317

commit v6 on v5

--- a/solution.py
+++ b/solution.py
@@ -9,8 +9,8 @@
 from jax.sharding import PartitionSpec as P
 
 LANES = 128
-IN_PARTS = 5
-IN_TILE = 512
+IN_PARTS = 4
+IN_TILE = 640
 CORES = 2
 HALF_GROUPS = 4
 DP = ("x", "core")
@@ -46,34 +46,48 @@
     return (parts[2] + parts[1]) + parts[0]
 
 
-def correct_kernel(g_hbm, f_hbm, q_hbm, p_ref, g_buf, f_buf, q_buf, sems):
-    width = g_buf.shape[1] // IN_PARTS
+def correct_kernel(g_hbm, f_hbm, q_hbm, p_ref, c_hbm, g_buf, f_buf, q_buf, c_buf, sems, c_sems):
+    half = c_buf.shape[1]
+    parts = IN_PARTS // CORES
+    width = half // parts
+    core = lax.axis_index("core")
     copies = []
     for s in range(IN_PARTS):
-        cols = pl.ds(s * width, width)
+        first = (1 - core if s < parts else core) * half + s % parts * width
+        there = pl.ds(pl.multiple_of(first, width), width)
+        here = pl.ds(s * width, width)
         part = [
-            pltpu.make_async_copy(g_hbm.at[0, :, cols], g_buf.at[:, cols], sems.at[0, s]),
-            pltpu.make_async_copy(f_hbm.at[0, :, cols], f_buf.at[:, cols], sems.at[1, s]),
-            pltpu.make_async_copy(q_hbm.at[:, cols], q_buf.at[:, cols], sems.at[2, s]),
+            pltpu.make_async_copy(g_hbm.at[0, :, there], g_buf.at[:, here], sems.at[0, s]),
+            pltpu.make_async_copy(f_hbm.at[0, :, there], f_buf.at[:, here], sems.at[1, s]),
+            pltpu.make_async_copy(q_hbm.at[:, there], q_buf.at[:, here], sems.at[2, s]),
         ]
         for copy in part:
             copy.start()
         copies.append(part)
     total = None
+    sends = []
     for s in range(IN_PARTS):
         for copy in copies[s]:
             copy.wait()
         for at in range(s * width, (s + 1) * width, IN_TILE):
             cols = slice(at, at + IN_TILE)
             local = g_buf[:, cols] + f_buf[:, cols]
+            if s < parts:
+                c_buf[:, cols] = local
             left = jnp.concatenate(split(q_buf[:, cols]), axis=0)
             right = jnp.concatenate(split(local), axis=0)
             part = bf16_dot(left, right, 1, 1)
             total = part if total is None else total + part
+        if s < parts:
+            cols = pl.ds(s * width, width)
+            sends.append(pltpu.make_async_copy(c_buf.at[:, cols], c_hbm.at[:, cols], c_sems.at[s]))
+            sends[-1].start()
     total = fold(fold(total, total.shape[0] // 3, 0), total.shape[1] // 3, 1)
     half = total.shape[0] // 2
     packed = jnp.concatenate([total[:half], total[half:]], axis=1)
     p_ref[...] = jnp.broadcast_to(packed[None], p_ref.shape)
+    for copy in sends:
+        copy.wait()
 
 
 def member_of(place):
@@ -97,31 +111,7 @@
     return pl.multiple_of((core * HALF_GROUPS + n) * width, width)
 
 
-def write_half(mean, core, g_ref, f_ref, msg_ref, c_ref):
-    rank = mean.shape[0]
-    width = c_ref.shape[1] // HALF_GROUPS
-    tiles = width // LANES
-    high, mid, low = split(mean)
-    none = jnp.zeros_like(high)
-    left = jnp.concatenate(
-        [jnp.concatenate(parts, axis=1) for parts in ((high, high, high), (mid, mid, none), (low, none, none))], axis=0
-    )
-    for n in range(HALF_GROUPS):
-        cols = pl.ds(column_at(core, n, width), width)
-        local = g_ref[0, :, cols] + f_ref[0, :, cols]
-        c_ref[:, n * width : (n + 1) * width] = local
-        out = fold(bf16_dot(left, jnp.concatenate(split(local), axis=0), 1, 0), rank, 0)
-        for i in range(tiles):
-            first = n * rank * (tiles + 1) + i
-            msg_ref[pl.ds(first, rank, stride=tiles + 1), :] = out[:, i * LANES : (i + 1) * LANES]
-
-
-def write_last(msg_ref, line):
-    count = msg_ref.shape[0] // 6
-    msg_ref[pl.ds(5, count, stride=6), :] = jnp.broadcast_to(line, (count, LANES))
-
-
-def other_kernel(p_ref, g_ref, f_ref, msg_ref, mean_ref, c_ref):
+def project_kernel(p_ref, g_ref, f_ref, arrived_ref, msg_ref, mean_ref):
     replicas = p_ref.shape[0]
     total = p_ref[0]
     for n in range(1, replicas):
@@ -130,21 +120,30 @@
     half = total.shape[1] // 2
     mean = jnp.concatenate([total[:, :half], total[:, half:]], axis=0)
     mean_ref[...] = mean
-    write_half(mean, 1 - lax.axis_index("core"), g_ref, f_ref, msg_ref, c_ref)
-    write_last(msg_ref, jnp.zeros((1, LANES), jnp.float32))
-
-
-def own_kernel(mean_ref, g_ref, f_ref, msg_ref, c_ref):
-    mean = mean_ref[...]
     rank = mean.shape[0]
-    write_half(mean, lax.axis_index("core"), g_ref, f_ref, msg_ref, c_ref)
+    high, mid, low = split(mean)
+    none = jnp.zeros_like(high)
+    left = jnp.concatenate(
+        [jnp.concatenate(parts, axis=1) for parts in ((high, high, high), (mid, mid, none), (low, none, none))], axis=0
+    )
+    width = arrived_ref.shape[1] // HALF_GROUPS
+    tiles = width // LANES
+    for n in range(HALF_GROUPS):
+        cols = pl.ds(column_at(lax.axis_index("core"), n, width), width)
+        pair = (g_ref[0, :, cols] + f_ref[0, :, cols]) + arrived_ref[:, n * width : (n + 1) * width]
+        out = fold(bf16_dot(left, jnp.concatenate(split(pair), axis=0), 1, 0), rank, 0)
+        for i in range(tiles):
+            first = n * rank * (tiles + 1) + i
+            msg_ref[pl.ds(first, rank, stride=tiles + 1), :] = out[:, i * LANES : (i + 1) * LANES]
     gram = dot(mean, jnp.concatenate([mean] * (LANES // rank), axis=0), 1, 1)
     share = rank // HALF_GROUPS
     row = lax.broadcasted_iota(jnp.int32, (rank, LANES), 0)
     lane = lax.broadcasted_iota(jnp.int32, (rank, LANES), 1)
     mine = row - share * member_of(lax.axis_index("x"))
     kept = (lane >= rank * mine) & (lane < rank * (mine + 1)) & (mine >= 0) & (mine < share)
-    write_last(msg_ref, jnp.sum(jnp.where(kept, gram, 0.0), axis=0, keepdims=True))
+    line = jnp.sum(jnp.where(kept, gram, 0.0), axis=0, keepdims=True)
+    count = msg_ref.shape[0] // (tiles + 1)
+    msg_ref[pl.ds(tiles, count, stride=tiles + 1), :] = jnp.broadcast_to(line, (count, LANES))
 
 
 def sum_kernel(in_ref, out_ref, gram_ref, part):
@@ -186,18 +185,19 @@
     return right * (1.0 / jnp.sqrt(pivots))
 
 
-def half_block(left, half_ref, c_ref, n, rank):
-    width = c_ref.shape[1] // HALF_GROUPS
+def half_block(left, half_ref, g_ref, f_ref, core, n, rank):
+    width = g_ref.shape[2] // CORES // HALF_GROUPS
     tiles = width // LANES
     raw = jnp.concatenate(
         [half_ref[pl.ds(n * rank * tiles + i, rank, stride=tiles), :] for i in range(tiles)], axis=1
     )
     high, mid, low = split(raw)
     out = bf16_dot(left, jnp.concatenate([high, mid, high, low, high, mid], axis=0), 1, 0)
-    return out[:rank], c_ref[:, n * width : (n + 1) * width] - out[rank:]
-
-
-def own_half_kernel(replicas, gram_ref, half_ref, mean_ref, c_ref, left_ref, po_ref, qf_ref, nf_ref):
+    cols = pl.ds(column_at(core, n, width), width)
+    return out[:rank], (g_ref[0, :, cols] + f_ref[0, :, cols]) - out[rank:]
+
+
+def own_half_kernel(replicas, gram_ref, half_ref, mean_ref, g_ref, f_ref, left_ref, po_ref, qf_ref, nf_ref):
     rank = mean_ref.shape[0]
     whole = inverse_factor(gram_ref[...])
     lower = whole[:, :rank]
@@ -208,18 +208,19 @@
     high, mid, low = split(both)
     left = jnp.concatenate([high, high, mid, high, low, mid], axis=1)
     left_ref[...] = left
-    width = c_ref.shape[1] // HALF_GROUPS
+    width = qf_ref.shape[1] // HALF_GROUPS
+    core = lax.axis_index("core")
     for n in range(HALF_GROUPS):
         cols = slice(n * width, (n + 1) * width)
-        qf_ref[:, cols], nf_ref[:, cols] = half_block(left, half_ref, c_ref, n, rank)
+        qf_ref[:, cols], nf_ref[:, cols] = half_block(left, half_ref, g_ref, f_ref, core, n, rank)
 
 
 def finish_kernel(
-    left_ref, po_ref, qf_ref, nf_ref, half_ref, c_ref, nf_hbm, po_hbm, qf_hbm, nf_buf, qf_buf, sems, half_sems
+    left_ref, po_ref, qf_ref, nf_ref, half_ref, g_ref, f_ref, nf_hbm, po_hbm, qf_hbm, nf_buf, qf_buf, sems, half_sems
 ):
     rank = po_ref.shape[0]
     core = lax.axis_index("core")
-    width = c_ref.shape[1] // HALF_GROUPS
+    width = qf_ref.shape[1] // HALF_GROUPS
     own = pl.ds(column_at(core, 0, width), HALF_GROUPS * width)
     copies = [
         pltpu.make_async_copy(nf_ref, nf_hbm.at[0, :, own], half_sems.at[0]),
@@ -231,7 +232,7 @@
     left = left_ref[...]
     for n in range(HALF_GROUPS):
         cols = slice(n * width, (n + 1) * width)
-        qf_buf[:, cols], nf_buf[:, cols] = half_block(left, half_ref, c_ref, n, rank)
+        qf_buf[:, cols], nf_buf[:, cols] = half_block(left, half_ref, g_ref, f_ref, 1 - core, n, rank)
         here = pl.ds(n * width, width)
         there = pl.ds(column_at(1 - core, n, width), width)
         part = [
@@ -255,16 +256,21 @@
     hbm = pl.BlockSpec(memory_space=pltpu.HBM)
     params = pltpu.CompilerParams(vmem_limit_bytes=16 * 2**20)
 
-    p_out = pl.pallas_call(
+    p_out, c_send = pl.pallas_call(
         correct_kernel,
         in_specs=[hbm, hbm, hbm],
-        out_specs=vmem,
-        out_shape=jax.ShapeDtypeStruct((dp, rank // 2, 2 * rows), f32),
+        out_specs=[vmem, hbm],
+        out_shape=[
+            jax.ShapeDtypeStruct((dp, rank // 2, 2 * rows), f32),
+            jax.ShapeDtypeStruct((rows, width // CORES), f32),
+        ],
         scratch_shapes=[
             pltpu.VMEM((rows, width), f32),
             pltpu.VMEM((rows, width), f32),
             pltpu.VMEM((rank, width), f32),
+            pltpu.VMEM((rows, width // CORES), f32),
             pltpu.SemaphoreType.DMA((3, IN_PARTS)),
+            pltpu.SemaphoreType.DMA((IN_PARTS // CORES,)),
         ],
         compiler_params=pltpu.CompilerParams(vmem_limit_bytes=int(53.75 * 2**20)),
         name="correct",
@@ -272,32 +278,22 @@
     sizes = tuple(lax.axis_size(name) for name in DP + MP)
     near = [[member_of(i) * CORES + core for i in range(sizes[0]) for core in (1, 0)]]
     chips = chip_groups(sizes)
+    arrived = lax.ppermute(c_send, "core", [(0, 1), (1, 0)])
     p_all = lax.all_to_all(p_out, DP, 0, 0, tiled=True, axis_index_groups=near)
 
     count = sizes[0] * mp
-    half_out = [
-        jax.ShapeDtypeStruct((count * (tiles + 1), LANES), f32),
-        jax.ShapeDtypeStruct((rows, width // CORES), f32),
-    ]
-    msg_other, p_mean, local_other = pl.pallas_call(
-        other_kernel,
-        in_specs=[vmem] * 3,
-        out_specs=[vmem] * 3,
-        out_shape=[half_out[0], jax.ShapeDtypeStruct((rank, rows), f32), half_out[1]],
+    msg, p_mean = pl.pallas_call(
+        project_kernel,
+        in_specs=[vmem] * 4,
+        out_specs=[vmem] * 2,
+        out_shape=[
+            jax.ShapeDtypeStruct((count * (tiles + 1), LANES), f32),
+            jax.ShapeDtypeStruct((rank, rows), f32),
+        ],
         compiler_params=params,
-        name="project_other",
-    )(p_all, gradient, feedback)
-    arrived = lax.ppermute(msg_other, "core", [(0, 1), (1, 0)])
-    msg_own, local_own = pl.pallas_call(
-        own_kernel,
-        in_specs=[vmem] * 3,
-        out_specs=[vmem] * 2,
-        out_shape=half_out,
-        compiler_params=params,
-        cost_estimate=pl.CostEstimate(flops=2 * rows * width * 96, bytes_accessed=8 * rows * width, transcendentals=0),
-        name="project_own",
-    )(p_mean, gradient, feedback)
-    msg = (msg_own + arrived).reshape(count, 1, (tiles + 1) * LANES)
+        name="project",
+    )(p_all, gradient, feedback, arrived)
+    msg = msg.reshape(count, 1, (tiles + 1) * LANES)
     terms = lax.all_to_all(msg, DP + MP, 0, 0, tiled=True, axis_index_groups=chips)
 
     own, gram = pl.pallas_call(
@@ -318,7 +314,7 @@
 
     left, p_ortho, q_half, f_half = pl.pallas_call(
         functools.partial(own_half_kernel, dp),
-        in_specs=[vmem] * 4,
+        in_specs=[vmem] * 5,
         out_specs=[vmem] * 4,
         out_shape=[
             jax.ShapeDtypeStruct((rank + rows, 6 * rank), jnp.bfloat16),
@@ -329,10 +325,10 @@
         compiler_params=params,
         cost_estimate=pl.CostEstimate(flops=2 * rows * width * 96, bytes_accessed=8 * rows * width, transcendentals=0),
         name="own_half",
-    )(gram, half, p_mean, local_own)
+    )(gram, half, p_mean, gradient, feedback)
     new_feedback, p_ortho, q_factor = pl.pallas_call(
         finish_kernel,
-        in_specs=[vmem] * 6,
+        in_specs=[vmem] * 7,
         out_specs=[hbm] * 3,
         out_shape=[
             jax.ShapeDtypeStruct((1, rows, width), f32),
@@ -347,7 +343,7 @@
         ],
         compiler_params=params,
         name="finish",
-    )(left, p_ortho, q_half, f_half, other, local_other)
+    )(left, p_ortho, q_half, f_half, other, gradient, feedback)
     return (new_feedback, p_ortho, q_factor)
 
 

time: 47.5 us -> 46.9 us (0.987)
  starting transfers between devices: 2.96 us -> 4.07 us
  blocking collectives: 37 us -> 36.1 us
  waiting for transfers between devices: 0.62 us -> 0.02 us
    ppermute x1, starting transfers between devices: 0.43 us -> 1.5 us  [body(): arrived = lax.ppermute(c_send, 'core', [(0, 1), (1, 0)])]
    all_to_all x1, blocking collectives: 8.51 us -> 7.57 us  [body(): p_all = lax.all_to_all(p_out, DP, 0, 0, tiled=True, axis_index_groups=near)]
    ppermute x1, waiting for transfers between devices: 0.58 us -> 0.01 us  [body(): arrived = lax.ppermute(c_send, 'core', [(0, 1), (1, 0)])]
    pallas_call x4 -> x3, Pallas kernels: 4.95 us -> 4.84 us  [the longest x1 3.05 us: body(): pl.pallas_call(correct_kernel, in_specs=[hbm, hbm, hbm], out_specs=[vmem,...]
  transfers between devices with their start and end apart: 2 -> 2, of which waited for: 1 -> 0; matrix products, arithmetic and copies ran while one was open for 0% -> 0% of each run, Pallas kernels for 3% -> 2%
where the time goes in v6:
time: 46.9 us; the launch traced here: 46.7 us
  blocking collectives  36.1 us (77%)
  Pallas kernels  5.88 us (13%)
  starting transfers between devices  4.07 us (9%)
  between operations  0.68 us (1%)
    all_to_all x1, blocking collectives, body(): lax.all_to_all(msg, DP + MP, 0, 0, tiled=True, axis_index_groups=chips)  15.6 us
    all_to_all x1, blocking collectives, body(): lax.all_to_all(own, DP + MP, 0, 0, tiled=True, axis_index_groups=chips)  12.9 us
    all_to_all x1, blocking collectives, body(): p_all = lax.all_to_all(p_out, DP, 0, 0, tiled=True, axis_index_groups=near)  7.57 us
    pallas_call x1, Pallas kernels, body(): pl.pallas_call(correct_kernel, in_specs=[hbm, hbm, hbm], out_specs=[vmem,...  3.05 us
    ppermute x1, starting transfers between devices, body(): other = lax.ppermute(half, 'core', [(0, 1), (1, 0)])  2.57 us
    ppermute x1, starting transfers between devices, body(): arrived = lax.ppermute(c_send, 'core', [(0, 1), (1, 0)])  1.5 us
    pallas_call x1, Pallas kernels, body(): pl.pallas_call(finish_kernel, in_specs=[vmem] * 7, out_specs=[hbm] * 3, o...  1.25 us
    pallas_call x1, Pallas kernels, body(): pl.pallas_call(functools.partial(own_half_kernel, dp), in_specs=[vmem] *...  1 us
  transfers between devices with their start and end apart: 2, of which 0 were waited for; matrix products, arithmetic and copies ran while one was open for 0% of the time, Pallas kernels for 2%

profile of v6, /device:TPU:1, one launch (start us, length us, event | category | flops | bytes accessed | tf_op | source)
XLA Modules:
  0.0 46.7 jit_solution(9200453531772418157)
XLA Ops:
  0.6 0.0 copy-start.1
  0.6 0.0 copy-start
  0.7 3.0 %correct.1 = (f32[8,8,128]{2,1,0:T(8,128)S(1)}, f32[64,2560]{1,0:T(8,128)}) custom-call(f32[1,64,5120]{2,1,0:T(8,128)} %g_ref.5, f32[1,64,5120]{2,1,0:T(8,128)} %f_ref.5, f32[16,5120]{1,0:T(8,128)} %q_hbm.1), custom_call_target="tpu_custom_call" | custom-call | tf_op jit(solution)/shard_map/correct/pallas_call | solution.py:259
  3.7 1.5 %collective-permute-start = (f32[64,2560]{1,0:T(8,128)}, f32[64,2560]{1,0:T(8,128)S(1)}, u32[]{:S(2)}, u32[]{:S(2)}) collective-permute-start(f32[64,2560]{1,0:T(8,128)} %get-tuple-element.14), channel_id=1, source_target_pairs={{0,16},{16,0},{1,17},{17,1},{2,18},{18,2},{3,19},{19,3},{4,20},{20... | collective-permute-start | bytes 1966088 | tf_op jit(solution)/shard_map/ppermute | solution.py:281
  5.2 7.6 %all_to_all.15.p_ref = f32[8,8,128]{2,1,0:T(8,128)S(1)} all-to-all(f32[8,8,128]{2,1,0:T(8,128)S(1)} %get-tuple-element.13), channel_id=1, replica_groups={{80,64,48,32,16,0,112,96},{81,65,49,33,17,1,113,97},{82,66,50,34,18,2,1..., dimensions={0} | all-to-all | bytes 65536 | tf_op jit(solution)/shard_map/all_to_all | solution.py:282
  12.8 0.0 collective-permute-done.arrived_ref
  12.8 0.0 copy-done.1
  12.8 0.0 copy-done
  12.8 0.5 %project.1 = (f32[384,128]{1,0:T(8,128)S(1)}, f32[16,64]{1,0:T(8,128)S(1)}) custom-call(f32[8,8,128]{2,1,0:T(8,128)S(1)} %all_to_all.15.p_ref, f32[1,64,5120]{2,1,0:T(8,128)S(1)} %copy-done, f32[1,64,5120]{2,1,0:T(8,128)S(1)} %copy-done.1, f32[64,2560]{1,0:T(8,128)S(1)} %collective-permute-done.arrived_ref), custom_call_target="tpu_custom_call" | custom-call | tf_op jit(solution)/shard_map/project/pallas_call | solution.py:285
  13.3 15.6 %all_to_all.16 = f32[64,1,768]{2,1,0:T(1,128)S(1)} all-to-all(f32[64,1,768]{2,1,0:T(1,128)S(1)} %bitcast.7), channel_id=1, replica_groups={{74,73,72,75,70,69,68,71,66,65,64,67,78,77,76,79,42,41,40,43,38,37,36,3..., dimensions={0} | all-to-all | bytes 393216 | tf_op jit(solution)/shard_map/all_to_all | solution.py:297
  29.0 12.9 %all_to_all.17 = f32[64,1,640]{2,1,0:T(1,128)S(1)} all-to-all(f32[64,1,640]{2,1,0:T(1,128)S(1)} %bitcast.8), channel_id=1, replica_groups={{74,73,72,75,70,69,68,71,66,65,64,67,78,77,76,79,42,41,40,43,38,37,36,3..., dimensions={0} | all-to-all | bytes 327680 | tf_op jit(solution)/shard_map/all_to_all | solution.py:312
  41.9 2.6 %collective-permute-start.1 = (f32[320,128]{1,0:T(8,128)S(1)}, f32[320,128]{1,0:T(8,128)S(1)}, u32[]{:S(2)}, u32[]{:S(2)}) collective-permute-start(f32[320,128]{1,0:T(8,128)S(1)} %bitcast.5), channel_id=1, source_target_pairs={{0,16},{16,0},{1,17},{17,1},{2,18},{18,2},{3,19},{19,3},{4,20},{20... | collective-permute-start | bytes 491528 | tf_op jit(solution)/shard_map/ppermute | solution.py:313
  44.4 1.0 %own_half.1 = (bf16[80,96]{1,0:T(8,128)(2,1)S(1)}, f32[16,64]{1,0:T(8,128)S(1)}, f32[16,2560]{1,0:T(8,128)S(1)}, f32[64,2560]{1,0:T(8,128)S(1)}) custom-call(f32[16,128]{1,0:T(8,128)S(1)} %get-tuple-element.16.gram_ref, f32[320,128]{1,0:T(8,128)S(1)} %bitcast.6, f32[16,64]{1,0:T(8,128)S(1)} %get-tuple-element.18.mean_ref, f32[1,64,5120]{2,1,0:T(8,128)S(1)} %copy-done, ...), custom_call_target="tpu_custom_call" | custom-call | flops 62914560 | bytes 2621440 | tf_op jit(solution)/shard_map/own_half/pallas_call | solution.py:315
  45.4 0.0 collective-permute-done.1.half_ref
  45.5 1.3 %finish.1 = (f32[1,64,5120]{2,1,0:T(8,128)}, f32[16,64]{1,0:T(8,128)}, f32[16,5120]{1,0:T(8,128)}) custom-call(bf16[80,96]{1,0:T(8,128)(2,1)S(1)} %get-tuple-element.19.left_ref, f32[16,64]{1,0:T(8,128)S(1)} %get-tuple-element.20.po_ref, f32[16,2560]{1,0:T(8,128)S(1)} %get-tuple-element.21.qf_ref, f32[64,2560]{1,0:T(8,128)S(1)} %get-tuple-element.22.nf_ref, ...), custom_call_target="tpu_custom_call" | custom-call | tf_op jit(solution)/shard_map/finish/pallas_call | solution.py:329
  (1 shorter events, 0.0 us)
Async XLA Ops:
  0.6 12.2 %copy-start.1 = (f32[1,64,5120]{2,1,0:T(8,128)S(1)}, f32[1,64,5120]{2,1,0:T(8,128)}, u32[]{:S(2)}) copy-start(f32[1,64,5120]{2,1,0:T(8,128)} %f_ref.5) | copy-start | bytes 3932164
  0.6 12.1 %copy-start = (f32[1,64,5120]{2,1,0:T(8,128)S(1)}, f32[1,64,5120]{2,1,0:T(8,128)}, u32[]{:S(2)}) copy-start(f32[1,64,5120]{2,1,0:T(8,128)} %g_ref.5) | copy-start | bytes 3932164
  3.7 9.1 %collective-permute-start = (f32[64,2560]{1,0:T(8,128)}, f32[64,2560]{1,0:T(8,128)S(1)}, u32[]{:S(2)}, u32[]{:S(2)}) collective-permute-start(f32[64,2560]{1,0:T(8,128)} %get-tuple-element.14), channel_id=1, source_target_pairs={{0,16},{16,0},{1,17},{17,1},{2,18},{18,2},{3,19},{19,3},{4,20},{20... | collective-permute-start | bytes 1966088 | tf_op jit(solution)/shard_map/ppermute | solution.py:281
  41.9 3.6 %collective-permute-start.1 = (f32[320,128]{1,0:T(8,128)S(1)}, f32[320,128]{1,0:T(8,128)S(1)}, u32[]{:S(2)}, u32[]{:S(2)}) collective-permute-start(f32[320,128]{1,0:T(8,128)S(1)} %bitcast.5), channel_id=1, source_target_pairs={{0,16},{16,0},{1,17},{17,1},{2,18},{18,2},{3,19},{19,3},{4,20},{20... | collective-permute-start | bytes 491528 | tf_op jit(solution)/shard_map/ppermute | solution.py:313

commit v7 on v6

--- a/solution.py
+++ b/solution.py
@@ -10,7 +10,7 @@
 
 LANES = 128
 IN_PARTS = 4
-IN_TILE = 640
+IN_TILE = 256
 CORES = 2
 HALF_GROUPS = 4
 DP = ("x", "core")
@@ -50,7 +50,7 @@
     half = c_buf.shape[1]
     parts = IN_PARTS // CORES
     width = half // parts
-    core = lax.axis_index("core")
+    core = half_of_core()
     copies = []
     for s in range(IN_PARTS):
         first = (1 - core if s < parts else core) * half + s % parts * width
@@ -98,13 +98,19 @@
     nx, nc, nz, ny = sizes
     return [
         [
-            ((member_of(i) * nc + core) * nz + member_of(j)) * ny + member_of(k)
+            ((member_of(i) * nc + (core ^ int(i + j + k == 0))) * nz + member_of(j)) * ny + member_of(k)
             for i in range(nx)
             for j in range(nz)
             for k in range(ny)
         ]
         for core in range(nc)
     ]
+
+
+def half_of_core():
+    core = lax.axis_index("core")
+    leads = (lax.axis_index("x") == 2) & (lax.axis_index("z") == 2) & (lax.axis_index("y") == 2)
+    return jnp.where(leads, 1 - core, core)
 
 
 def column_at(core, n, width):
@@ -129,7 +135,7 @@
     width = arrived_ref.shape[1] // HALF_GROUPS
     tiles = width // LANES
     for n in range(HALF_GROUPS):
-        cols = pl.ds(column_at(lax.axis_index("core"), n, width), width)
+        cols = pl.ds(column_at(half_of_core(), n, width), width)
         pair = (g_ref[0, :, cols] + f_ref[0, :, cols]) + arrived_ref[:, n * width : (n + 1) * width]
         out = fold(bf16_dot(left, jnp.concatenate(split(pair), axis=0), 1, 0), rank, 0)
         for i in range(tiles):
@@ -209,7 +215,7 @@
     left = jnp.concatenate([high, high, mid, high, low, mid], axis=1)
     left_ref[...] = left
     width = qf_ref.shape[1] // HALF_GROUPS
-    core = lax.axis_index("core")
+    core = half_of_core()
     for n in range(HALF_GROUPS):
         cols = slice(n * width, (n + 1) * width)
         qf_ref[:, cols], nf_ref[:, cols] = half_block(left, half_ref, g_ref, f_ref, core, n, rank)
@@ -219,7 +225,7 @@
     left_ref, po_ref, qf_ref, nf_ref, half_ref, g_ref, f_ref, nf_hbm, po_hbm, qf_hbm, nf_buf, qf_buf, sems, half_sems
 ):
     rank = po_ref.shape[0]
-    core = lax.axis_index("core")
+    core = half_of_core()
     width = qf_ref.shape[1] // HALF_GROUPS
     own = pl.ds(column_at(core, 0, width), HALF_GROUPS * width)
     copies = [
@@ -276,8 +282,9 @@
         name="correct",
     )(gradient, feedback, q_previous)
     sizes = tuple(lax.axis_size(name) for name in DP + MP)
-    near = [[member_of(i) * CORES + core for i in range(sizes[0]) for core in (1, 0)]]
+    near = [[member_of(i) * CORES + core for i in range(sizes[0]) for core in (0, 1)]]
     chips = chip_groups(sizes)
+    chips[1][0], chips[1][12] = chips[1][12], chips[1][0]
     arrived = lax.ppermute(c_send, "core", [(0, 1), (1, 0)])
     p_all = lax.all_to_all(p_out, DP, 0, 0, tiled=True, axis_index_groups=near)
 

time: 46.9 us -> 46.2 us (0.985)
  starting transfers between devices: 4.07 us -> 2.71 us
  blocking collectives: 36.1 us -> 36.8 us
    ppermute x1, starting transfers between devices: 2.57 us -> 1.21 us  [body(): other = lax.ppermute(half, 'core', [(0, 1), (1, 0)])]
    all_to_all x1, blocking collectives: 15.6 us -> 16.6 us  [body(): lax.all_to_all(msg, DP + MP, 0, 0, tiled=True, axis_index_groups=chips)]
where the time goes in v7:
time: 46.2 us; the launch traced here: 46 us
  blocking collectives  36.8 us (80%)
  Pallas kernels  5.77 us (12%)
  starting transfers between devices  2.71 us (6%)
  between operations  0.68 us (1%)
    all_to_all x1, blocking collectives, body(): lax.all_to_all(msg, DP + MP, 0, 0, tiled=True, axis_index_groups=chips)  16.6 us
    all_to_all x1, blocking collectives, body(): lax.all_to_all(own, DP + MP, 0, 0, tiled=True, axis_index_groups=chips)  13 us
    all_to_all x1, blocking collectives, body(): p_all = lax.all_to_all(p_out, DP, 0, 0, tiled=True, axis_index_groups=near)  7.15 us
    pallas_call x1, Pallas kernels, body(): pl.pallas_call(correct_kernel, in_specs=[hbm, hbm, hbm], out_specs=[vmem,...  2.85 us
    ppermute x1, starting transfers between devices, body(): arrived = lax.ppermute(c_send, 'core', [(0, 1), (1, 0)])  1.5 us
    pallas_call x1, Pallas kernels, body(): pl.pallas_call(finish_kernel, in_specs=[vmem] * 7, out_specs=[hbm] * 3, o...  1.33 us
    ppermute x1, starting transfers between devices, body(): other = lax.ppermute(half, 'core', [(0, 1), (1, 0)])  1.21 us
    pallas_call x1, Pallas kernels, body(): pl.pallas_call(functools.partial(own_half_kernel, dp), in_specs=[vmem] *...  1 us
  transfers between devices with their start and end apart: 2, of which 0 were waited for; matrix products, arithmetic and copies ran while one was open for 0% of the time, Pallas kernels for 2%

profile of v7, /device:TPU:1, one launch (start us, length us, event | category | flops | bytes accessed | tf_op | source)
XLA Modules:
  0.0 46.0 jit_solution(13753891104000176937)
XLA Ops:
  0.6 0.0 copy-start.1
  0.6 0.0 copy-start
  0.7 2.8 %correct.1 = (f32[8,8,128]{2,1,0:T(8,128)S(1)}, f32[64,2560]{1,0:T(8,128)}) custom-call(f32[1,64,5120]{2,1,0:T(8,128)} %g_ref.5, f32[1,64,5120]{2,1,0:T(8,128)} %f_ref.5, f32[16,5120]{1,0:T(8,128)} %q_hbm.1), custom_call_target="tpu_custom_call" | custom-call | tf_op jit(solution)/shard_map/correct/pallas_call | solution.py:265
  3.5 1.5 %collective-permute-start = (f32[64,2560]{1,0:T(8,128)}, f32[64,2560]{1,0:T(8,128)S(1)}, u32[]{:S(2)}, u32[]{:S(2)}) collective-permute-start(f32[64,2560]{1,0:T(8,128)} %get-tuple-element.14), channel_id=1, source_target_pairs={{0,16},{16,0},{1,17},{17,1},{2,18},{18,2},{3,19},{19,3},{4,20},{20... | collective-permute-start | bytes 1966088 | tf_op jit(solution)/shard_map/ppermute | solution.py:288
  5.0 7.2 %all_to_all.15.p_ref = f32[8,8,128]{2,1,0:T(8,128)S(1)} all-to-all(f32[8,8,128]{2,1,0:T(8,128)S(1)} %get-tuple-element.13), channel_id=1, replica_groups={{64,80,32,48,0,16,96,112},{65,81,33,49,1,17,97,113},{66,82,34,50,2,18,9..., dimensions={0} | all-to-all | bytes 65536 | tf_op jit(solution)/shard_map/all_to_all | solution.py:289
  12.2 0.0 collective-permute-done.arrived_ref
  12.2 0.0 copy-done.1
  12.2 0.0 copy-done
  12.2 0.5 %project.1 = (f32[384,128]{1,0:T(8,128)S(1)}, f32[16,64]{1,0:T(8,128)S(1)}) custom-call(f32[8,8,128]{2,1,0:T(8,128)S(1)} %all_to_all.15.p_ref, f32[1,64,5120]{2,1,0:T(8,128)S(1)} %copy-done, f32[1,64,5120]{2,1,0:T(8,128)S(1)} %copy-done.1, f32[64,2560]{1,0:T(8,128)S(1)} %collective-permute-done.arrived_ref), custom_call_target="tpu_custom_call" | custom-call | tf_op jit(solution)/shard_map/project/pallas_call | solution.py:292
  12.7 16.6 %all_to_all.16 = f32[64,1,768]{2,1,0:T(1,128)S(1)} all-to-all(f32[64,1,768]{2,1,0:T(1,128)S(1)} %bitcast.7), channel_id=1, replica_groups={{90,73,72,75,70,69,68,71,66,65,64,67,78,77,76,79,42,41,40,43,38,37,36,3..., dimensions={0} | all-to-all | bytes 393216 | tf_op jit(solution)/shard_map/all_to_all | solution.py:304
  29.4 13.0 %all_to_all.17 = f32[64,1,640]{2,1,0:T(1,128)S(1)} all-to-all(f32[64,1,640]{2,1,0:T(1,128)S(1)} %bitcast.8), channel_id=1, replica_groups={{90,73,72,75,70,69,68,71,66,65,64,67,78,77,76,79,42,41,40,43,38,37,36,3..., dimensions={0} | all-to-all | bytes 327680 | tf_op jit(solution)/shard_map/all_to_all | solution.py:319
  42.4 1.2 %collective-permute-start.1 = (f32[320,128]{1,0:T(8,128)S(1)}, f32[320,128]{1,0:T(8,128)S(1)}, u32[]{:S(2)}, u32[]{:S(2)}) collective-permute-start(f32[320,128]{1,0:T(8,128)S(1)} %bitcast.5), channel_id=1, source_target_pairs={{0,16},{16,0},{1,17},{17,1},{2,18},{18,2},{3,19},{19,3},{4,20},{20... | collective-permute-start | bytes 491528 | tf_op jit(solution)/shard_map/ppermute | solution.py:320
  43.6 1.0 %own_half.1 = (bf16[80,96]{1,0:T(8,128)(2,1)S(1)}, f32[16,64]{1,0:T(8,128)S(1)}, f32[16,2560]{1,0:T(8,128)S(1)}, f32[64,2560]{1,0:T(8,128)S(1)}) custom-call(f32[16,128]{1,0:T(8,128)S(1)} %get-tuple-element.16.gram_ref, f32[320,128]{1,0:T(8,128)S(1)} %bitcast.6, f32[16,64]{1,0:T(8,128)S(1)} %get-tuple-element.18.mean_ref, f32[1,64,5120]{2,1,0:T(8,128)S(1)} %copy-done, ...), custom_call_target="tpu_custom_call" | custom-call | flops 62914560 | bytes 2621440 | tf_op jit(solution)/shard_map/own_half/pallas_call | solution.py:322
  44.6 0.0 collective-permute-done.1.half_ref
  44.6 1.3 %finish.1 = (f32[1,64,5120]{2,1,0:T(8,128)}, f32[16,64]{1,0:T(8,128)}, f32[16,5120]{1,0:T(8,128)}) custom-call(bf16[80,96]{1,0:T(8,128)(2,1)S(1)} %get-tuple-element.19.left_ref, f32[16,64]{1,0:T(8,128)S(1)} %get-tuple-element.20.po_ref, f32[16,2560]{1,0:T(8,128)S(1)} %get-tuple-element.21.qf_ref, f32[64,2560]{1,0:T(8,128)S(1)} %get-tuple-element.22.nf_ref, ...), custom_call_target="tpu_custom_call" | custom-call | tf_op jit(solution)/shard_map/finish/pallas_call | solution.py:336
  (1 shorter events, 0.0 us)
Async XLA Ops:
  0.6 11.5 %copy-start.1 = (f32[1,64,5120]{2,1,0:T(8,128)S(1)}, f32[1,64,5120]{2,1,0:T(8,128)}, u32[]{:S(2)}) copy-start(f32[1,64,5120]{2,1,0:T(8,128)} %f_ref.5) | copy-start | bytes 3932164
  0.6 11.5 %copy-start = (f32[1,64,5120]{2,1,0:T(8,128)S(1)}, f32[1,64,5120]{2,1,0:T(8,128)}, u32[]{:S(2)}) copy-start(f32[1,64,5120]{2,1,0:T(8,128)} %g_ref.5) | copy-start | bytes 3932164
  3.5 8.7 %collective-permute-start = (f32[64,2560]{1,0:T(8,128)}, f32[64,2560]{1,0:T(8,128)S(1)}, u32[]{:S(2)}, u32[]{:S(2)}) collective-permute-start(f32[64,2560]{1,0:T(8,128)} %get-tuple-element.14), channel_id=1, source_target_pairs={{0,16},{16,0},{1,17},{17,1},{2,18},{18,2},{3,19},{19,3},{4,20},{20... | collective-permute-start | bytes 1966088 | tf_op jit(solution)/shard_map/ppermute | solution.py:288
  42.4 2.2 %collective-permute-start.1 = (f32[320,128]{1,0:T(8,128)S(1)}, f32[320,128]{1,0:T(8,128)S(1)}, u32[]{:S(2)}, u32[]{:S(2)}) collective-permute-start(f32[320,128]{1,0:T(8,128)S(1)} %bitcast.5), channel_id=1, source_target_pairs={{0,16},{16,0},{1,17},{17,1},{2,18},{18,2},{3,19},{19,3},{4,20},{20... | collective-permute-start | bytes 491528 | tf_op jit(solution)/shard_map/ppermute | solution.py:320

commit v8 on v7

--- a/solution.py
+++ b/solution.py
@@ -98,9 +98,9 @@
     nx, nc, nz, ny = sizes
     return [
         [
-            ((member_of(i) * nc + (core ^ int(i + j + k == 0))) * nz + member_of(j)) * ny + member_of(k)
+            ((member_of(i) * nc + (core ^ int((member_of(i), z, member_of(k)) == (2, 2, 2)))) * nz + z) * ny + member_of(k)
             for i in range(nx)
-            for j in range(nz)
+            for z in (2, 1, 3, 0)
             for k in range(ny)
         ]
         for core in range(nc)
@@ -284,7 +284,7 @@
     sizes = tuple(lax.axis_size(name) for name in DP + MP)
     near = [[member_of(i) * CORES + core for i in range(sizes[0]) for core in (0, 1)]]
     chips = chip_groups(sizes)
-    chips[1][0], chips[1][12] = chips[1][12], chips[1][0]
+    chips[1][0], chips[1][8] = chips[1][8], chips[1][0]
     arrived = lax.ppermute(c_send, "core", [(0, 1), (1, 0)])
     p_all = lax.all_to_all(p_out, DP, 0, 0, tiled=True, axis_index_groups=near)
 

time: 46.2 us -> 46.2 us (level)
  starting transfers between devices: 2.71 us -> 3.23 us
  blocking collectives: 36.8 us -> 36.3 us
    all_to_all x1, blocking collectives: 16.6 us -> 15.7 us  [body(): lax.all_to_all(msg, DP + MP, 0, 0, tiled=True, axis_index_groups=chips)]
    ppermute x1, starting transfers between devices: 1.21 us -> 1.72 us  [body(): other = lax.ppermute(half, 'core', [(0, 1), (1, 0)])]
    all_to_all x1, blocking collectives: 13 us -> 13.5 us  [body(): lax.all_to_all(own, DP + MP, 0, 0, tiled=True, axis_index_groups=chips)]
where the time goes in v8:
time: 46.2 us; the launch traced here: 46 us
  blocking collectives  36.3 us (79%)
  Pallas kernels  5.77 us (12%)
  starting transfers between devices  3.23 us (7%)
  between operations  0.68 us (1%)
    all_to_all x1, blocking collectives, body(): lax.all_to_all(msg, DP + MP, 0, 0, tiled=True, axis_index_groups=chips)  15.7 us
    all_to_all x1, blocking collectives, body(): lax.all_to_all(own, DP + MP, 0, 0, tiled=True, axis_index_groups=chips)  13.5 us
    all_to_all x1, blocking collectives, body(): p_all = lax.all_to_all(p_out, DP, 0, 0, tiled=True, axis_index_groups=near)  7.15 us
    pallas_call x1, Pallas kernels, body(): pl.pallas_call(correct_kernel, in_specs=[hbm, hbm, hbm], out_specs=[vmem,...  2.85 us
    ppermute x1, starting transfers between devices, body(): other = lax.ppermute(half, 'core', [(0, 1), (1, 0)])  1.72 us
    ppermute x1, starting transfers between devices, body(): arrived = lax.ppermute(c_send, 'core', [(0, 1), (1, 0)])  1.5 us
    pallas_call x1, Pallas kernels, body(): pl.pallas_call(finish_kernel, in_specs=[vmem] * 7, out_specs=[hbm] * 3, o...  1.33 us
    pallas_call x1, Pallas kernels, body(): pl.pallas_call(functools.partial(own_half_kernel, dp), in_specs=[vmem] *...  1 us
  transfers between devices with their start and end apart: 2, of which 0 were waited for; matrix products, arithmetic and copies ran while one was open for 0% of the time, Pallas kernels for 2%

profile of v8, /device:TPU:1, one launch (start us, length us, event | category | flops | bytes accessed | tf_op | source)
XLA Modules:
  0.0 46.0 jit_solution(10257973515377800131)
XLA Ops:
  0.6 0.0 copy-start.1
  0.6 0.0 copy-start
  0.7 2.8 %correct.1 = (f32[8,8,128]{2,1,0:T(8,128)S(1)}, f32[64,2560]{1,0:T(8,128)}) custom-call(f32[1,64,5120]{2,1,0:T(8,128)} %g_ref.5, f32[1,64,5120]{2,1,0:T(8,128)} %f_ref.5, f32[16,5120]{1,0:T(8,128)} %q_hbm.1), custom_call_target="tpu_custom_call" | custom-call | tf_op jit(solution)/shard_map/correct/pallas_call | solution.py:265
  3.5 1.5 %collective-permute-start = (f32[64,2560]{1,0:T(8,128)}, f32[64,2560]{1,0:T(8,128)S(1)}, u32[]{:S(2)}, u32[]{:S(2)}) collective-permute-start(f32[64,2560]{1,0:T(8,128)} %get-tuple-element.14), channel_id=1, source_target_pairs={{0,16},{16,0},{1,17},{17,1},{2,18},{18,2},{3,19},{19,3},{4,20},{20... | collective-permute-start | bytes 1966088 | tf_op jit(solution)/shard_map/ppermute | solution.py:288
  5.0 7.2 %all_to_all.15.p_ref = f32[8,8,128]{2,1,0:T(8,128)S(1)} all-to-all(f32[8,8,128]{2,1,0:T(8,128)S(1)} %get-tuple-element.13), channel_id=1, replica_groups={{64,80,32,48,0,16,96,112},{65,81,33,49,1,17,97,113},{66,82,34,50,2,18,9..., dimensions={0} | all-to-all | bytes 65536 | tf_op jit(solution)/shard_map/all_to_all | solution.py:289
  12.2 0.0 collective-permute-done.arrived_ref
  12.2 0.0 copy-done.1
  12.2 0.0 copy-done
  12.2 0.5 %project.1 = (f32[384,128]{1,0:T(8,128)S(1)}, f32[16,64]{1,0:T(8,128)S(1)}) custom-call(f32[8,8,128]{2,1,0:T(8,128)S(1)} %all_to_all.15.p_ref, f32[1,64,5120]{2,1,0:T(8,128)S(1)} %copy-done, f32[1,64,5120]{2,1,0:T(8,128)S(1)} %copy-done.1, f32[64,2560]{1,0:T(8,128)S(1)} %collective-permute-done.arrived_ref), custom_call_target="tpu_custom_call" | custom-call | tf_op jit(solution)/shard_map/project/pallas_call | solution.py:292
  12.7 15.7 %all_to_all.16 = f32[64,1,768]{2,1,0:T(1,128)S(1)} all-to-all(f32[64,1,768]{2,1,0:T(1,128)S(1)} %bitcast.7), channel_id=1, replica_groups={{90,73,72,75,70,69,68,71,78,77,76,79,66,65,64,67,42,41,40,43,38,37,36,3..., dimensions={0} | all-to-all | bytes 393216 | tf_op jit(solution)/shard_map/all_to_all | solution.py:304
  28.4 13.5 %all_to_all.17 = f32[64,1,640]{2,1,0:T(1,128)S(1)} all-to-all(f32[64,1,640]{2,1,0:T(1,128)S(1)} %bitcast.8), channel_id=1, replica_groups={{90,73,72,75,70,69,68,71,78,77,76,79,66,65,64,67,42,41,40,43,38,37,36,3..., dimensions={0} | all-to-all | bytes 327680 | tf_op jit(solution)/shard_map/all_to_all | solution.py:319
  41.9 1.7 %collective-permute-start.1 = (f32[320,128]{1,0:T(8,128)S(1)}, f32[320,128]{1,0:T(8,128)S(1)}, u32[]{:S(2)}, u32[]{:S(2)}) collective-permute-start(f32[320,128]{1,0:T(8,128)S(1)} %bitcast.5), channel_id=1, source_target_pairs={{0,16},{16,0},{1,17},{17,1},{2,18},{18,2},{3,19},{19,3},{4,20},{20... | collective-permute-start | bytes 491528 | tf_op jit(solution)/shard_map/ppermute | solution.py:320
  43.6 1.0 %own_half.1 = (bf16[80,96]{1,0:T(8,128)(2,1)S(1)}, f32[16,64]{1,0:T(8,128)S(1)}, f32[16,2560]{1,0:T(8,128)S(1)}, f32[64,2560]{1,0:T(8,128)S(1)}) custom-call(f32[16,128]{1,0:T(8,128)S(1)} %get-tuple-element.16.gram_ref, f32[320,128]{1,0:T(8,128)S(1)} %bitcast.6, f32[16,64]{1,0:T(8,128)S(1)} %get-tuple-element.18.mean_ref, f32[1,64,5120]{2,1,0:T(8,128)S(1)} %copy-done, ...), custom_call_target="tpu_custom_call" | custom-call | flops 62914560 | bytes 2621440 | tf_op jit(solution)/shard_map/own_half/pallas_call | solution.py:322
  44.6 0.0 collective-permute-done.1.half_ref
  44.7 1.3 %finish.1 = (f32[1,64,5120]{2,1,0:T(8,128)}, f32[16,64]{1,0:T(8,128)}, f32[16,5120]{1,0:T(8,128)}) custom-call(bf16[80,96]{1,0:T(8,128)(2,1)S(1)} %get-tuple-element.19.left_ref, f32[16,64]{1,0:T(8,128)S(1)} %get-tuple-element.20.po_ref, f32[16,2560]{1,0:T(8,128)S(1)} %get-tuple-element.21.qf_ref, f32[64,2560]{1,0:T(8,128)S(1)} %get-tuple-element.22.nf_ref, ...), custom_call_target="tpu_custom_call" | custom-call | tf_op jit(solution)/shard_map/finish/pallas_call | solution.py:336
  (1 shorter events, 0.0 us)
Async XLA Ops:
  0.6 11.5 %copy-start.1 = (f32[1,64,5120]{2,1,0:T(8,128)S(1)}, f32[1,64,5120]{2,1,0:T(8,128)}, u32[]{:S(2)}) copy-start(f32[1,64,5120]{2,1,0:T(8,128)} %f_ref.5) | copy-start | bytes 3932164
  0.6 11.5 %copy-start = (f32[1,64,5120]{2,1,0:T(8,128)S(1)}, f32[1,64,5120]{2,1,0:T(8,128)}, u32[]{:S(2)}) copy-start(f32[1,64,5120]{2,1,0:T(8,128)} %g_ref.5) | copy-start | bytes 3932164
  3.5 8.7 %collective-permute-start = (f32[64,2560]{1,0:T(8,128)}, f32[64,2560]{1,0:T(8,128)S(1)}, u32[]{:S(2)}, u32[]{:S(2)}) collective-permute-start(f32[64,2560]{1,0:T(8,128)} %get-tuple-element.14), channel_id=1, source_target_pairs={{0,16},{16,0},{1,17},{17,1},{2,18},{18,2},{3,19},{19,3},{4,20},{20... | collective-permute-start | bytes 1966088 | tf_op jit(solution)/shard_map/ppermute | solution.py:288
  41.9 2.8 %collective-permute-start.1 = (f32[320,128]{1,0:T(8,128)S(1)}, f32[320,128]{1,0:T(8,128)S(1)}, u32[]{:S(2)}, u32[]{:S(2)}) collective-permute-start(f32[320,128]{1,0:T(8,128)S(1)} %bitcast.5), channel_id=1, source_target_pairs={{0,16},{16,0},{1,17},{17,1},{2,18},{18,2},{3,19},{19,3},{4,20},{20... | collective-permute-start | bytes 491528 | tf_op jit(solution)/shard_map/ppermute | solution.py:320

commit v9 on v8

--- a/solution.py
+++ b/solution.py
@@ -12,7 +12,8 @@
 IN_PARTS = 4
 IN_TILE = 256
 CORES = 2
-HALF_GROUPS = 4
+HALF_GROUPS = 2
+BLOCKS = 4
 DP = ("x", "core")
 MP = ("z", "y")
 
@@ -90,21 +91,19 @@
         copy.wait()
 
 
-def member_of(place):
-    return (6 - place) % 4
-
-
 def chip_groups(sizes):
     nx, nc, nz, ny = sizes
-    return [
-        [
-            ((member_of(i) * nc + (core ^ int((member_of(i), z, member_of(k)) == (2, 2, 2)))) * nz + z) * ny + member_of(k)
-            for i in range(nx)
-            for z in (2, 1, 3, 0)
-            for k in range(ny)
-        ]
-        for core in range(nc)
-    ]
+    groups = []
+    for group in range(nc):
+        for half in ((2, 1), (3, 0)):
+            groups.append([
+                ((x * nc + (group ^ int((x, z, y) == (2, 2, 2)))) * nz + z) * ny + y
+                for x in half
+                for z in (2, 1, 3, 0)
+                for y in (2, 1, 0, 3)
+            ])
+    groups[2][0], groups[2][8] = groups[2][8], groups[2][0]
+    return groups
 
 
 def half_of_core():
@@ -113,8 +112,13 @@
     return jnp.where(leads, 1 - core, core)
 
 
-def column_at(core, n, width):
-    return pl.multiple_of((core * HALF_GROUPS + n) * width, width)
+def column_at(core, block, width):
+    return pl.multiple_of((core * BLOCKS + block) * width, width)
+
+
+def first_row(block, rank, tiles, length):
+    per_group = BLOCKS // HALF_GROUPS
+    return block // per_group * rank * length + block % per_group * tiles
 
 
 def project_kernel(p_ref, g_ref, f_ref, arrived_ref, msg_ref, mean_ref):
@@ -132,39 +136,44 @@
     left = jnp.concatenate(
         [jnp.concatenate(parts, axis=1) for parts in ((high, high, high), (mid, mid, none), (low, none, none))], axis=0
     )
-    width = arrived_ref.shape[1] // HALF_GROUPS
+    width = arrived_ref.shape[1] // BLOCKS
     tiles = width // LANES
-    for n in range(HALF_GROUPS):
+    length = BLOCKS // HALF_GROUPS * tiles + 1
+    for n in range(BLOCKS):
         cols = pl.ds(column_at(half_of_core(), n, width), width)
         pair = (g_ref[0, :, cols] + f_ref[0, :, cols]) + arrived_ref[:, n * width : (n + 1) * width]
         out = fold(bf16_dot(left, jnp.concatenate(split(pair), axis=0), 1, 0), rank, 0)
         for i in range(tiles):
-            first = n * rank * (tiles + 1) + i
-            msg_ref[pl.ds(first, rank, stride=tiles + 1), :] = out[:, i * LANES : (i + 1) * LANES]
+            first = first_row(n, rank, tiles, length) + i
+            for at in (first, first + msg_ref.shape[0] // 2):
+                msg_ref[pl.ds(at, rank, stride=length), :] = out[:, i * LANES : (i + 1) * LANES]
     gram = dot(mean, jnp.concatenate([mean] * (LANES // rank), axis=0), 1, 1)
     share = rank // HALF_GROUPS
     row = lax.broadcasted_iota(jnp.int32, (rank, LANES), 0)
     lane = lax.broadcasted_iota(jnp.int32, (rank, LANES), 1)
-    mine = row - share * member_of(lax.axis_index("x"))
+    mine = row - share * jnp.where(lax.axis_index("x") < 2, 1, 0)
     kept = (lane >= rank * mine) & (lane < rank * (mine + 1)) & (mine >= 0) & (mine < share)
     line = jnp.sum(jnp.where(kept, gram, 0.0), axis=0, keepdims=True)
-    count = msg_ref.shape[0] // (tiles + 1)
-    msg_ref[pl.ds(tiles, count, stride=tiles + 1), :] = jnp.broadcast_to(line, (count, LANES))
+    count = msg_ref.shape[0] // length
+    msg_ref[pl.ds(length - 1, count, stride=length), :] = jnp.broadcast_to(line, (count, LANES))
 
 
 def sum_kernel(in_ref, out_ref, gram_ref, part):
-    peers = in_ref.shape[0] // 6
-    total = in_ref[0:24]
-    for s in range(1, peers // 4):
-        total = total + in_ref[24 * s : 24 * (s + 1)]
+    members = HALF_GROUPS * gram_ref.shape[0]
+    length = in_ref.shape[0] // (2 * members)
+    rows = part.shape[0]
+    total = in_ref[0:rows]
+    for s in range(1, in_ref.shape[0] // rows):
+        total = total + in_ref[rows * s : rows * (s + 1)]
     part[...] = total
-    for i in range(5):
-        line = jnp.sum(part[pl.ds(i, 4, stride=6), :], axis=0, keepdims=True)
-        out_ref[pl.ds(i, peers, stride=5), :] = jnp.broadcast_to(line, (peers, LANES))
-    shards = peers // HALF_GROUPS
+    copies = out_ref.shape[0] // (length - 1)
+    for i in range(length - 1):
+        line = jnp.sum(part[pl.ds(i, rows // length, stride=length), :], axis=0, keepdims=True)
+        out_ref[pl.ds(i, copies, stride=length - 1), :] = jnp.broadcast_to(line, (copies, LANES))
+    shards = members // HALF_GROUPS
     share = gram_ref.shape[0] // HALF_GROUPS
     for n in range(HALF_GROUPS):
-        terms = in_ref[pl.ds(n * shards * 6 + 5, shards, stride=6), :]
+        terms = in_ref[pl.ds(n * shards * length + length - 1, shards, stride=length), :]
         line = jnp.sum(terms, axis=0, keepdims=True)
         gram_ref[n * share : (n + 1) * share, :] = jnp.broadcast_to(line, (share, LANES))
 
@@ -192,11 +201,11 @@
 
 
 def half_block(left, half_ref, g_ref, f_ref, core, n, rank):
-    width = g_ref.shape[2] // CORES // HALF_GROUPS
+    width = g_ref.shape[2] // CORES // BLOCKS
     tiles = width // LANES
-    raw = jnp.concatenate(
-        [half_ref[pl.ds(n * rank * tiles + i, rank, stride=tiles), :] for i in range(tiles)], axis=1
-    )
+    length = BLOCKS // HALF_GROUPS * tiles
+    first = first_row(n, rank, tiles, length)
+    raw = jnp.concatenate([half_ref[pl.ds(first + i, rank, stride=length), :] for i in range(tiles)], axis=1)
     high, mid, low = split(raw)
     out = bf16_dot(left, jnp.concatenate([high, mid, high, low, high, mid], axis=0), 1, 0)
     cols = pl.ds(column_at(core, n, width), width)
@@ -214,9 +223,9 @@
     high, mid, low = split(both)
     left = jnp.concatenate([high, high, mid, high, low, mid], axis=1)
     left_ref[...] = left
-    width = qf_ref.shape[1] // HALF_GROUPS
+    width = qf_ref.shape[1] // BLOCKS
     core = half_of_core()
-    for n in range(HALF_GROUPS):
+    for n in range(BLOCKS):
         cols = slice(n * width, (n + 1) * width)
         qf_ref[:, cols], nf_ref[:, cols] = half_block(left, half_ref, g_ref, f_ref, core, n, rank)
 
@@ -226,8 +235,8 @@
 ):
     rank = po_ref.shape[0]
     core = half_of_core()
-    width = qf_ref.shape[1] // HALF_GROUPS
-    own = pl.ds(column_at(core, 0, width), HALF_GROUPS * width)
+    width = qf_ref.shape[1] // BLOCKS
+    own = pl.ds(column_at(core, 0, width), BLOCKS * width)
     copies = [
         pltpu.make_async_copy(nf_ref, nf_hbm.at[0, :, own], half_sems.at[0]),
         pltpu.make_async_copy(qf_ref, qf_hbm.at[:, own], half_sems.at[1]),
@@ -236,7 +245,7 @@
     for copy in copies:
         copy.start()
     left = left_ref[...]
-    for n in range(HALF_GROUPS):
+    for n in range(BLOCKS):
         cols = slice(n * width, (n + 1) * width)
         qf_buf[:, cols], nf_buf[:, cols] = half_block(left, half_ref, g_ref, f_ref, 1 - core, n, rank)
         here = pl.ds(n * width, width)
@@ -258,6 +267,7 @@
     _, rows, width = gradient.shape
     rank = q_previous.shape[0]
     tiles = width // CORES // HALF_GROUPS // LANES
+    members = HALF_GROUPS * rank
     vmem = pl.BlockSpec(memory_space=pltpu.VMEM)
     hbm = pl.BlockSpec(memory_space=pltpu.HBM)
     params = pltpu.CompilerParams(vmem_limit_bytes=16 * 2**20)
@@ -282,9 +292,9 @@
         name="correct",
     )(gradient, feedback, q_previous)
     sizes = tuple(lax.axis_size(name) for name in DP + MP)
-    near = [[member_of(i) * CORES + core for i in range(sizes[0]) for core in (0, 1)]]
-    chips = chip_groups(sizes)
-    chips[1][0], chips[1][8] = chips[1][8], chips[1][0]
+    near = [[x * CORES + core for x in (2, 1, 0, 3) for core in (0, 1)]]
+    halves = chip_groups(sizes)
+    chips = [halves[2 * n] + halves[2 * n + 1] for n in range(CORES)]
     arrived = lax.ppermute(c_send, "core", [(0, 1), (1, 0)])
     p_all = lax.all_to_all(p_out, DP, 0, 0, tiled=True, axis_index_groups=near)
 
@@ -308,15 +318,15 @@
         in_specs=[vmem],
         out_specs=[vmem, vmem],
         out_shape=[
-            jax.ShapeDtypeStruct((count * tiles, LANES), f32),
+            jax.ShapeDtypeStruct((members * tiles, LANES), f32),
             jax.ShapeDtypeStruct((rank, LANES), f32),
         ],
-        scratch_shapes=[pltpu.VMEM((24, LANES), f32)],
+        scratch_shapes=[pltpu.VMEM((8 * (tiles + 1), LANES), f32)],
         compiler_params=params,
         name="sum_terms",
     )(terms.reshape(count * (tiles + 1), LANES))
-    own = own.reshape(count, 1, tiles * LANES)
-    half = lax.all_to_all(own, DP + MP, 0, 0, tiled=True, axis_index_groups=chips).reshape(count * tiles, LANES)
+    own = own.reshape(members, 1, tiles * LANES)
+    half = lax.all_to_all(own, DP + MP, 0, 0, tiled=True, axis_index_groups=halves).reshape(members * tiles, LANES)
     other = lax.ppermute(half, "core", [(0, 1), (1, 0)])
 
     left, p_ortho, q_half, f_half = pl.pallas_call(
@@ -345,7 +355,7 @@
         scratch_shapes=[
             pltpu.VMEM((rows, width // CORES), f32),
             pltpu.VMEM((rank, width // CORES), f32),
-            pltpu.SemaphoreType.DMA((2, HALF_GROUPS)),
+            pltpu.SemaphoreType.DMA((2, BLOCKS)),
             pltpu.SemaphoreType.DMA((3,)),
         ],
         compiler_params=params,

time: 46.2 us -> 46.8 us (1.013)
  starting transfers between devices: 3.23 us -> 3.93 us
    all_to_all x1, blocking collectives: 13.5 us -> 11.2 us  [body(): lax.all_to_all(own, DP + MP, 0, 0, tiled=True, axis_index_groups=halves)]
    all_to_all x1, blocking collectives: 15.7 us -> 17.8 us  [body(): lax.all_to_all(msg, DP + MP, 0, 0, tiled=True, axis_index_groups=chips)]
    ppermute x1, starting transfers between devices: 1.72 us -> 2.43 us  [body(): other = lax.ppermute(half, 'core', [(0, 1), (1, 0)])]
where the time goes in v9:
time: 46.8 us; the launch traced here: 46.6 us
  blocking collectives  36.2 us (77%)
  Pallas kernels  5.77 us (12%)
  starting transfers between devices  3.93 us (8%)
  between operations  0.68 us (1%)
    all_to_all x1, blocking collectives, body(): lax.all_to_all(msg, DP + MP, 0, 0, tiled=True, axis_index_groups=chips)  17.8 us
    all_to_all x1, blocking collectives, body(): lax.all_to_all(own, DP + MP, 0, 0, tiled=True, axis_index_groups=halves)  11.2 us
    all_to_all x1, blocking collectives, body(): p_all = lax.all_to_all(p_out, DP, 0, 0, tiled=True, axis_index_groups=near)  7.15 us
    pallas_call x1, Pallas kernels, body(): pl.pallas_call(correct_kernel, in_specs=[hbm, hbm, hbm], out_specs=[vmem,...  2.85 us
    ppermute x1, starting transfers between devices, body(): other = lax.ppermute(half, 'core', [(0, 1), (1, 0)])  2.43 us
    ppermute x1, starting transfers between devices, body(): arrived = lax.ppermute(c_send, 'core', [(0, 1), (1, 0)])  1.5 us
    pallas_call x1, Pallas kernels, body(): pl.pallas_call(finish_kernel, in_specs=[vmem] * 7, out_specs=[hbm] * 3, o...  1.33 us
    pallas_call x1, Pallas kernels, body(): pl.pallas_call(functools.partial(own_half_kernel, dp), in_specs=[vmem] *...  1 us
  transfers between devices with their start and end apart: 2, of which 0 were waited for; matrix products, arithmetic and copies ran while one was open for 0% of the time, Pallas kernels for 2%

profile of v9, /device:TPU:1, one launch (start us, length us, event | category | flops | bytes accessed | tf_op | source)
XLA Modules:
  0.0 46.6 jit_solution(5802123851384716641)
XLA Ops:
  0.6 0.0 copy-start.1
  0.6 0.0 copy-start
  0.7 2.8 %correct.1 = (f32[8,8,128]{2,1,0:T(8,128)S(1)}, f32[64,2560]{1,0:T(8,128)}) custom-call(f32[1,64,5120]{2,1,0:T(8,128)} %g_ref.5, f32[1,64,5120]{2,1,0:T(8,128)} %f_ref.5, f32[16,5120]{1,0:T(8,128)} %q_hbm.1), custom_call_target="tpu_custom_call" | custom-call | tf_op jit(solution)/shard_map/correct/pallas_call | solution.py:275
  3.5 1.5 %collective-permute-start = (f32[64,2560]{1,0:T(8,128)}, f32[64,2560]{1,0:T(8,128)S(1)}, u32[]{:S(2)}, u32[]{:S(2)}) collective-permute-start(f32[64,2560]{1,0:T(8,128)} %get-tuple-element.14), channel_id=1, source_target_pairs={{0,16},{16,0},{1,17},{17,1},{2,18},{18,2},{3,19},{19,3},{4,20},{20... | collective-permute-start | bytes 1966088 | tf_op jit(solution)/shard_map/ppermute | solution.py:298
  5.0 7.2 %all_to_all.15.p_ref = f32[8,8,128]{2,1,0:T(8,128)S(1)} all-to-all(f32[8,8,128]{2,1,0:T(8,128)S(1)} %get-tuple-element.13), channel_id=1, replica_groups={{64,80,32,48,0,16,96,112},{65,81,33,49,1,17,97,113},{66,82,34,50,2,18,9..., dimensions={0} | all-to-all | bytes 65536 | tf_op jit(solution)/shard_map/all_to_all | solution.py:299
  12.2 0.0 collective-permute-done.arrived_ref
  12.2 0.0 copy-done.1
  12.2 0.0 copy-done
  12.2 0.5 %project.1 = (f32[704,128]{1,0:T(8,128)S(1)}, f32[16,64]{1,0:T(8,128)S(1)}) custom-call(f32[8,8,128]{2,1,0:T(8,128)S(1)} %all_to_all.15.p_ref, f32[1,64,5120]{2,1,0:T(8,128)S(1)} %copy-done, f32[1,64,5120]{2,1,0:T(8,128)S(1)} %copy-done.1, f32[64,2560]{1,0:T(8,128)S(1)} %collective-permute-done.arrived_ref), custom_call_target="tpu_custom_call" | custom-call | tf_op jit(solution)/shard_map/project/pallas_call | solution.py:302
  12.7 17.8 %all_to_all.16 = f32[64,1,1408]{2,1,0:T(1,128)S(1)} all-to-all(f32[64,1,1408]{2,1,0:T(1,128)S(1)} %bitcast.7), channel_id=1, replica_groups={{90,73,72,75,70,69,68,71,78,77,76,79,66,65,64,67,42,41,40,43,38,37,36,3..., dimensions={0} | all-to-all | bytes 720896 | tf_op jit(solution)/shard_map/all_to_all | solution.py:314
  30.6 11.2 %all_to_all.17 = f32[32,1,1280]{2,1,0:T(1,128)S(1)} all-to-all(f32[32,1,1280]{2,1,0:T(1,128)S(1)} %bitcast.8), channel_id=1, replica_groups={{90,73,72,75,70,69,68,71,78,77,76,79,66,65,64,67,42,41,40,43,38,37,36,3..., dimensions={0} | all-to-all | bytes 327680 | tf_op jit(solution)/shard_map/all_to_all | solution.py:329
  41.8 2.4 %collective-permute-start.1 = (f32[320,128]{1,0:T(8,128)S(1)}, f32[320,128]{1,0:T(8,128)S(1)}, u32[]{:S(2)}, u32[]{:S(2)}) collective-permute-start(f32[320,128]{1,0:T(8,128)S(1)} %bitcast.5), channel_id=1, source_target_pairs={{0,16},{16,0},{1,17},{17,1},{2,18},{18,2},{3,19},{19,3},{4,20},{20... | collective-permute-start | bytes 491528 | tf_op jit(solution)/shard_map/ppermute | solution.py:330
  44.3 1.0 %own_half.1 = (bf16[80,96]{1,0:T(8,128)(2,1)S(1)}, f32[16,64]{1,0:T(8,128)S(1)}, f32[16,2560]{1,0:T(8,128)S(1)}, f32[64,2560]{1,0:T(8,128)S(1)}) custom-call(f32[16,128]{1,0:T(8,128)S(1)} %get-tuple-element.16.gram_ref, f32[320,128]{1,0:T(8,128)S(1)} %bitcast.6, f32[16,64]{1,0:T(8,128)S(1)} %get-tuple-element.18.mean_ref, f32[1,64,5120]{2,1,0:T(8,128)S(1)} %copy-done, ...), custom_call_target="tpu_custom_call" | custom-call | flops 62914560 | bytes 2621440 | tf_op jit(solution)/shard_map/own_half/pallas_call | solution.py:332
  45.3 0.0 collective-permute-done.1.half_ref
  45.3 1.3 %finish.1 = (f32[1,64,5120]{2,1,0:T(8,128)}, f32[16,64]{1,0:T(8,128)}, f32[16,5120]{1,0:T(8,128)}) custom-call(bf16[80,96]{1,0:T(8,128)(2,1)S(1)} %get-tuple-element.19.left_ref, f32[16,64]{1,0:T(8,128)S(1)} %get-tuple-element.20.po_ref, f32[16,2560]{1,0:T(8,128)S(1)} %get-tuple-element.21.qf_ref, f32[64,2560]{1,0:T(8,128)S(1)} %get-tuple-element.22.nf_ref, ...), custom_call_target="tpu_custom_call" | custom-call | tf_op jit(solution)/shard_map/finish/pallas_call | solution.py:346
  (1 shorter events, 0.0 us)
Async XLA Ops:
  0.6 11.5 %copy-start.1 = (f32[1,64,5120]{2,1,0:T(8,128)S(1)}, f32[1,64,5120]{2,1,0:T(8,128)}, u32[]{:S(2)}) copy-start(f32[1,64,5120]{2,1,0:T(8,128)} %f_ref.5) | copy-start | bytes 3932164
  0.6 11.5 %copy-start = (f32[1,64,5120]{2,1,0:T(8,128)S(1)}, f32[1,64,5120]{2,1,0:T(8,128)}, u32[]{:S(2)}) copy-start(f32[1,64,5120]{2,1,0:T(8,128)} %g_ref.5) | copy-start | bytes 3932164
  3.5 8.7 %collective-permute-start = (f32[64,2560]{1,0:T(8,128)}, f32[64,2560]{1,0:T(8,128)S(1)}, u32[]{:S(2)}, u32[]{:S(2)}) collective-permute-start(f32[64,2560]{1,0:T(8,128)} %get-tuple-element.14), channel_id=1, source_target_pairs={{0,16},{16,0},{1,17},{17,1},{2,18},{18,2},{3,19},{19,3},{4,20},{20... | collective-permute-start | bytes 1966088 | tf_op jit(solution)/shard_map/ppermute | solution.py:298
  41.8 3.5 %collective-permute-start.1 = (f32[320,128]{1,0:T(8,128)S(1)}, f32[320,128]{1,0:T(8,128)S(1)}, u32[]{:S(2)}, u32[]{:S(2)}) collective-permute-start(f32[320,128]{1,0:T(8,128)S(1)} %bitcast.5), channel_id=1, source_target_pairs={{0,16},{16,0},{1,17},{17,1},{2,18},{18,2},{3,19},{19,3},{4,20},{20... | collective-permute-start | bytes 491528 | tf_op jit(solution)/shard_map/ppermute | solution.py:330

commit v10 on v9

--- a/solution.py
+++ b/solution.py
@@ -95,7 +95,7 @@
     nx, nc, nz, ny = sizes
     groups = []
     for group in range(nc):
-        for half in ((2, 1), (3, 0)):
+        for half in ((2, 3), (1, 0)):
             groups.append([
                 ((x * nc + (group ^ int((x, z, y) == (2, 2, 2)))) * nz + z) * ny + y
                 for x in half
@@ -151,7 +151,7 @@
     share = rank // HALF_GROUPS
     row = lax.broadcasted_iota(jnp.int32, (rank, LANES), 0)
     lane = lax.broadcasted_iota(jnp.int32, (rank, LANES), 1)
-    mine = row - share * jnp.where(lax.axis_index("x") < 2, 1, 0)
+    mine = row - share * jnp.where((lax.axis_index("x") == 3) | (lax.axis_index("x") == 0), 1, 0)
     kept = (lane >= rank * mine) & (lane < rank * (mine + 1)) & (mine >= 0) & (mine < share)
     line = jnp.sum(jnp.where(kept, gram, 0.0), axis=0, keepdims=True)
     count = msg_ref.shape[0] // length

time: 46.8 us -> 45.5 us (0.972)
  blocking collectives: 36.2 us -> 35.4 us
  starting transfers between devices: 3.93 us -> 3.42 us
    all_to_all x1, blocking collectives: 11.2 us -> 10.4 us  [body(): lax.all_to_all(own, DP + MP, 0, 0, tiled=True, axis_index_groups=halves)]
    ppermute x1, starting transfers between devices: 2.43 us -> 1.91 us  [body(): other = lax.ppermute(half, 'core', [(0, 1), (1, 0)])]
where the time goes in v10:
time: 45.5 us; the launch traced here: 45.3 us
  blocking collectives  35.4 us (78%)
  Pallas kernels  5.77 us (13%)
  starting transfers between devices  3.42 us (8%)
  between operations  0.68 us (1%)
    all_to_all x1, blocking collectives, body(): lax.all_to_all(msg, DP + MP, 0, 0, tiled=True, axis_index_groups=chips)  17.8 us
    all_to_all x1, blocking collectives, body(): lax.all_to_all(own, DP + MP, 0, 0, tiled=True, axis_index_groups=halves)  10.4 us
    all_to_all x1, blocking collectives, body(): p_all = lax.all_to_all(p_out, DP, 0, 0, tiled=True, axis_index_groups=near)  7.15 us
    pallas_call x1, Pallas kernels, body(): pl.pallas_call(correct_kernel, in_specs=[hbm, hbm, hbm], out_specs=[vmem,...  2.85 us
    ppermute x1, starting transfers between devices, body(): other = lax.ppermute(half, 'core', [(0, 1), (1, 0)])  1.91 us
    ppermute x1, starting transfers between devices, body(): arrived = lax.ppermute(c_send, 'core', [(0, 1), (1, 0)])  1.5 us
    pallas_call x1, Pallas kernels, body(): pl.pallas_call(finish_kernel, in_specs=[vmem] * 7, out_specs=[hbm] * 3, o...  1.33 us
    pallas_call x1, Pallas kernels, body(): pl.pallas_call(functools.partial(own_half_kernel, dp), in_specs=[vmem] *...  1 us
  transfers between devices with their start and end apart: 2, of which 0 were waited for; matrix products, arithmetic and copies ran while one was open for 0% of the time, Pallas kernels for 2%

profile of v10, /device:TPU:1, one launch (start us, length us, event | category | flops | bytes accessed | tf_op | source)
XLA Modules:
  0.0 45.3 jit_solution(16582305832016730796)
XLA Ops:
  0.6 0.0 copy-start.1
  0.6 0.0 copy-start
  0.7 2.8 %correct.1 = (f32[8,8,128]{2,1,0:T(8,128)S(1)}, f32[64,2560]{1,0:T(8,128)}) custom-call(f32[1,64,5120]{2,1,0:T(8,128)} %g_ref.5, f32[1,64,5120]{2,1,0:T(8,128)} %f_ref.5, f32[16,5120]{1,0:T(8,128)} %q_hbm.1), custom_call_target="tpu_custom_call" | custom-call | tf_op jit(solution)/shard_map/correct/pallas_call | solution.py:275
  3.5 1.5 %collective-permute-start = (f32[64,2560]{1,0:T(8,128)}, f32[64,2560]{1,0:T(8,128)S(1)}, u32[]{:S(2)}, u32[]{:S(2)}) collective-permute-start(f32[64,2560]{1,0:T(8,128)} %get-tuple-element.14), channel_id=1, source_target_pairs={{0,16},{16,0},{1,17},{17,1},{2,18},{18,2},{3,19},{19,3},{4,20},{20... | collective-permute-start | bytes 1966088 | tf_op jit(solution)/shard_map/ppermute | solution.py:298
  5.0 7.2 %all_to_all.15.p_ref = f32[8,8,128]{2,1,0:T(8,128)S(1)} all-to-all(f32[8,8,128]{2,1,0:T(8,128)S(1)} %get-tuple-element.13), channel_id=1, replica_groups={{64,80,32,48,0,16,96,112},{65,81,33,49,1,17,97,113},{66,82,34,50,2,18,9..., dimensions={0} | all-to-all | bytes 65536 | tf_op jit(solution)/shard_map/all_to_all | solution.py:299
  12.2 0.0 collective-permute-done.arrived_ref
  12.2 0.0 copy-done.1
  12.2 0.0 copy-done
  12.2 0.5 %project.1 = (f32[704,128]{1,0:T(8,128)S(1)}, f32[16,64]{1,0:T(8,128)S(1)}) custom-call(f32[8,8,128]{2,1,0:T(8,128)S(1)} %all_to_all.15.p_ref, f32[1,64,5120]{2,1,0:T(8,128)S(1)} %copy-done, f32[1,64,5120]{2,1,0:T(8,128)S(1)} %copy-done.1, f32[64,2560]{1,0:T(8,128)S(1)} %collective-permute-done.arrived_ref), custom_call_target="tpu_custom_call" | custom-call | tf_op jit(solution)/shard_map/project/pallas_call | solution.py:302
  12.7 17.8 %all_to_all.16 = f32[64,1,1408]{2,1,0:T(1,128)S(1)} all-to-all(f32[64,1,1408]{2,1,0:T(1,128)S(1)} %bitcast.7), channel_id=1, replica_groups={{90,73,72,75,70,69,68,71,78,77,76,79,66,65,64,67,106,105,104,107,102,10..., dimensions={0} | all-to-all | bytes 720896 | tf_op jit(solution)/shard_map/all_to_all | solution.py:314
  30.6 10.4 %all_to_all.17 = f32[32,1,1280]{2,1,0:T(1,128)S(1)} all-to-all(f32[32,1,1280]{2,1,0:T(1,128)S(1)} %bitcast.8), channel_id=1, replica_groups={{90,73,72,75,70,69,68,71,78,77,76,79,66,65,64,67,106,105,104,107,102,10..., dimensions={0} | all-to-all | bytes 327680 | tf_op jit(solution)/shard_map/all_to_all | solution.py:329
  41.0 1.9 %collective-permute-start.1 = (f32[320,128]{1,0:T(8,128)S(1)}, f32[320,128]{1,0:T(8,128)S(1)}, u32[]{:S(2)}, u32[]{:S(2)}) collective-permute-start(f32[320,128]{1,0:T(8,128)S(1)} %bitcast.5), channel_id=1, source_target_pairs={{0,16},{16,0},{1,17},{17,1},{2,18},{18,2},{3,19},{19,3},{4,20},{20... | collective-permute-start | bytes 491528 | tf_op jit(solution)/shard_map/ppermute | solution.py:330
  42.9 1.0 %own_half.1 = (bf16[80,96]{1,0:T(8,128)(2,1)S(1)}, f32[16,64]{1,0:T(8,128)S(1)}, f32[16,2560]{1,0:T(8,128)S(1)}, f32[64,2560]{1,0:T(8,128)S(1)}) custom-call(f32[16,128]{1,0:T(8,128)S(1)} %get-tuple-element.16.gram_ref, f32[320,128]{1,0:T(8,128)S(1)} %bitcast.6, f32[16,64]{1,0:T(8,128)S(1)} %get-tuple-element.18.mean_ref, f32[1,64,5120]{2,1,0:T(8,128)S(1)} %copy-done, ...), custom_call_target="tpu_custom_call" | custom-call | flops 62914560 | bytes 2621440 | tf_op jit(solution)/shard_map/own_half/pallas_call | solution.py:332
  43.9 0.0 collective-permute-done.1.half_ref
  44.0 1.3 %finish.1 = (f32[1,64,5120]{2,1,0:T(8,128)}, f32[16,64]{1,0:T(8,128)}, f32[16,5120]{1,0:T(8,128)}) custom-call(bf16[80,96]{1,0:T(8,128)(2,1)S(1)} %get-tuple-element.19.left_ref, f32[16,64]{1,0:T(8,128)S(1)} %get-tuple-element.20.po_ref, f32[16,2560]{1,0:T(8,128)S(1)} %get-tuple-element.21.qf_ref, f32[64,2560]{1,0:T(8,128)S(1)} %get-tuple-element.22.nf_ref, ...), custom_call_target="tpu_custom_call" | custom-call | tf_op jit(solution)/shard_map/finish/pallas_call | solution.py:346
  (1 shorter events, 0.0 us)
Async XLA Ops:
  0.6 11.5 %copy-start.1 = (f32[1,64,5120]{2,1,0:T(8,128)S(1)}, f32[1,64,5120]{2,1,0:T(8,128)}, u32[]{:S(2)}) copy-start(f32[1,64,5120]{2,1,0:T(8,128)} %f_ref.5) | copy-start | bytes 3932164
  0.6 11.5 %copy-start = (f32[1,64,5120]{2,1,0:T(8,128)S(1)}, f32[1,64,5120]{2,1,0:T(8,128)}, u32[]{:S(2)}) copy-start(f32[1,64,5120]{2,1,0:T(8,128)} %g_ref.5) | copy-start | bytes 3932164
  3.5 8.7 %collective-permute-start = (f32[64,2560]{1,0:T(8,128)}, f32[64,2560]{1,0:T(8,128)S(1)}, u32[]{:S(2)}, u32[]{:S(2)}) collective-permute-start(f32[64,2560]{1,0:T(8,128)} %get-tuple-element.14), channel_id=1, source_target_pairs={{0,16},{16,0},{1,17},{17,1},{2,18},{18,2},{3,19},{19,3},{4,20},{20... | collective-permute-start | bytes 1966088 | tf_op jit(solution)/shard_map/ppermute | solution.py:298
  41.0 2.9 %collective-permute-start.1 = (f32[320,128]{1,0:T(8,128)S(1)}, f32[320,128]{1,0:T(8,128)S(1)}, u32[]{:S(2)}, u32[]{:S(2)}) collective-permute-start(f32[320,128]{1,0:T(8,128)S(1)} %bitcast.5), channel_id=1, source_target_pairs={{0,16},{16,0},{1,17},{17,1},{2,18},{18,2},{3,19},{19,3},{4,20},{20... | collective-permute-start | bytes 491528 | tf_op jit(solution)/shard_map/ppermute | solution.py:330

commit v11 on v10

--- a/solution.py
+++ b/solution.py
@@ -97,7 +97,7 @@
     for group in range(nc):
         for half in ((2, 3), (1, 0)):
             groups.append([
-                ((x * nc + (group ^ int((x, z, y) == (2, 2, 2)))) * nz + z) * ny + y
+                ((x * nc + (group ^ int((x, z, y) in ((2, 2, 2), (1, 2, 2))))) * nz + z) * ny + y
                 for x in half
                 for z in (2, 1, 3, 0)
                 for y in (2, 1, 0, 3)
@@ -108,7 +108,7 @@
 
 def half_of_core():
     core = lax.axis_index("core")
-    leads = (lax.axis_index("x") == 2) & (lax.axis_index("z") == 2) & (lax.axis_index("y") == 2)
+    leads = ((lax.axis_index("x") == 2) | (lax.axis_index("x") == 1)) & (lax.axis_index("z") == 2) & (lax.axis_index("y") == 2)
     return jnp.where(leads, 1 - core, core)
 
 

time: 45.5 us -> 45.2 us (level)
  starting transfers between devices: 3.42 us -> 2.86 us
    ppermute x1, starting transfers between devices: 1.91 us -> 1.35 us  [body(): other = lax.ppermute(half, 'core', [(0, 1), (1, 0)])]
where the time goes in v11:
time: 45.2 us; the launch traced here: 45 us
  blocking collectives  35.7 us (79%)
  Pallas kernels  5.77 us (13%)
  starting transfers between devices  2.86 us (6%)
  between operations  0.68 us (2%)
    all_to_all x1, blocking collectives, body(): lax.all_to_all(msg, DP + MP, 0, 0, tiled=True, axis_index_groups=chips)  17.9 us
    all_to_all x1, blocking collectives, body(): lax.all_to_all(own, DP + MP, 0, 0, tiled=True, axis_index_groups=halves)  10.6 us
    all_to_all x1, blocking collectives, body(): p_all = lax.all_to_all(p_out, DP, 0, 0, tiled=True, axis_index_groups=near)  7.15 us
    pallas_call x1, Pallas kernels, body(): pl.pallas_call(correct_kernel, in_specs=[hbm, hbm, hbm], out_specs=[vmem,...  2.85 us
    ppermute x1, starting transfers between devices, body(): arrived = lax.ppermute(c_send, 'core', [(0, 1), (1, 0)])  1.5 us
    ppermute x1, starting transfers between devices, body(): other = lax.ppermute(half, 'core', [(0, 1), (1, 0)])  1.35 us
    pallas_call x1, Pallas kernels, body(): pl.pallas_call(finish_kernel, in_specs=[vmem] * 7, out_specs=[hbm] * 3, o...  1.33 us
    pallas_call x1, Pallas kernels, body(): pl.pallas_call(functools.partial(own_half_kernel, dp), in_specs=[vmem] *...  1 us
  transfers between devices with their start and end apart: 2, of which 0 were waited for; matrix products, arithmetic and copies ran while one was open for 0% of the time, Pallas kernels for 2%

profile of v11, /device:TPU:1, one launch (start us, length us, event | category | flops | bytes accessed | tf_op | source)
XLA Modules:
  0.0 45.0 jit_solution(17293514491296365745)
XLA Ops:
  0.6 0.0 copy-start.1
  0.6 0.0 copy-start
  0.7 2.8 %correct.1 = (f32[8,8,128]{2,1,0:T(8,128)S(1)}, f32[64,2560]{1,0:T(8,128)}) custom-call(f32[1,64,5120]{2,1,0:T(8,128)} %g_ref.5, f32[1,64,5120]{2,1,0:T(8,128)} %f_ref.5, f32[16,5120]{1,0:T(8,128)} %q_hbm.1), custom_call_target="tpu_custom_call" | custom-call | tf_op jit(solution)/shard_map/correct/pallas_call | solution.py:275
  3.5 1.5 %collective-permute-start = (f32[64,2560]{1,0:T(8,128)}, f32[64,2560]{1,0:T(8,128)S(1)}, u32[]{:S(2)}, u32[]{:S(2)}) collective-permute-start(f32[64,2560]{1,0:T(8,128)} %get-tuple-element.14), channel_id=1, source_target_pairs={{0,16},{16,0},{1,17},{17,1},{2,18},{18,2},{3,19},{19,3},{4,20},{20... | collective-permute-start | bytes 1966088 | tf_op jit(solution)/shard_map/ppermute | solution.py:298
  5.0 7.2 %all_to_all.15.p_ref = f32[8,8,128]{2,1,0:T(8,128)S(1)} all-to-all(f32[8,8,128]{2,1,0:T(8,128)S(1)} %get-tuple-element.13), channel_id=1, replica_groups={{64,80,32,48,0,16,96,112},{65,81,33,49,1,17,97,113},{66,82,34,50,2,18,9..., dimensions={0} | all-to-all | bytes 65536 | tf_op jit(solution)/shard_map/all_to_all | solution.py:299
  12.2 0.0 collective-permute-done.arrived_ref
  12.2 0.0 copy-done.1
  12.2 0.0 copy-done
  12.2 0.5 %project.1 = (f32[704,128]{1,0:T(8,128)S(1)}, f32[16,64]{1,0:T(8,128)S(1)}) custom-call(f32[8,8,128]{2,1,0:T(8,128)S(1)} %all_to_all.15.p_ref, f32[1,64,5120]{2,1,0:T(8,128)S(1)} %copy-done, f32[1,64,5120]{2,1,0:T(8,128)S(1)} %copy-done.1, f32[64,2560]{1,0:T(8,128)S(1)} %collective-permute-done.arrived_ref), custom_call_target="tpu_custom_call" | custom-call | tf_op jit(solution)/shard_map/project/pallas_call | solution.py:302
  12.7 17.9 %all_to_all.16 = f32[64,1,1408]{2,1,0:T(1,128)S(1)} all-to-all(f32[64,1,1408]{2,1,0:T(1,128)S(1)} %bitcast.7), channel_id=1, replica_groups={{90,73,72,75,70,69,68,71,78,77,76,79,66,65,64,67,106,105,104,107,102,10..., dimensions={0} | all-to-all | bytes 720896 | tf_op jit(solution)/shard_map/all_to_all | solution.py:314
  30.6 10.6 %all_to_all.17 = f32[32,1,1280]{2,1,0:T(1,128)S(1)} all-to-all(f32[32,1,1280]{2,1,0:T(1,128)S(1)} %bitcast.8), channel_id=1, replica_groups={{90,73,72,75,70,69,68,71,78,77,76,79,66,65,64,67,106,105,104,107,102,10..., dimensions={0} | all-to-all | bytes 327680 | tf_op jit(solution)/shard_map/all_to_all | solution.py:329
  41.3 1.4 %collective-permute-start.1 = (f32[320,128]{1,0:T(8,128)S(1)}, f32[320,128]{1,0:T(8,128)S(1)}, u32[]{:S(2)}, u32[]{:S(2)}) collective-permute-start(f32[320,128]{1,0:T(8,128)S(1)} %bitcast.5), channel_id=1, source_target_pairs={{0,16},{16,0},{1,17},{17,1},{2,18},{18,2},{3,19},{19,3},{4,20},{20... | collective-permute-start | bytes 491528 | tf_op jit(solution)/shard_map/ppermute | solution.py:330
  42.6 1.0 %own_half.1 = (bf16[80,96]{1,0:T(8,128)(2,1)S(1)}, f32[16,64]{1,0:T(8,128)S(1)}, f32[16,2560]{1,0:T(8,128)S(1)}, f32[64,2560]{1,0:T(8,128)S(1)}) custom-call(f32[16,128]{1,0:T(8,128)S(1)} %get-tuple-element.16.gram_ref, f32[320,128]{1,0:T(8,128)S(1)} %bitcast.6, f32[16,64]{1,0:T(8,128)S(1)} %get-tuple-element.18.mean_ref, f32[1,64,5120]{2,1,0:T(8,128)S(1)} %copy-done, ...), custom_call_target="tpu_custom_call" | custom-call | flops 62914560 | bytes 2621440 | tf_op jit(solution)/shard_map/own_half/pallas_call | solution.py:332
  43.6 0.0 collective-permute-done.1.half_ref
  43.7 1.3 %finish.1 = (f32[1,64,5120]{2,1,0:T(8,128)}, f32[16,64]{1,0:T(8,128)}, f32[16,5120]{1,0:T(8,128)}) custom-call(bf16[80,96]{1,0:T(8,128)(2,1)S(1)} %get-tuple-element.19.left_ref, f32[16,64]{1,0:T(8,128)S(1)} %get-tuple-element.20.po_ref, f32[16,2560]{1,0:T(8,128)S(1)} %get-tuple-element.21.qf_ref, f32[64,2560]{1,0:T(8,128)S(1)} %get-tuple-element.22.nf_ref, ...), custom_call_target="tpu_custom_call" | custom-call | tf_op jit(solution)/shard_map/finish/pallas_call | solution.py:346
  (1 shorter events, 0.0 us)
Async XLA Ops:
  0.6 11.5 %copy-start.1 = (f32[1,64,5120]{2,1,0:T(8,128)S(1)}, f32[1,64,5120]{2,1,0:T(8,128)}, u32[]{:S(2)}) copy-start(f32[1,64,5120]{2,1,0:T(8,128)} %f_ref.5) | copy-start | bytes 3932164
  0.6 11.5 %copy-start = (f32[1,64,5120]{2,1,0:T(8,128)S(1)}, f32[1,64,5120]{2,1,0:T(8,128)}, u32[]{:S(2)}) copy-start(f32[1,64,5120]{2,1,0:T(8,128)} %g_ref.5) | copy-start | bytes 3932164
  3.5 8.7 %collective-permute-start = (f32[64,2560]{1,0:T(8,128)}, f32[64,2560]{1,0:T(8,128)S(1)}, u32[]{:S(2)}, u32[]{:S(2)}) collective-permute-start(f32[64,2560]{1,0:T(8,128)} %get-tuple-element.14), channel_id=1, source_target_pairs={{0,16},{16,0},{1,17},{17,1},{2,18},{18,2},{3,19},{19,3},{4,20},{20... | collective-permute-start | bytes 1966088 | tf_op jit(solution)/shard_map/ppermute | solution.py:298
  41.3 2.4 %collective-permute-start.1 = (f32[320,128]{1,0:T(8,128)S(1)}, f32[320,128]{1,0:T(8,128)S(1)}, u32[]{:S(2)}, u32[]{:S(2)}) collective-permute-start(f32[320,128]{1,0:T(8,128)S(1)} %bitcast.5), channel_id=1, source_target_pairs={{0,16},{16,0},{1,17},{17,1},{2,18},{18,2},{3,19},{19,3},{4,20},{20... | collective-permute-start | bytes 491528 | tf_op jit(solution)/shard_map/ppermute | solution.py:330
